TPU v7x, 32 devices: a whole 2x2x4 slice. The times are simulated.
32 devices in a mesh: section: 2 (over core), dp: 4 (over z), tensor: 4 (over y, x).
Axes of the slice: x: 2, y: 2, z: 4, core: 2. Of those that a mesh axis runs over, the one named last changes fastest.
Arguments:
- layer_in: bfloat16 [2, 4, 2048, 1024], P('section', None, ('dp', 'tensor')), may hold values from -6 to 6
- segments: int32 [2, 4, 4, 512], P(None, None, 'dp'), may hold values from 0 to 3, never falling along the last dimension, each value on 1 to 256 neighbouring positions
- cotangent: bfloat16 [4, 2048, 1024], P(None, ('dp', 'tensor')), may hold values from -6 to 6
- self_qkv: bfloat16 [2, 1024, 3072], P('section', None, 'tensor'), may hold values from -0.1875 to 0.1875
- self_out: bfloat16 [2, 1024, 1024], P('section', 'tensor'), may hold values from -0.75 to 0.75
- cross_proj: bfloat16 [2, 1024, 2048], P('section', None, 'tensor'), may hold values from -0.75 to 0.75
- ffn_up: bfloat16 [2, 1024, 4096], P('section', None, 'tensor'), may hold values from -0.1875 to 0.1875
- ffn_down: bfloat16 [2, 4096, 1024], P('section', 'tensor'), may hold values from -0.09375 to 0.09375
- norm_gain: float32 [2, 3, 1024], P('section'), may hold values from 0.1 to 1.9
- norm_bias: float32 [2, 3, 1024], P('section'), may hold values from -1.8 to 1.8
Outputs:
- layer_out: bfloat16 [2, 4, 2048, 1024], P('section', None, ('dp', 'tensor'))
- input_grad: bfloat16 [2, 4, 2048, 1024], P('section', None, ('dp', 'tensor'))
- self_qkv_grad: float32 [2, 1024, 3072], P('section', None, 'tensor')
- self_out_grad: float32 [2, 1024, 1024], P('section', 'tensor')
- cross_grad: float32 [2, 1024, 2048], P('section', None, 'tensor')
- ffn_up_grad: float32 [2, 1024, 4096], P('section', None, 'tensor')
- ffn_down_grad: float32 [2, 4096, 1024], P('section', 'tensor')
- gain_grad: float32 [2, 3, 1024], P('section', None, 'tensor')
- bias_grad: float32 [2, 3, 1024], P('section', None, 'tensor')
Inputs may be any that keep to these rules, and one draw needn't show every extreme that they name: `segments`: every packed row of 512 tokens holds documents 0 to 3 in order, each of 1 to 256 tokens, so every decoder document has its namesake in the encoder row of the same place.
All inputs are finite; a program needn't handle non-finite values.
Results may differ from a plain program's by a relative error of at most 0.03.
Values may be sent and summed in bfloat16 or wider, within the bound.
No kernel may reach another device: no remote copies, remote signals or barrier semaphores. Data moves between devices by JAX's collectives and lax.ppermute only.
A program may use at most 320 MiB of HBM per device.

v0:
```python
import jax
import jax.numpy as jnp
from jax import lax
from jax.sharding import PartitionSpec as P

HD = 64


eps_norm = 1e-05
masked_score = -1e30


def shifted(value, axis, steps):
    count = lax.axis_size(axis)
    leading, last = (max(0, -steps), min(count, count - steps))
    return lax.ppermute(value, axis, [(source, source + steps) for source in range(leading, last)])


def normalize(values, gain_row, bias_row):
    centre = values - jnp.mean(values, axis=-1, keepdims=True)
    inv_scale = lax.rsqrt(jnp.mean(centre * centre, axis=-1, keepdims=True) + eps_norm)
    normed = centre * inv_scale
    return (normed * gain_row + bias_row, (normed, inv_scale))


def normalize_back(upstream, norm_stats, gain_row):
    normed, inv_scale = norm_stats
    scaled = upstream * gain_row
    inner_grad = (
        scaled
        - jnp.mean(scaled, axis=-1, keepdims=True)
        - normed * jnp.mean(scaled * normed, axis=-1, keepdims=True)
    )
    return (inner_grad * inv_scale, jnp.sum(upstream * normed, axis=0), jnp.sum(upstream, axis=0))


def rows_product(left, right):
    return lax.dot_general(
        left, right, (((0,), (0,)), ((), ())), preferred_element_type=jnp.float32
    )


def transposed_product(left, right):
    return lax.dot_general(
        left, right, (((1,), (1,)), ((), ())), preferred_element_type=jnp.float32
    )


def exact_gelu(values):
    return jax.nn.gelu(values, approximate=False)


def gelu_back(pre_values, upstream):
    unused, pull_back = jax.vjp(exact_gelu, pre_values)
    return pull_back(upstream)[0]


def gather_rows(rows_low):
    return lax.all_gather(rows_low, "tensor", axis=0, tiled=True)


def gather_grads(grads_low):
    return lax.all_gather(grads_low, "tensor", axis=0, tiled=True)


def sum_rows(values, weight, share_rows):

    def partial_term(first_row, row_count):
        return jnp.dot(values, weight, preferred_element_type=jnp.float32)

    return lax.psum_scatter(
        partial_term(jnp.int32(0), share_rows * lax.axis_size("tensor")).astype(jnp.bfloat16),
        "tensor",
        scatter_dimension=0,
        tiled=True,
    ).astype(jnp.float32)


def sum_grads(grads_low, weight, share_rows):

    def partial_term(first_row, row_count):
        return transposed_product(grads_low, weight)

    return lax.psum_scatter(
        partial_term(jnp.int32(0), share_rows * lax.axis_size("tensor")).astype(jnp.bfloat16),
        "tensor",
        scatter_dimension=0,
        tiled=True,
    ).astype(jnp.float32)


def score_block(queries, keys_in, seg_query, seg_key, causal):
    scale_factor = queries.shape[-1] ** (-0.5)
    scores = (
        jnp.einsum("bihe,bjhe->bhij", queries, keys_in, preferred_element_type=jnp.float32)
        * scale_factor
    )
    length = queries.shape[1]
    rows_at = lax.broadcasted_iota(jnp.int32, (length, length), 0)
    cols_at = lax.broadcasted_iota(jnp.int32, (length, length), 1)
    allowed = seg_query[:, None, :, None] == seg_key[:, None, None, :]
    allowed = allowed & ((cols_at <= rows_at) | jnp.logical_not(causal))[None, None]
    return jnp.where(allowed, scores, masked_score)


def attend(queries, keys_in, values, seg_query, seg_key, causal):
    masked = score_block(queries, keys_in, seg_query, seg_key, causal)
    row_peak = jnp.max(masked, axis=-1, keepdims=True)
    exponent = jnp.exp(masked - row_peak)
    row_total = jnp.sum(exponent, axis=-1, keepdims=True)
    probs_low = (exponent / row_total).astype(jnp.bfloat16)
    mixed = jnp.einsum("bhij,bjhe->bihe", probs_low, values, preferred_element_type=jnp.float32)
    return (mixed, row_peak + jnp.log(row_total))


def attend_back(queries, keys_in, values, seg_query, seg_key, causal, log_total, grad_low):
    scale_factor = queries.shape[-1] ** (-0.5)
    masked = score_block(queries, keys_in, seg_query, seg_key, causal)
    probs_full = jnp.exp(masked - log_total)
    probs_low = probs_full.astype(jnp.bfloat16)
    grad_probs = jnp.einsum("bihe,bjhe->bhij", grad_low, values, preferred_element_type=jnp.float32)
    grad_values = jnp.einsum(
        "bhij,bihe->bjhe", probs_low, grad_low, preferred_element_type=jnp.float32
    )
    inner_sum = jnp.sum(probs_full * grad_probs, axis=-1, keepdims=True)
    grad_scores = (probs_full * (grad_probs - inner_sum)).astype(jnp.bfloat16)
    grad_queries = (
        jnp.einsum("bhij,bjhe->bihe", grad_scores, keys_in, preferred_element_type=jnp.float32)
        * scale_factor
    )
    grad_keys = (
        jnp.einsum("bhij,bihe->bjhe", grad_scores, queries, preferred_element_type=jnp.float32)
        * scale_factor
    )
    return (grad_queries, grad_keys, grad_values)


def place_micro(stacked_rows, fresh_rows, micro_index, is_valid):
    current = lax.dynamic_index_in_dim(stacked_rows, micro_index, 0, keepdims=False)
    chosen = jnp.where(is_valid, fresh_rows, current)
    return lax.dynamic_update_index_in_dim(stacked_rows, chosen, micro_index, 0)


def on_device(
    layer_in,
    segments,
    cotangent,
    self_qkv,
    self_out,
    cross_proj,
    ffn_up,
    ffn_down,
    norm_gain,
    norm_bias,
):
    section_index = lax.axis_index("section")
    is_first = section_index == 0
    is_decoder = jnp.logical_not(is_first)
    micro_count = layer_in.shape[1]
    share_rows = layer_in.shape[2]
    model_width = layer_in.shape[3]
    packed = segments.shape[2]
    length = segments.shape[3]
    all_rows = packed * length
    shards = (self_qkv[0], self_out[0], cross_proj[0], ffn_up[0], ffn_down[0])
    w_qkv, w_out, w_cross, w_up, w_down = shards
    gain_rows = norm_gain[0]
    bias_rows = norm_bias[0]
    local_heads = w_out.shape[0] // HD
    cross_back = jnp.transpose(
        w_cross.reshape(model_width, local_heads, 2, HD)[:, :, 1, :].reshape(
            model_width, local_heads * HD
        )
    )

    def spread_rows(rows_low):
        return gather_rows(rows_low)

    def spread_grads(grads_low):
        return gather_grads(grads_low)

    def reduce_rows(values, weight):
        return sum_rows(values, weight, share_rows)

    def reduce_grads(grads_low, weight):
        return sum_grads(grads_low, weight, share_rows)

    def attention_forward(queries, key_values, seg_query, seg_key, causal):
        shaped_query = queries.reshape(packed, length, local_heads, HD)
        shaped_keys = key_values.reshape(packed, length, local_heads, 2, HD)
        mixed, log_total = attend(
            shaped_query,
            shaped_keys[:, :, :, 0],
            shaped_keys[:, :, :, 1],
            seg_query,
            seg_key,
            causal,
        )
        mixed = mixed.reshape(all_rows, local_heads, HD)
        return (mixed, log_total, key_values)

    def attention_backward(queries, full_keys, seg_query, seg_key, causal, log_total, grad_low):
        shaped_query = queries.reshape(packed, length, local_heads, HD)
        shaped_keys = full_keys.reshape(packed, length, local_heads, 2, HD)
        grad_query, grad_key, grad_value = attend_back(
            shaped_query,
            shaped_keys[:, :, :, 0],
            shaped_keys[:, :, :, 1],
            seg_query,
            seg_key,
            causal,
            log_total,
            grad_low.reshape(packed, length, local_heads, HD),
        )
        grad_query = grad_query.reshape(all_rows, local_heads, HD)
        grad_pair = jnp.stack([grad_key, grad_value], axis=3).reshape(all_rows, local_heads, 2, HD)
        return (grad_query, grad_pair)

    def forward_tick(tick_index, held_rows):
        micro_index = jnp.clip(tick_index - section_index, 0, micro_count - 1)
        source = lax.dynamic_index_in_dim(layer_in[0], micro_index, 0, keepdims=False).astype(
            jnp.float32
        )
        seg_pair = lax.dynamic_index_in_dim(segments, micro_index, 1, keepdims=False)
        seg_own = lax.dynamic_index_in_dim(seg_pair, section_index, 0, keepdims=False)
        seg_memory = seg_pair[0]
        normed_in, stats_in = normalize(source, gain_rows[1], bias_rows[1])
        start_rows = jnp.where(is_first, normed_in, source)
        gathered_in = spread_rows(start_rows.astype(jnp.bfloat16))
        mixed_qkv = jnp.dot(gathered_in, w_qkv, preferred_element_type=jnp.float32).astype(
            jnp.bfloat16
        )
        mixed_qkv = mixed_qkv.reshape(all_rows, local_heads, 3, HD)
        self_heads, self_total, self_keys = attention_forward(
            mixed_qkv[:, :, 0], mixed_qkv[:, :, 1:3], seg_own, seg_own, is_decoder
        )
        self_flat = self_heads.astype(jnp.bfloat16).reshape(all_rows, local_heads * HD)
        self_mix = reduce_rows(self_flat, w_out)
        after_self, stats_self = normalize(start_rows + self_mix, gain_rows[0], bias_rows[0])
        cross_rows = jnp.where(is_first, held_rows, after_self)
        gathered_cross = spread_rows(cross_rows.astype(jnp.bfloat16))
        projected = jnp.dot(gathered_cross, w_cross, preferred_element_type=jnp.float32).astype(
            jnp.bfloat16
        )
        received = shifted(projected, "section", 1)
        own_heads = projected.reshape(all_rows, local_heads, 2, HD)
        memory_heads = received.reshape(all_rows, local_heads, 2, HD)
        cross_heads, cross_total, memory_keys = attention_forward(
            own_heads[:, :, 0], memory_heads, seg_own, seg_memory, False
        )
        cross_flat = cross_heads.astype(jnp.bfloat16).reshape(all_rows, local_heads * HD)
        cross_mix = reduce_rows(cross_flat, cross_back)
        after_cross, stats_cross = normalize(after_self + cross_mix, gain_rows[1], bias_rows[1])
        middle = jnp.where(is_first, after_self, after_cross)
        gathered_mid = spread_rows(middle.astype(jnp.bfloat16))
        hidden_pre = jnp.dot(gathered_mid, w_up, preferred_element_type=jnp.float32)
        hidden = exact_gelu(hidden_pre).astype(jnp.bfloat16)
        ffn_mix = reduce_rows(hidden, w_down)
        result, stats_out = normalize(middle + ffn_mix, gain_rows[2], bias_rows[2])
        record = {
            "micro_index": micro_index,
            "seg_own": seg_own,
            "seg_memory": seg_memory,
            "stats_in": stats_in,
            "gathered_in": gathered_in,
            "mixed_qkv": mixed_qkv,
            "self_total": self_total,
            "self_keys": self_keys,
            "self_flat": self_flat,
            "stats_self": stats_self,
            "gathered_cross": gathered_cross,
            "projected": projected,
            "memory_keys": memory_keys,
            "cross_total": cross_total,
            "cross_flat": cross_flat,
            "stats_cross": stats_cross,
            "gathered_mid": gathered_mid,
            "hidden_pre": hidden_pre,
            "hidden": hidden,
            "stats_out": stats_out,
        }
        return (result, record)

    held_rows = jnp.zeros((share_rows, model_width), jnp.float32)
    outputs = jnp.zeros(layer_in.shape[1:], jnp.bfloat16)
    held_list = []
    for tick_index in range(micro_count + 1):
        held_list.append(held_rows)
        result, record = forward_tick(tick_index, held_rows)
        is_valid = (tick_index - section_index >= 0) & (tick_index - section_index < micro_count)
        outputs = place_micro(outputs, result.astype(jnp.bfloat16), record["micro_index"], is_valid)
        held_rows = result
    grad_qkv = jnp.zeros(w_qkv.shape, jnp.float32)
    grad_out = jnp.zeros(w_out.shape, jnp.float32)
    grad_cross = jnp.zeros(w_cross.shape, jnp.float32)
    grad_up = jnp.zeros(w_up.shape, jnp.float32)
    grad_down = jnp.zeros(w_down.shape, jnp.float32)
    grad_gain = jnp.zeros((3, model_width), jnp.float32)
    grad_bias = jnp.zeros((3, model_width), jnp.float32)
    carried = jnp.zeros((share_rows, model_width), jnp.float32)
    input_grads = jnp.zeros(layer_in.shape[1:], jnp.bfloat16)
    for tick_index in reversed(range(micro_count + 1)):
        record = forward_tick(tick_index, held_list[tick_index])[1]
        is_valid = (tick_index - section_index >= 0) & (tick_index - section_index < micro_count)
        micro_index = record["micro_index"]
        seg_own = record["seg_own"]
        seg_memory = record["seg_memory"]
        cot_rows = lax.dynamic_index_in_dim(cotangent, micro_index, 0, keepdims=False).astype(
            jnp.float32
        )
        top_grad = jnp.where(is_first, carried, jnp.where(is_valid, cot_rows, 0.0))
        grad_mid, gain_last, bias_last = normalize_back(top_grad, record["stats_out"], gain_rows[2])
        ffn_full = spread_grads(grad_mid.astype(jnp.bfloat16))
        grad_down = grad_down + rows_product(record["hidden"], ffn_full)
        grad_hidden = transposed_product(ffn_full, w_down)
        grad_pre = gelu_back(record["hidden_pre"], grad_hidden).astype(jnp.bfloat16)
        grad_up = grad_up + rows_product(record["gathered_mid"], grad_pre)
        grad_middle = grad_mid + reduce_grads(grad_pre, w_up)
        grad_cross_sum, gain_cross, bias_cross = normalize_back(
            grad_middle, record["stats_cross"], gain_rows[1]
        )
        grad_cross_sum = jnp.where(is_first, 0.0, grad_cross_sum)
        cross_full = spread_grads(grad_cross_sum.astype(jnp.bfloat16))
        grad_cross_out = rows_product(record["cross_flat"], cross_full)
        grad_cross_heads = (
            transposed_product(cross_full, cross_back)
            .astype(jnp.bfloat16)
            .reshape(all_rows, local_heads, HD)
        )
        own_heads = record["projected"].reshape(all_rows, local_heads, 2, HD)
        grad_query, grad_memory = attention_backward(
            own_heads[:, :, 0],
            record["memory_keys"],
            seg_own,
            seg_memory,
            False,
            record["cross_total"],
            grad_cross_heads,
        )
        sent_grads = grad_memory.astype(jnp.bfloat16).reshape(all_rows, local_heads * 2 * HD)
        returned = shifted(sent_grads, "section", -1)
        own_grads = (
            jnp.stack([grad_query, jnp.zeros_like(grad_query)], axis=2)
            .astype(jnp.bfloat16)
            .reshape(all_rows, local_heads * 2 * HD)
        )
        grad_projected = jnp.where(is_first, returned, own_grads)
        out_part = jnp.transpose(grad_cross_out).reshape(model_width, local_heads, 1, HD)
        out_part = jnp.concatenate([jnp.zeros_like(out_part), out_part], axis=2).reshape(
            model_width, local_heads * 2 * HD
        )
        grad_cross = grad_cross + rows_product(record["gathered_cross"], grad_projected) + out_part
        grad_cross_rows = reduce_grads(grad_projected, w_cross)
        carried = jnp.where(is_first, grad_cross_rows, 0.0)
        grad_after_self = jnp.where(is_first, grad_middle, grad_cross_sum + grad_cross_rows)
        grad_self_sum, gain_self, bias_self = normalize_back(
            grad_after_self, record["stats_self"], gain_rows[0]
        )
        self_full = spread_grads(grad_self_sum.astype(jnp.bfloat16))
        grad_out = grad_out + rows_product(record["self_flat"], self_full)
        grad_self_heads = (
            transposed_product(self_full, w_out)
            .astype(jnp.bfloat16)
            .reshape(all_rows, local_heads, HD)
        )
        mixed_qkv = record["mixed_qkv"]
        grad_query, grad_pair = attention_backward(
            mixed_qkv[:, :, 0],
            record["self_keys"],
            seg_own,
            seg_own,
            is_decoder,
            record["self_total"],
            grad_self_heads,
        )
        grad_mixed = (
            jnp.concatenate([grad_query[:, :, None], grad_pair], axis=2)
            .astype(jnp.bfloat16)
            .reshape(all_rows, local_heads * 3 * HD)
        )
        grad_qkv = grad_qkv + rows_product(record["gathered_in"], grad_mixed)
        grad_start = grad_self_sum + reduce_grads(grad_mixed, w_qkv)
        grad_norm_in, gain_first, bias_first = normalize_back(
            grad_start, record["stats_in"], gain_rows[1]
        )
        grad_source = jnp.where(is_first, grad_norm_in, grad_start)
        grad_gain = grad_gain + jnp.stack(
            [gain_self, jnp.where(is_first, gain_first, gain_cross), gain_last]
        )
        grad_bias = grad_bias + jnp.stack(
            [bias_self, jnp.where(is_first, bias_first, bias_cross), bias_last]
        )
        input_grads = place_micro(
            input_grads, grad_source.astype(jnp.bfloat16), micro_index, is_valid
        )
    grad_qkv = grad_qkv + 0.0
    gain_shares = (
        lax.psum_scatter(grad_gain, "tensor", scatter_dimension=1, tiled=True),
        lax.psum_scatter(grad_bias, "tensor", scatter_dimension=1, tiled=True),
    )
    totals = (
        lax.psum(grad_qkv.astype(jnp.bfloat16), "dp").astype(jnp.float32),
        lax.psum(grad_out.astype(jnp.bfloat16), "dp").astype(jnp.float32),
        lax.psum(grad_cross.astype(jnp.bfloat16), "dp").astype(jnp.float32),
        lax.psum(grad_up.astype(jnp.bfloat16), "dp").astype(jnp.float32),
        lax.psum(grad_down.astype(jnp.bfloat16), "dp").astype(jnp.float32),
        lax.psum(gain_shares[0].astype(jnp.bfloat16), "dp").astype(jnp.float32),
        lax.psum(gain_shares[1].astype(jnp.bfloat16), "dp").astype(jnp.float32),
    )
    return (
        outputs[None],
        input_grads[None],
        totals[0][None],
        totals[1][None],
        totals[2][None],
        totals[3][None],
        totals[4][None],
        totals[5][None],
        totals[6][None],
    )


def solution(mesh):
    return jax.shard_map(
        on_device,
        mesh=mesh,
        in_specs=(
            P("section", None, ("dp", "tensor"), None),
            P(None, None, "dp", None),
            P(None, ("dp", "tensor"), None),
            P("section", None, "tensor"),
            P("section", "tensor", None),
            P("section", None, "tensor"),
            P("section", None, "tensor"),
            P("section", "tensor", None),
            P("section", None, None),
            P("section", None, None),
        ),
        out_specs=(
            P("section", None, ("dp", "tensor"), None),
            P("section", None, ("dp", "tensor"), None),
            P("section", None, "tensor"),
            P("section", "tensor", None),
            P("section", None, "tensor"),
            P("section", None, "tensor"),
            P("section", "tensor", None),
            P("section", None, "tensor"),
            P("section", None, "tensor"),
        ),
        check_vma=False,
    )
```

profile of v0, /device:TPU:0, one launch (start us, length us, event | category | flops | bytes accessed | tf_op | source)
XLA Modules:
  0.0 2358.9 jit_solution(11898195702888242948)
XLA Ops:
  16.0 28.2 %all-gather.43.cloned.1.call-done = bf16[512,1024]{1,0:T(8,128)(2,1)} async-done(((bf16[128,1024]{1,0:T(8,128)(2,1)}), bf16[512,1024]{1,0:T(8,128)(2,1)}) %all-gather.43.cloned.1.call-update) | async-done | bytes 1048592 | tf_op jit(solution)/shard_map/all_gather | solution.py:59
  56.9 27.3 %reduce-scatter.49.cloned.1.call-done = bf16[128,1024]{1,0:T(8,128)(2,1)} async-done(((bf16[512,1024]{1,0:T(8,128)(2,1)}), bf16[128,1024]{1,0:T(8,128)(2,1)}) %reduce-scatter.49.cloned.1.call-update) | async-done | bytes 262160 | tf_op jit(solution)/shard_map/reduce_scatter | solution.py:71
  93.6 22.2 all-gather.37.cloned.1.call-done
  130.0 15.0 all-gather.31.cloned.1.call-done
  158.6 15.4 all-gather.49.cloned.1.call-done
  187.7 15.3 all-gather.55.cloned.1.call-done
  217.0 17.5 reduce-scatter.43.cloned.1.call-done
  234.5 31.2 %reduce-scatter.37.cloned.1.call-done = bf16[128,1024]{1,0:T(8,128)(2,1)} async-done(((bf16[512,1024]{1,0:T(8,128)(2,1)}), bf16[128,1024]{1,0:T(8,128)(2,1)}) %reduce-scatter.37.cloned.1.call-update) | async-done | bytes 262160 | tf_op jit(solution)/shard_map/reduce_scatter | solution.py:71
  265.8 31.5 %reduce-scatter.55.cloned.1.call-done = bf16[128,1024]{1,0:T(8,128)(2,1)} async-done(((bf16[512,1024]{1,0:T(8,128)(2,1)}), bf16[128,1024]{1,0:T(8,128)(2,1)}) %reduce-scatter.55.cloned.1.call-update) | async-done | bytes 262160 | tf_op jit(solution)/shard_map/reduce_scatter | solution.py:71
  299.1 29.2 %reduce-scatter.61.cloned.1.call-done = bf16[128,1024]{1,0:T(8,128)(2,1)} async-done(((bf16[512,1024]{1,0:T(8,128)(2,1)}), bf16[128,1024]{1,0:T(8,128)(2,1)}) %reduce-scatter.61.cloned.1.call-update) | async-done | bytes 262160 | tf_op jit(solution)/shard_map/reduce_scatter | solution.py:71
  331.6 26.7 %all-gather.33.cloned.1.call-done = bf16[512,1024]{1,0:T(8,128)(2,1)} async-done(((bf16[128,1024]{1,0:T(8,128)(2,1)}), bf16[512,1024]{1,0:T(8,128)(2,1)}) %all-gather.33.cloned.1.call-update) | async-done | bytes 1048592 | tf_op jit(solution)/shard_map/all_gather | solution.py:59
  375.0 27.8 %reduce-scatter.39.cloned.1.call-done = bf16[128,1024]{1,0:T(8,128)(2,1)} async-done(((bf16[512,1024]{1,0:T(8,128)(2,1)}), bf16[128,1024]{1,0:T(8,128)(2,1)}) %reduce-scatter.39.cloned.1.call-update) | async-done | bytes 262160 | tf_op jit(solution)/shard_map/reduce_scatter | solution.py:71
  407.6 26.7 %all-gather.35.cloned.1.call-done = bf16[512,1024]{1,0:T(8,128)(2,1)} async-done(((bf16[128,1024]{1,0:T(8,128)(2,1)}), bf16[512,1024]{1,0:T(8,128)(2,1)}) %all-gather.35.cloned.1.call-update) | async-done | bytes 1048592 | tf_op jit(solution)/shard_map/all_gather | solution.py:59
  434.3 8.2 multiply_convert_fusion.14
  445.9 27.8 %reduce-scatter.41.cloned.1.call-done = bf16[128,1024]{1,0:T(8,128)(2,1)} async-done(((bf16[512,1024]{1,0:T(8,128)(2,1)}), bf16[128,1024]{1,0:T(8,128)(2,1)}) %reduce-scatter.41.cloned.1.call-update) | async-done | bytes 262160 | tf_op jit(solution)/shard_map/reduce_scatter | solution.py:71
  477.4 26.7 %all-gather.39.cloned.1.call-done = bf16[512,1024]{1,0:T(8,128)(2,1)} async-done(((bf16[128,1024]{1,0:T(8,128)(2,1)}), bf16[512,1024]{1,0:T(8,128)(2,1)}) %all-gather.39.cloned.1.call-update) | async-done | bytes 1048592 | tf_op jit(solution)/shard_map/all_gather | solution.py:59
  515.3 27.9 %reduce-scatter.45.cloned.1.call-done = bf16[128,1024]{1,0:T(8,128)(2,1)} async-done(((bf16[512,1024]{1,0:T(8,128)(2,1)}), bf16[128,1024]{1,0:T(8,128)(2,1)}) %reduce-scatter.45.cloned.1.call-update) | async-done | bytes 262160 | tf_op jit(solution)/shard_map/reduce_scatter | solution.py:71
  548.0 26.7 %all-gather.41.cloned.1.call-done = bf16[512,1024]{1,0:T(8,128)(2,1)} async-done(((bf16[128,1024]{1,0:T(8,128)(2,1)}), bf16[512,1024]{1,0:T(8,128)(2,1)}) %all-gather.41.cloned.1.call-update) | async-done | bytes 1048592 | tf_op jit(solution)/shard_map/all_gather | solution.py:59
  574.7 8.2 multiply_convert_fusion.13
  588.3 25.8 %reduce-scatter.47.cloned.1.call-done = bf16[128,1024]{1,0:T(8,128)(2,1)} async-done(((bf16[512,1024]{1,0:T(8,128)(2,1)}), bf16[128,1024]{1,0:T(8,128)(2,1)}) %reduce-scatter.47.cloned.1.call-update) | async-done | bytes 262160 | tf_op jit(solution)/shard_map/reduce_scatter | solution.py:71
  619.1 26.7 %all-gather.45.cloned.1.call-done = bf16[512,1024]{1,0:T(8,128)(2,1)} async-done(((bf16[128,1024]{1,0:T(8,128)(2,1)}), bf16[512,1024]{1,0:T(8,128)(2,1)}) %all-gather.45.cloned.1.call-update) | async-done | bytes 1048592 | tf_op jit(solution)/shard_map/all_gather | solution.py:59
  656.8 27.9 %reduce-scatter.51.cloned.1.call-done = bf16[128,1024]{1,0:T(8,128)(2,1)} async-done(((bf16[512,1024]{1,0:T(8,128)(2,1)}), bf16[128,1024]{1,0:T(8,128)(2,1)}) %reduce-scatter.51.cloned.1.call-update) | async-done | bytes 262160 | tf_op jit(solution)/shard_map/reduce_scatter | solution.py:71
  689.5 26.7 %all-gather.47.cloned.1.call-done = bf16[512,1024]{1,0:T(8,128)(2,1)} async-done(((bf16[128,1024]{1,0:T(8,128)(2,1)}), bf16[512,1024]{1,0:T(8,128)(2,1)}) %all-gather.47.cloned.1.call-update) | async-done | bytes 1048592 | tf_op jit(solution)/shard_map/all_gather | solution.py:59
  716.2 8.3 multiply_convert_fusion.12
  727.8 27.8 %reduce-scatter.53.cloned.1.call-done = bf16[128,1024]{1,0:T(8,128)(2,1)} async-done(((bf16[512,1024]{1,0:T(8,128)(2,1)}), bf16[128,1024]{1,0:T(8,128)(2,1)}) %reduce-scatter.53.cloned.1.call-update) | async-done | bytes 262160 | tf_op jit(solution)/shard_map/reduce_scatter | solution.py:71
  760.0 26.7 %all-gather.51.cloned.1.call-done = bf16[512,1024]{1,0:T(8,128)(2,1)} async-done(((bf16[128,1024]{1,0:T(8,128)(2,1)}), bf16[512,1024]{1,0:T(8,128)(2,1)}) %all-gather.51.cloned.1.call-update) | async-done | bytes 1048592 | tf_op jit(solution)/shard_map/all_gather | solution.py:59
  798.0 27.7 %reduce-scatter.57.cloned.1.call-done = bf16[128,1024]{1,0:T(8,128)(2,1)} async-done(((bf16[512,1024]{1,0:T(8,128)(2,1)}), bf16[128,1024]{1,0:T(8,128)(2,1)}) %reduce-scatter.57.cloned.1.call-update) | async-done | bytes 262160 | tf_op jit(solution)/shard_map/reduce_scatter | solution.py:71
  830.5 26.7 %all-gather.53.cloned.1.call-done = bf16[512,1024]{1,0:T(8,128)(2,1)} async-done(((bf16[128,1024]{1,0:T(8,128)(2,1)}), bf16[512,1024]{1,0:T(8,128)(2,1)}) %all-gather.53.cloned.1.call-update) | async-done | bytes 1048592 | tf_op jit(solution)/shard_map/all_gather | solution.py:59
  857.2 8.3 multiply_convert_fusion.11
  868.9 27.8 %reduce-scatter.59.cloned.1.call-done = bf16[128,1024]{1,0:T(8,128)(2,1)} async-done(((bf16[512,1024]{1,0:T(8,128)(2,1)}), bf16[128,1024]{1,0:T(8,128)(2,1)}) %reduce-scatter.59.cloned.1.call-update) | async-done | bytes 262160 | tf_op jit(solution)/shard_map/reduce_scatter | solution.py:71
  900.6 26.7 %all-gather.57.cloned.1.call-done = bf16[512,1024]{1,0:T(8,128)(2,1)} async-done(((bf16[128,1024]{1,0:T(8,128)(2,1)}), bf16[512,1024]{1,0:T(8,128)(2,1)}) %all-gather.57.cloned.1.call-update) | async-done | bytes 1048592 | tf_op jit(solution)/shard_map/all_gather | solution.py:59
  938.4 27.9 %reduce-scatter.63.cloned.1.call-done = bf16[128,1024]{1,0:T(8,128)(2,1)} async-done(((bf16[512,1024]{1,0:T(8,128)(2,1)}), bf16[128,1024]{1,0:T(8,128)(2,1)}) %reduce-scatter.63.cloned.1.call-update) | async-done | bytes 262160 | tf_op jit(solution)/shard_map/reduce_scatter | solution.py:71
  970.8 26.5 %all-gather.59.cloned.1.call-done = bf16[512,1024]{1,0:T(8,128)(2,1)} async-done(((bf16[128,1024]{1,0:T(8,128)(2,1)}), bf16[512,1024]{1,0:T(8,128)(2,1)}) %all-gather.59.cloned.1.call-update) | async-done | bytes 1048592 | tf_op jit(solution)/shard_map/all_gather | solution.py:59
  997.3 8.3 multiply_convert_fusion.10
  1008.9 27.8 %reduce-scatter.65.cloned.1.call-done = bf16[128,1024]{1,0:T(8,128)(2,1)} async-done(((bf16[512,1024]{1,0:T(8,128)(2,1)}), bf16[128,1024]{1,0:T(8,128)(2,1)}) %reduce-scatter.65.cloned.1.call-update) | async-done | bytes 262160 | tf_op jit(solution)/shard_map/reduce_scatter | solution.py:71
  1040.3 26.7 %all-gather.61.cloned.1.call-done = bf16[512,1024]{1,0:T(8,128)(2,1)} async-done(((bf16[128,1024]{1,0:T(8,128)(2,1)}), bf16[512,1024]{1,0:T(8,128)(2,1)}) %all-gather.61.cloned.1.call-update) | async-done | bytes 1048592 | tf_op jit(solution)/shard_map/all_gather | solution.py:63
  1075.4 27.8 %reduce-scatter.67.cloned.1.call-done = bf16[128,1024]{1,0:T(8,128)(2,1)} async-done(((bf16[512,1024]{1,0:T(8,128)(2,1)}), bf16[128,1024]{1,0:T(8,128)(2,1)}) %reduce-scatter.67.cloned.1.call-update) | async-done | bytes 262160 | tf_op jit(solution)/shard_map/reduce_scatter | solution.py:84
  1107.2 26.7 %all-gather.63.cloned.1.call-done = bf16[512,1024]{1,0:T(8,128)(2,1)} async-done(((bf16[128,1024]{1,0:T(8,128)(2,1)}), bf16[512,1024]{1,0:T(8,128)(2,1)}) %all-gather.63.cloned.1.call-update) | async-done | bytes 1048592 | tf_op jit(solution)/shard_map/all_gather | solution.py:63
  1148.9 27.8 %reduce-scatter.69.cloned.1.call-done = bf16[128,1024]{1,0:T(8,128)(2,1)} async-done(((bf16[512,1024]{1,0:T(8,128)(2,1)}), bf16[128,1024]{1,0:T(8,128)(2,1)}) %reduce-scatter.69.cloned.1.call-update) | async-done | bytes 262160 | tf_op jit(solution)/shard_map/reduce_scatter | solution.py:84
  1181.0 26.7 %all-gather.67.cloned.1.call-done = bf16[512,1024]{1,0:T(8,128)(2,1)} async-done(((bf16[128,1024]{1,0:T(8,128)(2,1)}), bf16[512,1024]{1,0:T(8,128)(2,1)}) %all-gather.67.cloned.1.call-update) | async-done | bytes 1048592 | tf_op jit(solution)/shard_map/all_gather | solution.py:63
  1216.1 27.8 %reduce-scatter.73.cloned.1.call-done = bf16[128,1024]{1,0:T(8,128)(2,1)} async-done(((bf16[512,1024]{1,0:T(8,128)(2,1)}), bf16[128,1024]{1,0:T(8,128)(2,1)}) %reduce-scatter.73.cloned.1.call-update) | async-done | bytes 262160 | tf_op jit(solution)/shard_map/reduce_scatter | solution.py:84
  1247.4 26.7 %all-gather.69.cloned.1.call-done = bf16[512,1024]{1,0:T(8,128)(2,1)} async-done(((bf16[128,1024]{1,0:T(8,128)(2,1)}), bf16[512,1024]{1,0:T(8,128)(2,1)}) %all-gather.69.cloned.1.call-update) | async-done | bytes 1048592 | tf_op jit(solution)/shard_map/all_gather | solution.py:63
  1288.9 27.8 %reduce-scatter.75.cloned.1.call-done = bf16[128,1024]{1,0:T(8,128)(2,1)} async-done(((bf16[512,1024]{1,0:T(8,128)(2,1)}), bf16[128,1024]{1,0:T(8,128)(2,1)}) %reduce-scatter.75.cloned.1.call-update) | async-done | bytes 262160 | tf_op jit(solution)/shard_map/reduce_scatter | solution.py:84
  1321.5 26.6 %all-gather.73.cloned.1.call-done = bf16[512,1024]{1,0:T(8,128)(2,1)} async-done(((bf16[128,1024]{1,0:T(8,128)(2,1)}), bf16[512,1024]{1,0:T(8,128)(2,1)}) %all-gather.73.cloned.1.call-update) | async-done | bytes 1048592 | tf_op jit(solution)/shard_map/all_gather | solution.py:63
  1356.4 27.8 %reduce-scatter.79.cloned.1.call-done = bf16[128,1024]{1,0:T(8,128)(2,1)} async-done(((bf16[512,1024]{1,0:T(8,128)(2,1)}), bf16[128,1024]{1,0:T(8,128)(2,1)}) %reduce-scatter.79.cloned.1.call-update) | async-done | bytes 262160 | tf_op jit(solution)/shard_map/reduce_scatter | solution.py:84
  1387.9 26.7 %all-gather.75.cloned.1.call-done = bf16[512,1024]{1,0:T(8,128)(2,1)} async-done(((bf16[128,1024]{1,0:T(8,128)(2,1)}), bf16[512,1024]{1,0:T(8,128)(2,1)}) %all-gather.75.cloned.1.call-update) | async-done | bytes 1048592 | tf_op jit(solution)/shard_map/all_gather | solution.py:63
  1429.5 27.8 %reduce-scatter.81.cloned.1.call-done = bf16[128,1024]{1,0:T(8,128)(2,1)} async-done(((bf16[512,1024]{1,0:T(8,128)(2,1)}), bf16[128,1024]{1,0:T(8,128)(2,1)}) %reduce-scatter.81.cloned.1.call-update) | async-done | bytes 262160 | tf_op jit(solution)/shard_map/reduce_scatter | solution.py:84
  1461.9 26.7 %all-gather.79.cloned.1.call-done = bf16[512,1024]{1,0:T(8,128)(2,1)} async-done(((bf16[128,1024]{1,0:T(8,128)(2,1)}), bf16[512,1024]{1,0:T(8,128)(2,1)}) %all-gather.79.cloned.1.call-update) | async-done | bytes 1048592 | tf_op jit(solution)/shard_map/all_gather | solution.py:63
  1497.1 27.6 %reduce-scatter.85.cloned.1.call-done = bf16[128,1024]{1,0:T(8,128)(2,1)} async-done(((bf16[512,1024]{1,0:T(8,128)(2,1)}), bf16[128,1024]{1,0:T(8,128)(2,1)}) %reduce-scatter.85.cloned.1.call-update) | async-done | bytes 262160 | tf_op jit(solution)/shard_map/reduce_scatter | solution.py:84
  1533.5 25.0 %all-gather.81.cloned.1.call-done = bf16[512,1024]{1,0:T(8,128)(2,1)} async-done(((bf16[128,1024]{1,0:T(8,128)(2,1)}), bf16[512,1024]{1,0:T(8,128)(2,1)}) %all-gather.81.cloned.1.call-update) | async-done | bytes 1048592 | tf_op jit(solution)/shard_map/all_gather | solution.py:63
  1638.2 19.6 all-gather.85.cloned.1.call-done
  1699.7 18.1 reduce-scatter.91.cloned.1.call-done
  1739.5 9.4 reduce-scatter.83.cloned.1.call-done
  1748.9 31.5 %reduce-scatter.77.cloned.1.call-done = bf16[128,1024]{1,0:T(8,128)(2,1)} async-done(((bf16[512,1024]{1,0:T(8,128)(2,1)}), bf16[128,1024]{1,0:T(8,128)(2,1)}) %reduce-scatter.77.cloned.1.call-update) | async-done | bytes 262160 | tf_op jit(solution)/shard_map/reduce_scatter | solution.py:84
  1783.1 26.2 %all-gather.87.cloned.1.call-done = bf16[512,1024]{1,0:T(8,128)(2,1)} async-done(((bf16[128,1024]{1,0:T(8,128)(2,1)}), bf16[512,1024]{1,0:T(8,128)(2,1)}) %all-gather.87.cloned.1.call-update) | async-done | bytes 1048592 | tf_op jit(solution)/shard_map/all_gather | solution.py:63
  1825.8 9.8 fusion.131
  1849.6 19.5 reduce-scatter.93.cloned.1.call-done
  1884.2 13.5 all-gather.65.cloned.1.call-done
  1961.6 27.8 %reduce-scatter.71.cloned.1.call-done = bf16[128,1024]{1,0:T(8,128)(2,1)} async-done(((bf16[512,1024]{1,0:T(8,128)(2,1)}), bf16[128,1024]{1,0:T(8,128)(2,1)}) %reduce-scatter.71.cloned.1.call-update) | async-done | bytes 262160 | tf_op jit(solution)/shard_map/reduce_scatter | solution.py:84
  1989.3 31.5 %reduce-scatter.95.cloned.1.call-done = bf16[128,1024]{1,0:T(8,128)(2,1)} async-done(((bf16[512,1024]{1,0:T(8,128)(2,1)}), bf16[128,1024]{1,0:T(8,128)(2,1)}) %reduce-scatter.95.cloned.1.call-update) | async-done | bytes 262160 | tf_op jit(solution)/shard_map/reduce_scatter | solution.py:84
  2040.7 10.1 reduce-scatter.99.cloned.1.call-done
  2051.8 27.5 %reduce-scatter.97.cloned.1.call-done = f32[256,3]{1,0:T(8,128)} async-done(((f32[1024,3]{1,0:T(8,128)}), f32[256,3]{1,0:T(8,128)}) %reduce-scatter.97.cloned.1.call-update) | async-done | bytes 3088
  2080.2 11.8 all-reduce.10
  2093.2 247.4 %all-reduce.14.cloned.1.call-done = (bf16[1,1024,768]{2,1,0:T(8,128)(2,1)}, bf16[1,256,1024]{2,1,0:T(8,128)(2,1)}, bf16[1,1024,512]{2,1,0:T(8,128)(2,1)}, bf16[1...) async-done(((bf16[1,1024,768]{2,1,0:T(8,128)(2,1)}, bf16[1,256,1024]{2,1,0:T(8,128)(2,1)}, bf16[1,1024,512]{2,1,0:T(8,128)(2,1)}, bf16[1,1024,1024]{2,1,0:T(8,128)(2,1)}, ...) | async-done | bytes 7340048 | tf_op jit(solution)/shard_map/psum | solution.py:402
  (1247 shorter events, 611.9 us)
Async XLA Ops:
  7.2 37.0 %all-gather.43.cloned.1.call-start = ((), (), s32[]{:S(2)}) async-start(), calls=%async_computation.44 | async-start | bytes 1310720 | tf_op jit(solution)/shard_map/all_gather | solution.py:59
  14.7 69.5 %reduce-scatter.49.cloned.1.call-start = ((), (), s32[]{:S(2)}) async-start(), calls=%async_computation.45 | async-start | bytes 1310720 | tf_op jit(solution)/shard_map/reduce_scatter | solution.py:71
  56.3 59.5 %all-gather.37.cloned.1.call-start = ((), (), s32[]{:S(2)}) async-start(), calls=%async_computation.38 | async-start | bytes 1310720 | tf_op jit(solution)/shard_map/all_gather | solution.py:59
  89.1 55.9 %all-gather.31.cloned.1.call-start = ((), (), s32[]{:S(2)}) async-start(), calls=%async_computation.32 | async-start | bytes 1310720 | tf_op jit(solution)/shard_map/all_gather | solution.py:59
  89.6 84.3 %all-gather.49.cloned.1.call-start = ((), (), s32[]{:S(2)}) async-start(), calls=%async_computation.50 | async-start | bytes 1310720 | tf_op jit(solution)/shard_map/all_gather | solution.py:59
  90.2 112.8 %all-gather.55.cloned.1.call-start = ((), (), s32[]{:S(2)}) async-start(), calls=%async_computation.56 | async-start | bytes 1310720 | tf_op jit(solution)/shard_map/all_gather | solution.py:59
  93.6 141.0 %reduce-scatter.43.cloned.1.call-start = ((), (), s32[]{:S(2)}) async-start(), calls=%async_computation.39 | async-start | bytes 1310720 | tf_op jit(solution)/shard_map/reduce_scatter | solution.py:71
  129.4 136.3 %reduce-scatter.37.cloned.1.call-start = ((), (), s32[]{:S(2)}) async-start(), calls=%async_computation.33 | async-start | bytes 1310720 | tf_op jit(solution)/shard_map/reduce_scatter | solution.py:71
  158.6 138.6 %reduce-scatter.55.cloned.1.call-start = ((), (), s32[]{:S(2)}) async-start(), calls=%async_computation.51 | async-start | bytes 1310720 | tf_op jit(solution)/shard_map/reduce_scatter | solution.py:71
  187.7 140.6 %reduce-scatter.61.cloned.1.call-start = ((), (), s32[]{:S(2)}) async-start(), calls=%async_computation.57 | async-start | bytes 1310720 | tf_op jit(solution)/shard_map/reduce_scatter | solution.py:71
  216.8 141.5 %all-gather.33.cloned.1.call-start = ((), (), s32[]{:S(2)}) async-start(), calls=%async_computation.34 | async-start | bytes 1310720 | tf_op jit(solution)/shard_map/all_gather | solution.py:59
  331.6 71.2 %reduce-scatter.39.cloned.1.call-start = ((), (), s32[]{:S(2)}) async-start(), calls=%async_computation.35 | async-start | bytes 1310720 | tf_op jit(solution)/shard_map/reduce_scatter | solution.py:71
  361.4 6.0 collective-permute-start
  374.9 59.4 %all-gather.35.cloned.1.call-start = ((), (), s32[]{:S(2)}) async-start(), calls=%async_computation.36 | async-start | bytes 1310720 | tf_op jit(solution)/shard_map/all_gather | solution.py:59
  407.6 66.1 %reduce-scatter.41.cloned.1.call-start = ((), (), s32[]{:S(2)}) async-start(), calls=%async_computation.37 | async-start | bytes 1310720 | tf_op jit(solution)/shard_map/reduce_scatter | solution.py:71
  445.8 58.4 %all-gather.39.cloned.1.call-start = ((), (), s32[]{:S(2)}) async-start(), calls=%async_computation.40 | async-start | bytes 1310720 | tf_op jit(solution)/shard_map/all_gather | solution.py:59
  477.4 65.8 %reduce-scatter.45.cloned.1.call-start = ((), (), s32[]{:S(2)}) async-start(), calls=%async_computation.41 | async-start | bytes 1310720 | tf_op jit(solution)/shard_map/reduce_scatter | solution.py:71
  515.3 59.5 %all-gather.41.cloned.1.call-start = ((), (), s32[]{:S(2)}) async-start(), calls=%async_computation.42 | async-start | bytes 1310720 | tf_op jit(solution)/shard_map/all_gather | solution.py:59
  547.9 66.1 %reduce-scatter.47.cloned.1.call-start = ((), (), s32[]{:S(2)}) async-start(), calls=%async_computation.43 | async-start | bytes 1310720 | tf_op jit(solution)/shard_map/reduce_scatter | solution.py:71
  586.2 59.6 %all-gather.45.cloned.1.call-start = ((), (), s32[]{:S(2)}) async-start(), calls=%async_computation.46 | async-start | bytes 1310720 | tf_op jit(solution)/shard_map/all_gather | solution.py:59
  619.0 65.6 %reduce-scatter.51.cloned.1.call-start = ((), (), s32[]{:S(2)}) async-start(), calls=%async_computation.47 | async-start | bytes 1310720 | tf_op jit(solution)/shard_map/reduce_scatter | solution.py:71
  656.8 59.4 %all-gather.47.cloned.1.call-start = ((), (), s32[]{:S(2)}) async-start(), calls=%async_computation.48 | async-start | bytes 1310720 | tf_op jit(solution)/shard_map/all_gather | solution.py:59
  689.4 66.2 %reduce-scatter.53.cloned.1.call-start = ((), (), s32[]{:S(2)}) async-start(), calls=%async_computation.49 | async-start | bytes 1310720 | tf_op jit(solution)/shard_map/reduce_scatter | solution.py:71
  727.7 59.0 %all-gather.51.cloned.1.call-start = ((), (), s32[]{:S(2)}) async-start(), calls=%async_computation.52 | async-start | bytes 1310720 | tf_op jit(solution)/shard_map/all_gather | solution.py:59
  760.0 65.7 %reduce-scatter.57.cloned.1.call-start = ((), (), s32[]{:S(2)}) async-start(), calls=%async_computation.53 | async-start | bytes 1310720 | tf_op jit(solution)/shard_map/reduce_scatter | solution.py:71
  797.8 59.4 %all-gather.53.cloned.1.call-start = ((), (), s32[]{:S(2)}) async-start(), calls=%async_computation.54 | async-start | bytes 1310720 | tf_op jit(solution)/shard_map/all_gather | solution.py:59
  830.5 66.2 %reduce-scatter.59.cloned.1.call-start = ((), (), s32[]{:S(2)}) async-start(), calls=%async_computation.55 | async-start | bytes 1310720 | tf_op jit(solution)/shard_map/reduce_scatter | solution.py:71
  868.8 58.5 %all-gather.57.cloned.1.call-start = ((), (), s32[]{:S(2)}) async-start(), calls=%async_computation.58 | async-start | bytes 1310720 | tf_op jit(solution)/shard_map/all_gather | solution.py:59
  900.5 65.7 %reduce-scatter.63.cloned.1.call-start = ((), (), s32[]{:S(2)}) async-start(), calls=%async_computation.59 | async-start | bytes 1310720 | tf_op jit(solution)/shard_map/reduce_scatter | solution.py:71
  938.3 58.9 %all-gather.59.cloned.1.call-start = ((), (), s32[]{:S(2)}) async-start(), calls=%async_computation.60 | async-start | bytes 1310720 | tf_op jit(solution)/shard_map/all_gather | solution.py:59
  970.5 66.2 %reduce-scatter.65.cloned.1.call-start = ((), (), s32[]{:S(2)}) async-start(), calls=%async_computation.61 | async-start | bytes 1310720 | tf_op jit(solution)/shard_map/reduce_scatter | solution.py:71
  1008.8 58.3 %all-gather.61.cloned.1.call-start = ((), (), s32[]{:S(2)}) async-start(), calls=%async_computation.62 | async-start | bytes 1310720 | tf_op jit(solution)/shard_map/all_gather | solution.py:63
  1040.3 63.0 %reduce-scatter.67.cloned.1.call-start = ((), (), s32[]{:S(2)}) async-start(), calls=%async_computation.63 | async-start | bytes 1310720 | tf_op jit(solution)/shard_map/reduce_scatter | solution.py:84
  1075.4 58.5 %all-gather.63.cloned.1.call-start = ((), (), s32[]{:S(2)}) async-start(), calls=%async_computation.64 | async-start | bytes 1310720 | tf_op jit(solution)/shard_map/all_gather | solution.py:63
  1107.1 69.6 %reduce-scatter.69.cloned.1.call-start = ((), (), s32[]{:S(2)}) async-start(), calls=%async_computation.65 | async-start | bytes 1310720 | tf_op jit(solution)/shard_map/reduce_scatter | solution.py:84
  1148.9 58.8 %all-gather.67.cloned.1.call-start = ((), (), s32[]{:S(2)}) async-start(), calls=%async_computation.68 | async-start | bytes 1310720 | tf_op jit(solution)/shard_map/all_gather | solution.py:63
  1180.9 63.0 %reduce-scatter.73.cloned.1.call-start = ((), (), s32[]{:S(2)}) async-start(), calls=%async_computation.69 | async-start | bytes 1310720 | tf_op jit(solution)/shard_map/reduce_scatter | solution.py:84
  1216.0 58.1 %all-gather.69.cloned.1.call-start = ((), (), s32[]{:S(2)}) async-start(), calls=%async_computation.70 | async-start | bytes 1310720 | tf_op jit(solution)/shard_map/all_gather | solution.py:63
  1247.3 69.5 %reduce-scatter.75.cloned.1.call-start = ((), (), s32[]{:S(2)}) async-start(), calls=%async_computation.71 | async-start | bytes 1310720 | tf_op jit(solution)/shard_map/reduce_scatter | solution.py:84
  1288.9 59.2 %all-gather.73.cloned.1.call-start = ((), (), s32[]{:S(2)}) async-start(), calls=%async_computation.74 | async-start | bytes 1310720 | tf_op jit(solution)/shard_map/all_gather | solution.py:63
  1321.3 62.9 %reduce-scatter.79.cloned.1.call-start = ((), (), s32[]{:S(2)}) async-start(), calls=%async_computation.75 | async-start | bytes 1310720 | tf_op jit(solution)/shard_map/reduce_scatter | solution.py:84
  1356.3 58.3 %all-gather.75.cloned.1.call-start = ((), (), s32[]{:S(2)}) async-start(), calls=%async_computation.76 | async-start | bytes 1310720 | tf_op jit(solution)/shard_map/all_gather | solution.py:63
  1387.8 69.5 %reduce-scatter.81.cloned.1.call-start = ((), (), s32[]{:S(2)}) async-start(), calls=%async_computation.77 | async-start | bytes 1310720 | tf_op jit(solution)/shard_map/reduce_scatter | solution.py:84
  1429.4 59.2 %all-gather.79.cloned.1.call-start = ((), (), s32[]{:S(2)}) async-start(), calls=%async_computation.80 | async-start | bytes 1310720 | tf_op jit(solution)/shard_map/all_gather | solution.py:63
  1461.8 62.9 %reduce-scatter.85.cloned.1.call-start = ((), (), s32[]{:S(2)}) async-start(), calls=%async_computation.81 | async-start | bytes 1310720 | tf_op jit(solution)/shard_map/reduce_scatter | solution.py:84
  1496.8 61.6 %all-gather.81.cloned.1.call-start = ((), (), s32[]{:S(2)}) async-start(), calls=%async_computation.82 | async-start | bytes 1310720 | tf_op jit(solution)/shard_map/all_gather | solution.py:63
  1531.7 75.1 %reduce-scatter.87.cloned.1.call-start = ((), (), s32[]{:S(2)}) async-start(), calls=%async_computation.83 | async-start | bytes 1310720 | tf_op jit(solution)/shard_map/reduce_scatter | solution.py:84
  1572.4 63.4 %all-gather.77.cloned.1.call-start = ((), (), s32[]{:S(2)}) async-start(), calls=%async_computation.78 | async-start | bytes 1310720 | tf_op jit(solution)/shard_map/all_gather | solution.py:63
  1593.1 64.7 %all-gather.85.cloned.1.call-start = ((), (), s32[]{:S(2)}) async-start(), calls=%async_computation.86 | async-start | bytes 1310720 | tf_op jit(solution)/shard_map/all_gather | solution.py:63
  1610.5 75.9 %all-gather.71.cloned.1.call-start = ((), (), s32[]{:S(2)}) async-start(), calls=%async_computation.72 | async-start | bytes 1310720 | tf_op jit(solution)/shard_map/all_gather | solution.py:63
  1630.9 87.0 %reduce-scatter.91.cloned.1.call-start = ((), (), s32[]{:S(2)}) async-start(), calls=%async_computation.87 | async-start | bytes 1310720 | tf_op jit(solution)/shard_map/reduce_scatter | solution.py:84
  1666.1 82.9 %reduce-scatter.83.cloned.1.call-start = ((), (), s32[]{:S(2)}) async-start(), calls=%async_computation.79 | async-start | bytes 1310720 | tf_op jit(solution)/shard_map/reduce_scatter | solution.py:84
  1678.3 102.1 %reduce-scatter.77.cloned.1.call-start = ((), (), s32[]{:S(2)}) async-start(), calls=%async_computation.73 | async-start | bytes 1310720 | tf_op jit(solution)/shard_map/reduce_scatter | solution.py:84
  1699.7 109.6 %all-gather.87.cloned.1.call-start = ((), (), s32[]{:S(2)}) async-start(), calls=%async_computation.88 | async-start | bytes 1310720 | tf_op jit(solution)/shard_map/all_gather | solution.py:63
  1724.0 117.9 %all-gather.83.cloned.1.call-start = ((), (), s32[]{:S(2)}) async-start(), calls=%async_computation.84 | async-start | bytes 1310720 | tf_op jit(solution)/shard_map/all_gather | solution.py:63
  1783.0 86.0 %reduce-scatter.93.cloned.1.call-start = ((), (), s32[]{:S(2)}) async-start(), calls=%async_computation.89 | async-start | bytes 1310720 | tf_op jit(solution)/shard_map/reduce_scatter | solution.py:84
  1825.0 72.8 %all-gather.65.cloned.1.call-start = ((), (), s32[]{:S(2)}) async-start(), calls=%async_computation.66 | async-start | bytes 1310720 | tf_op jit(solution)/shard_map/all_gather | solution.py:63
  1841.9 85.1 %all-gather.89.cloned.1.call-start = ((), (), s32[]{:S(2)}) async-start(), calls=%async_computation.90 | async-start | bytes 1310720 | tf_op jit(solution)/shard_map/all_gather | solution.py:63
  1872.0 89.5 %reduce-scatter.89.cloned.1.call-start = ((), (), s32[]{:S(2)}) async-start(), calls=%async_computation.85 | async-start | bytes 1310720 | tf_op jit(solution)/shard_map/reduce_scatter | solution.py:84
  1883.9 105.4 %reduce-scatter.71.cloned.1.call-start = ((), (), s32[]{:S(2)}) async-start(), calls=%async_computation.67 | async-start | bytes 1310720 | tf_op jit(solution)/shard_map/reduce_scatter | solution.py:84
  1911.1 109.7 %reduce-scatter.95.cloned.1.call-start = ((), (), s32[]{:S(2)}) async-start(), calls=%async_computation.91 | async-start | bytes 1310720 | tf_op jit(solution)/shard_map/reduce_scatter | solution.py:84
  1940.3 110.6 %reduce-scatter.99.cloned.1.call-start = ((), (), s32[]{:S(2)}) async-start(), calls=%async_computation.93 | async-start | bytes 655360
  2025.9 53.4 %reduce-scatter.97.cloned.1.call-start = ((), (), s32[]{:S(2)}) async-start(), calls=%async_computation.92 | async-start | bytes 655360
  2027.9 312.8 %all-reduce.14.cloned.1.call-start = ((), (), s32[]{:S(2)}) async-start(), calls=%async_computation.94 | async-start | bytes 14680064 | tf_op jit(solution)/shard_map/psum | solution.py:402
  (345 other events, 7431.8 us)
Sparse Core Ops, SparseCore 0:
  14.9 29.3 all-gather.42
  56.5 27.7 reduce-scatter.48
  89.2 26.6 all-gather.36
  118.3 26.6 all-gather.30
  147.3 26.6 all-gather.48
  176.4 26.6 all-gather.54
  206.8 27.6 reduce-scatter.42
  238.0 27.7 reduce-scatter.36
  269.5 27.7 reduce-scatter.54
  300.6 27.7 reduce-scatter.60
  331.7 26.6 all-gather.32
  375.0 27.7 reduce-scatter.38
  407.7 26.6 all-gather.34
  445.9 27.7 reduce-scatter.40
  477.5 26.6 all-gather.38
  515.4 27.7 reduce-scatter.44
  548.1 26.6 all-gather.40
  586.3 27.7 reduce-scatter.46
  619.2 26.6 all-gather.44
  656.9 27.7 reduce-scatter.50
  689.6 26.6 all-gather.46
  727.8 27.7 reduce-scatter.52
  760.1 26.6 all-gather.50
  797.9 27.7 reduce-scatter.56
  830.6 26.6 all-gather.52
  868.9 27.7 reduce-scatter.58
  900.6 26.6 all-gather.56
  938.4 27.7 reduce-scatter.62
  970.6 26.6 all-gather.58
  1008.9 27.7 reduce-scatter.64
  1040.4 26.6 all-gather.60
  1075.5 27.7 reduce-scatter.66
  1107.2 26.6 all-gather.62
  1149.0 27.6 reduce-scatter.68
  1181.0 26.6 all-gather.66
  1216.1 27.7 reduce-scatter.72
  1247.4 26.6 all-gather.68
  1289.0 27.7 reduce-scatter.74
  1321.4 26.6 all-gather.72
  1356.4 27.7 reduce-scatter.78
  1387.9 26.6 all-gather.74
  1429.5 27.7 reduce-scatter.80
  1461.9 26.6 all-gather.78
  1497.0 27.7 reduce-scatter.84
  1531.8 26.6 all-gather.80
  1572.5 27.7 reduce-scatter.86
  1602.1 26.6 all-gather.76
  1631.2 26.6 all-gather.84
  1659.7 26.6 all-gather.70
  1690.1 27.7 reduce-scatter.90
  1721.2 27.7 reduce-scatter.82
  1752.7 27.6 reduce-scatter.76
  1782.7 26.6 all-gather.86
  1811.2 26.6 all-gather.82
  1841.3 27.7 reduce-scatter.92
  1871.0 26.6 all-gather.64
  1900.3 26.6 all-gather.88
  1930.5 27.6 reduce-scatter.88
  1961.6 27.7 reduce-scatter.70
  1993.0 27.6 reduce-scatter.94
  2026.0 24.7 reduce-scatter.98
  2054.5 24.7 reduce-scatter.96
  2082.4 258.1 all-reduce.13
where the time goes:
time: 2370 us; the launch traced here: 2360 us
  waiting for transfers between devices  1700 us (72%)
  matrix products  351 us (15%)
  other arithmetic  155 us (7%)
  local copies, waits for them, and re-layouts  102 us (4%)
    reduce_scatter x15, waiting for transfers between devices, sum_rows(): lax.psum_scatter(partial_term(jnp.int32(0), share_rows * lax.axis_size('t...  413 us
    all_gather x15, waiting for transfers between devices, gather_rows(): return lax.all_gather(rows_low, 'tensor', axis=0, tiled=True)  363 us
    reduce_scatter x15, waiting for transfers between devices, sum_grads(): lax.psum_scatter(partial_term(jnp.int32(0), share_rows * lax.axis_size('t...  332 us
    all_gather x15, waiting for transfers between devices, gather_grads(): return lax.all_gather(grads_low, 'tensor', axis=0, tiled=True)  287 us
    psum x1, waiting for transfers between devices, on_device(): lax.psum(grad_qkv.astype(jnp.bfloat16), 'dp').astype(jnp.float32)  247 us
    dot_general x30, matrix products, rows_product(): lax.dot_general(left, right, (((0,), (0,)), ((), ())), preferred_element_...  92.7 us
    dot_general x30, matrix products, transposed_product(): lax.dot_general(left, right, (((1,), (1,)), ((), ())), preferred_element_...  73.9 us
    unnamed x681, local copies, waits for them, and re-layouts  60.8 us
  transfers between devices with their start and end apart: 73, of which 68 were waited for; matrix products, arithmetic and copies ran while one was open for 12% of the time, Pallas kernels for 0%

commit v1 on v0

v1 whole, which is shorter than its diff:
```python
import math

import jax
import jax.numpy as jnp
from jax import lax
from jax.experimental import pallas as pl
from jax.experimental.pallas import tpu as pltpu
from jax.sharding import PartitionSpec as P

HD = 64
EPS = 1e-05
MASKED = -1e30
BF = jnp.bfloat16
F32 = jnp.float32
VMEM_SPARE = 6 * 1024 * 1024
GELU_C = 0.7071067811865476
PHI_C = 0.3989422804014327


LIGHT = pl.CostEstimate(flops=1024, bytes_accessed=1024, transcendentals=0)


def mm(a, b):
    return jnp.dot(a, b, preferred_element_type=F32)


def mm_bt(a, b):
    return lax.dot_general(a, b, (((1,), (1,)), ((), ())), preferred_element_type=F32)


def mm_at(a, b):
    return lax.dot_general(a, b, (((0,), (0,)), ((), ())), preferred_element_type=F32)


def spec(shape, dtype=BF):
    return jax.ShapeDtypeStruct(shape, dtype)


class Saved:
    def __init__(self, shape, dtype=BF):
        self.shape, self.dtype, self.size = shape, jnp.dtype(dtype), math.prod(shape)


def in_hbm(array):
    return pltpu.with_memory_space_constraint(array, pltpu.HBM)


class Near:
    def __init__(self, shape, p, q=None, at=0):
        self.shape, self.p, self.q, self.at = shape, p, q, at
        self.dtype, self.size = p.dtype, shape[0] * shape[1]


STRICT = [True]
ORDER = []


def in_order(deps):
    return (*deps, *ORDER[-1:]) if STRICT[-1] else tuple(deps)


def note(results):
    ORDER.append(results[0] if isinstance(results, (tuple, list)) else results)
    return results


def sectioned(
    body, core, flags, small, big, outs, scratch, flops, trans=0, deps=(), owners=None, sums=()
):
    deps = in_order(deps)
    terms = [array for chain in sums for array in (chain.value, chain.got)]
    n_terms = len(terms)
    sources, places = [], []
    for i, array in enumerate(big):
        if isinstance(array, Near) and array.q is None:
            places.append((i, array.shape[0], array.at, None))
            sources.append(array.p)
        elif isinstance(array, Near):
            half = array.shape[0] // 2
            for turn, part in enumerate((array.p, array.q)):
                places.append((i, half, array.at, turn))
                sources.append(part)
        else:
            places.append((i, None, None, None))
            sources.append(array)
    n_small, n_big, n_deps, n_out = len(small), len(big), len(deps), len(outs)
    n_src = len(sources)

    def kernel(flags_ref, *refs):
        small_refs = refs[:n_small]
        big_hbm = refs[n_small : n_small + n_src]
        at = n_small + n_src
        term_hbm = refs[at : at + n_terms]
        at += n_terms + n_deps
        out_hbm = refs[at : at + n_out]
        at += n_out
        sum_hbm = refs[at : at + len(sums)]
        at += len(sums)
        big_refs = refs[at : at + n_big]
        at += n_big
        out_refs = refs[at : at + n_out]
        at += n_out
        term_refs = refs[at : at + n_terms]
        at += n_terms
        extra = refs[at:-4]
        in_sem, out_sem, term_sem, sum_sem = refs[-4:]

        def start_sums():
            loads = [
                pltpu.make_async_copy(term_hbm[i], term_refs[i], term_sem.at[i])
                for i in range(n_terms)
            ]
            for load in loads:
                load.start()
            return loads

        def end_sums(loads):
            stores = []
            for i in range(len(sums)):
                loads[2 * i].wait()
                loads[2 * i + 1].wait()
                a_ref, b_ref = term_refs[2 * i], term_refs[2 * i + 1]
                chunk = 64 if a_ref.shape[0] % 64 == 0 else a_ref.shape[0]

                @pl.loop(0, a_ref.shape[0] // chunk)
                def _(r):
                    at = pl.ds(pl.multiple_of(r * chunk, chunk), chunk)
                    a_ref[at, :] = (a_ref[at, :].astype(F32) + b_ref[at, :].astype(F32)).astype(BF)

                stores.append(pltpu.make_async_copy(a_ref, sum_hbm[i], sum_sem.at[i]))
                stores[-1].start()
            return stores

        def run():
            copies = [[] for _ in range(n_big)]
            for s, (i, half, first, turn) in enumerate(places):
                if half is None:
                    copy = pltpu.make_async_copy(big_hbm[s], big_refs[i], in_sem.at[s])
                elif turn is None:
                    copy = pltpu.make_async_copy(
                        big_hbm[s].at[pl.ds(first, half), :], big_refs[i], in_sem.at[s]
                    )
                else:
                    odd = flags_ref[1] if turn == 0 else 1 - flags_ref[1]
                    copy = pltpu.make_async_copy(
                        big_hbm[s].at[pl.ds(first, half), :],
                        big_refs[i].at[pl.ds(pl.multiple_of(odd * half, half), half), :],
                        in_sem.at[s],
                    )
                if owners is None:
                    copy.start()
                else:
                    pl.when(flags_ref[0] == owners[i])(copy.start)
                copies[i].append(copy)
            done = [
                pltpu.make_async_copy(out_refs[i], out_hbm[i], out_sem.at[i]) for i in range(n_out)
            ]
            loads = start_sums() if sums and core is not None else None
            body(
                flags_ref, small_refs, big_refs, out_refs, extra,
                lambda *which: [copy.wait() for i in which for copy in copies[i]],
                lambda *which: [done[i].start() for i in which],
            )
            if loads:
                done.extend(end_sums(loads))
            for copy in done:
                copy.wait()

        if core is None:
            run()
        else:
            pl.when(flags_ref[0] == core)(run)
        if sums and core is None:

            @pl.when(flags_ref[0] == sums[0].core)
            def _():
                for copy in end_sums(start_sums()):
                    copy.wait()

    nbytes = sum(a.size * a.dtype.itemsize for a in (*big, *outs))
    nbytes += sum(a.size * 2 for a in terms)
    held = nbytes + sum(math.prod(a.shape) * jnp.dtype(a.dtype).itemsize for a in scratch)
    results = note(pl.pallas_call(
        kernel,
        out_shape=tuple(pltpu.HBM(a.shape, a.dtype) if isinstance(a, Saved) else a for a in outs)
        + tuple(spec(chain.value.shape) for chain in sums),
        in_specs=[pl.BlockSpec(memory_space=pltpu.SMEM)]
        + [pl.BlockSpec(memory_space=pltpu.VMEM)] * n_small
        + [pl.BlockSpec(memory_space=pl.ANY)] * (n_src + n_terms + n_deps),
        out_specs=tuple(
            pl.BlockSpec(memory_space=pltpu.HBM if isinstance(a, Saved) else pl.ANY) for a in outs
        )
        + tuple([pl.BlockSpec(memory_space=pl.ANY)] * len(sums)),
        scratch_shapes=[pltpu.VMEM(a.shape, a.dtype) for a in (*big, *outs)]
        + [pltpu.VMEM(a.shape, BF) for a in terms]
        + list(scratch)
        + [
            pltpu.SemaphoreType.DMA((max(1, n_src),)), pltpu.SemaphoreType.DMA((n_out,)),
            pltpu.SemaphoreType.DMA((max(1, n_terms),)),
            pltpu.SemaphoreType.DMA((max(1, len(sums)),)),
        ],
        compiler_params=pltpu.CompilerParams(vmem_limit_bytes=int(held) + VMEM_SPARE),
        cost_estimate=LIGHT,
    )(flags, *small, *sources, *terms, *deps))
    for chain, value in zip(sums, results[n_out:]):
        chain.forward(value)
    return results[:n_out]


def norm_rows(terms, gain, bias, x_ref, hat_ref, inv_ref, chunk=32):
    rows, width = x_ref.shape

    @pl.loop(0, rows // chunk, unroll=4)
    def _(i):
        at = pl.ds(pl.multiple_of(i * chunk, chunk), chunk)
        v = sum(term[at, :].astype(F32) for term in terms)
        centre = v - jnp.mean(v, axis=-1, keepdims=True)
        inv = lax.rsqrt(jnp.mean(centre * centre, axis=-1, keepdims=True) + EPS)
        hat = centre * inv
        x_ref[at, :] = (hat * gain[...] + bias[...]).astype(BF)
        if hat_ref is not None:
            hat_ref[at, :] = hat.astype(BF)
            inv_ref[at, :] = jnp.broadcast_to(inv, (chunk, 128))


def norm_back_rows(terms, hat_ref, inv_ref, gain, dv_ref, n_ref, chunk=32):
    rows, width = dv_ref.shape

    def step(i, sums):
        at = pl.ds(pl.multiple_of(i * chunk, chunk), chunk)
        dy = sum(term[at, :].astype(F32) for term in terms)
        hat = hat_ref[at, :].astype(F32)
        t = dy * gain[...]
        dv = (
            t
            - jnp.mean(t, axis=-1, keepdims=True)
            - hat * jnp.mean(t * hat, axis=-1, keepdims=True)
        ) * inv_ref[at, :1]
        dv_ref[at, :] = dv.astype(BF)
        return (
            sums[0] + (dy * hat).reshape(chunk // 8, 8, width).sum(0),
            sums[1] + dy.reshape(chunk // 8, 8, width).sum(0),
        )

    zero = jnp.zeros((8, width), F32)
    n_ref[0], n_ref[1] = lax.fori_loop(0, rows // chunk, step, (zero, zero), unroll=4)


def matmul_into(x_ref, w_ref, out_ref, at=0, tile=256):
    columns = w_ref.shape[1]
    tile = min(tile, columns)
    for c in range(0, columns, tile):
        out_ref[:, at + c : at + c + tile] = mm(x_ref[...], w_ref[:, c : c + tile]).astype(BF)


def matmul_bt_into(x_ref, w_ref, out_ref, at=0, tile=256):
    rows = w_ref.shape[0]
    tile = min(tile, rows)
    for c in range(0, rows, tile):
        out_ref[:, at + c : at + c + tile] = mm_bt(x_ref[...], w_ref[c : c + tile, :]).astype(BF)


def attend(heads, length, step, offsets, o_step, causal, q_ref, kv_ref, segq, segk, o_ref, lse_ref, bias_ref):
    q_off, k_off, v_off, o_off = offsets
    tile = min(256, length)
    if o_step != HD:
        o_ref[...] = jnp.zeros_like(o_ref)
    lse_ref[...] = jnp.zeros_like(lse_ref)
    for p in range(q_ref.shape[0] // length):
        base = p * length
        all_rows = slice(base, base + length)
        same = segq[all_rows, :] == segk[p : p + 1, :]
        if causal is not None:
            rows = lax.broadcasted_iota(jnp.int32, (length, length), 0)
            cols = lax.broadcasted_iota(jnp.int32, (length, length), 1)
            same = same & (cols * causal <= rows)
        bias_ref[...] = jnp.where(same, 0.0, MASKED)
        for h in range(heads):
            k = kv_ref[all_rows, h * step + k_off : h * step + k_off + HD]
            v = kv_ref[all_rows, h * step + v_off : h * step + v_off + HD]
            for r in range(0, length, tile):
                at = slice(base + r, base + r + tile)
                q = q_ref[at, h * step + q_off : h * step + q_off + HD] * jnp.asarray(HD**-0.5, BF)
                s = mm_bt(q, k) + bias_ref[r : r + tile, :]
                top = jnp.max(s, axis=-1, keepdims=True)
                e = jnp.exp(s - top)
                total = jnp.sum(e, axis=-1, keepdims=True)
                prob = (e * (1.0 / total)).astype(BF)
                o_ref[at, h * o_step + o_off : h * o_step + o_off + HD] = mm(prob, v).astype(BF)
                lse_ref[at, h : h + 1] = top + jnp.log(total)


def attend_back(
    heads, length, step, offsets, o_step, causal, q_ref, kv_ref, segq, segk, o_ref, lse_ref, do_ref,
    dq_ref, dkv_ref, bias_ref, inner_ref,
):
    q_off, k_off, v_off, o_off = offsets
    tile = min(256, length)
    if dq_ref is not dkv_ref:
        dq_ref[...] = jnp.zeros_like(dq_ref)
    for p in range(q_ref.shape[0] // length):
        base = p * length
        all_rows = slice(base, base + length)
        same = segk[all_rows, :] == segq[p : p + 1, :]
        if causal is not None:
            keys = lax.broadcasted_iota(jnp.int32, (length, length), 0)
            queries = lax.broadcasted_iota(jnp.int32, (length, length), 1)
            same = same & (keys * causal <= queries)
        bias_ref[...] = jnp.where(same, 0.0, MASKED)
        inner_ref[...] = jnp.zeros_like(inner_ref)
        for h in range(heads):
            cols = slice(h * o_step + o_off, h * o_step + o_off + HD)
            prod = do_ref[all_rows, cols].astype(F32) * o_ref[all_rows, cols].astype(F32)
            inner_ref[:, h : h + 1] = jnp.sum(prod, axis=-1, keepdims=True)
        inner_t = jnp.transpose(inner_ref[...])
        lse_t = jnp.transpose(lse_ref[all_rows, :])
        for h in range(heads):
            q_cols = slice(h * step + q_off, h * step + q_off + HD)
            k_cols = slice(h * step + k_off, h * step + k_off + HD)
            v_cols = slice(h * step + v_off, h * step + v_off + HD)
            q = q_ref[all_rows, q_cols] * jnp.asarray(HD**-0.5, BF)
            do = do_ref[all_rows, h * o_step + o_off : h * o_step + o_off + HD]
            dq = jnp.zeros((length, HD), F32)
            for r in range(0, length, tile):
                rows = slice(base + r, base + r + tile)
                k = kv_ref[rows, k_cols]
                v = kv_ref[rows, v_cols]
                s = mm_bt(k, q) + bias_ref[r : r + tile, :]
                prob = jnp.exp(s - lse_t[h : h + 1, :])
                dkv_ref[rows, v_cols] = mm(prob.astype(BF), do).astype(BF)
                ds = (prob * (mm_bt(v, do) - inner_t[h : h + 1, :])).astype(BF)
                dkv_ref[rows, k_cols] = mm(ds, q).astype(BF)
                dq = dq + mm_at(ds, k)
            dq_ref[all_rows, q_cols] = (dq * HD**-0.5).astype(BF)


SELF_AT = (0, HD, 2 * HD, 0)
CROSS_AT = (0, 0, HD, HD)


def self_forward(flags, src, seg, gain, bias, w_qkv, w_out, deps=()):
    packed, length = seg.shape
    rows, width = src.shape
    heads = 2 * w_out[0].shape[0] // HD
    part = w_qkv[0].shape[1]

    def body(flags, small, big, outs, extra, wait, flush):
        segq, segk, gain, bias = small
        src, qkv_a, qkv_b, out_a, out_b = big
        x, hat, inv, qkv, o, lse, partial = outs
        (mask,) = extra
        wait(0)

        @pl.when(flags[0] == 0)
        def _():
            norm_rows([src], gain, bias, x, hat, inv)

        @pl.when(flags[0] != 0)
        def _():
            x[...] = src[...]

        flush(0, 1, 2)
        wait(1)
        matmul_into(x, qkv_a, qkv)
        wait(2)
        matmul_into(x, qkv_b, qkv, part)
        flush(3)
        attend(heads, length, 3 * HD, SELF_AT, HD, flags[0], qkv, qkv, segq, segk, o, lse, mask)
        flush(4, 5)
        wait(3, 4)
        half = heads // 2 * HD
        for c in range(0, width, 256):
            partial[:, c : c + 256] = (
                mm(o[:, :half], out_a[:, c : c + 256]) + mm(o[:, half:], out_b[:, c : c + 256])
            ).astype(BF)
        flush(6)

    return sectioned(
        body, None, flags,
        (seg.reshape(rows, 1), seg, gain, bias),
        (src, *w_qkv, *w_out),
        (
            spec((rows, width)), Saved((rows, width)), Saved((rows, 128), F32),
            Saved((rows, 2 * part)), Saved((rows, heads * HD)), Saved((rows, 128), F32),
            spec((rows, width)),
        ),
        [pltpu.VMEM((length, length), F32)],
        2 * rows * width * heads * HD * 4 + 16 * heads * rows * length * HD,
        heads * rows * length, deps,
    )


def ffn_forward(core, flags, res, pair, gain, bias, w_up, w_down, deps=()):
    rows, width = res.shape
    part = w_up[0].shape[1]
    tile = min(512, part)

    def body(flags, small, big, outs, extra, wait, flush):
        gain, bias = small
        res, own, got, up_a, up_b, down_a, down_b = big
        x, hat, inv, hidden, slope, partial = outs
        (total,) = extra
        wait(0, 1, 2)
        norm_rows([res, own, got], gain, bias, x, hat, inv)
        flush(0, 1, 2)
        for i, (up, down) in enumerate(((up_a, down_a), (up_b, down_b))):
            wait(3 + i, 5 + i)
            for c in range(0, part, tile):
                at = slice(i * part + c, i * part + c + tile)
                u = mm(x[...], up[:, c : c + tile])
                phi = 0.5 * (1.0 + lax.erf(u * GELU_C))
                slope[:, at] = (phi + u * (PHI_C * jnp.exp(-0.5 * u * u))).astype(BF)
                hidden[:, at] = (u * phi).astype(BF)
                term = mm(hidden[:, at], down[c : c + tile, :])
                if i == 0 and c == 0:
                    total[...] = term
                else:
                    total[...] += term
        partial[...] = total[...].astype(BF)
        flush(3, 4, 5)

    return sectioned(
        body, core, flags, (gain, bias), (res, *pair, *w_up, *w_down),
        (
            spec((rows, width)), Saved((rows, width)), Saved((rows, 128), F32),
            Saved((rows, 2 * part)), Saved((rows, 2 * part)), spec((rows, width)),
        ),
        [pltpu.VMEM((rows, width), F32)],
        8 * rows * width * part, rows * part * 4, deps,
    )


def norm_project(core, flags, res, pair, gain, bias, w, deps=()):
    rows, width = res.shape
    part = w[0].shape[1]

    def body(flags, small, big, outs, extra, wait, flush):
        gain, bias = small
        res, own, got, w_a, w_b = big
        x, hat, inv, proj = outs
        wait(0, 1, 2)
        norm_rows([res, own, got], gain, bias, x, hat, inv)
        flush(0, 1, 2)
        wait(3)
        matmul_into(x, w_a, proj)
        wait(4)
        matmul_into(x, w_b, proj, part)
        flush(3)

    return sectioned(
        body, core, flags, (gain, bias), (res, *pair, *w),
        (spec((rows, width)), Saved((rows, width)), Saved((rows, 128), F32), spec((rows, 2 * part))),
        [], 4 * rows * width * part, 0, deps,
    )


def cross_forward(core, flags, q, kv, segq, segk, w, deps=()):
    packed, length = segq.shape
    rows = q.shape[0]
    width, part = w[0].shape
    heads = 2 * part // (2 * HD)

    def body(flags, small, big, outs, extra, wait, flush):
        segq, segk = small
        q, kv, w_a, w_b = big
        c, lse, partial = outs
        (mask,) = extra
        wait(0, 1)
        attend(heads, length, 2 * HD, CROSS_AT, 2 * HD, None, q, kv, segq, segk, c, lse, mask)
        flush(0, 1)
        wait(2, 3)
        for r in range(0, width, 256):
            partial[:, r : r + 256] = (
                mm_bt(c[:, :part], w_a[r : r + 256, :]) + mm_bt(c[:, part:], w_b[r : r + 256, :])
            ).astype(BF)
        flush(2)

    return sectioned(
        body, core, flags, (segq.reshape(rows, 1), segk), (q, kv, *w),
        (Saved((rows, 2 * part)), Saved((rows, 128), F32), spec((rows, width))),
        [pltpu.VMEM((length, length), F32)],
        4 * rows * width * part + 16 * heads * rows * length * HD, heads * rows * length, deps,
    )


def ffn_back_loop(df, slope, up, down, du, total, partial, wait, first):
    part = up[0].shape[1]
    tile = min(512, part)
    for i in range(2):
        wait(first + i, first + 2 + i)
        for c in range(0, part, tile):
            at = slice(i * part + c, i * part + c + tile)
            dh = mm_bt(df[...], down[i][c : c + tile, :])
            du[:, at] = (dh * slope[:, at].astype(F32)).astype(BF)
            term = mm_bt(du[:, at], up[i][:, c : c + tile])
            if i == 0 and c == 0:
                total[...] = term
            else:
                total[...] += term
    partial[...] = total[...].astype(BF)


def top_backward(core, flags, res, pair, cot, gain, bias, slope, w_up, w_down, deps=()):
    rows, width = res.shape
    part = w_up[0].shape[1]

    def body(flags, small, big, outs, extra, wait, flush):
        gain, bias = small
        res, own, got, cot, slope, up_a, up_b, down_a, down_b = big
        y, df, n, du, partial = outs
        total, hat, inv = extra
        wait(0, 1, 2)
        norm_rows([res, own, got], gain, bias, y, hat, inv)
        flush(0)
        wait(3)
        norm_back_rows([cot], hat, inv, gain, df, n)
        flush(1, 2)
        wait(4)
        ffn_back_loop(df, slope, (up_a, up_b), (down_a, down_b), du, total, partial, wait, 5)
        flush(3, 4)

    return sectioned(
        body, core, flags, (gain, bias), (res, *pair, in_hbm(cot), in_hbm(slope), *w_up, *w_down),
        (
            Saved((rows, width)), spec((rows, width)), Saved((2, 8, width), F32),
            Saved((rows, 2 * part)), spec((rows, width)),
        ),
        [pltpu.VMEM((rows, width), F32), pltpu.VMEM((rows, width), BF), pltpu.VMEM((rows, 128), F32)],
        8 * rows * width * part, 0, deps,
    )


def ffn_backward(core, flags, terms, kept, gain, slope, w_up, w_down, deps=()):
    rows, width = terms[0].shape
    part = w_up[0].shape[1]
    k = len(terms)

    def body(flags, small, big, outs, extra, wait, flush):
        (gain,) = small
        terms = big[:k]
        hat, inv, slope, up_a, up_b, down_a, down_b = big[k:]
        df, n, du, partial = outs
        (total,) = extra
        wait(*range(k + 2))
        norm_back_rows(terms, hat, inv, gain, df, n)
        flush(0, 1)
        wait(k + 2)
        ffn_back_loop(df, slope, (up_a, up_b), (down_a, down_b), du, total, partial, wait, k + 3)
        flush(2, 3)

    return sectioned(
        body, core, flags, (gain,), (*terms, *map(in_hbm, kept), in_hbm(slope), *w_up, *w_down),
        (
            spec((rows, width)), Saved((2, 8, width), F32), Saved((rows, 2 * part)),
            spec((rows, width)),
        ),
        [pltpu.VMEM((rows, width), F32)],
        8 * rows * width * part, 0, deps,
    )


def cross_backward(core, flags, terms, kept, gain, q, kv, segq, segk, c, lse, w, deps=()):
    packed, length = segq.shape
    rows, width = terms[0].shape
    part = w[0].shape[1]
    heads = 2 * part // (2 * HD)
    k = len(terms)

    def body(flags, small, big, outs, extra, wait, flush):
        segq, segk, gain = small
        terms = big[:k]
        hat, inv, w_a, w_b, q, kv, c, lse = big[k:]
        dca, n, dq, dkv, partial = outs
        dc, mask, inner = extra
        wait(*range(k + 2))
        norm_back_rows(terms, hat, inv, gain, dca, n)
        flush(0, 1)
        wait(k + 2, k + 3)
        matmul_into(dca, w_a, dc)
        matmul_into(dca, w_b, dc, part)
        wait(*range(k + 4, k + 8))
        attend_back(
            heads, length, 2 * HD, CROSS_AT, 2 * HD, None, q, kv, segq, segk, c, lse, dc, dq, dkv,
            mask, inner,
        )
        flush(2, 3)
        for r in range(0, width, 256):
            partial[:, r : r + 256] = (
                mm_bt(dq[:, :part], w_a[r : r + 256, :]) + mm_bt(dq[:, part:], w_b[r : r + 256, :])
            ).astype(BF)
        flush(4)

    return sectioned(
        body, core, flags, (segq, segk.reshape(rows, 1), gain),
        (*terms, *map(in_hbm, kept), *w, *map(in_hbm, (q, kv, c, lse))),
        (
            spec((rows, width)), Saved((2, 8, width), F32), Saved((rows, 2 * part)),
            spec((rows, 2 * part)), spec((rows, width)),
        ),
        [
            pltpu.VMEM((rows, 2 * part), BF), pltpu.VMEM((length, length), F32),
            pltpu.VMEM((length, 128), F32),
        ],
        8 * rows * width * part + 40 * heads * rows * length * HD, heads * rows * length, deps,
    )


def memory_backward(core, flags, dkv, w, deps=()):
    rows = dkv.shape[0]
    width, part = w[0].shape

    def body(flags, small, big, outs, extra, wait, flush):
        dkv, w_a, w_b = big
        (partial,) = outs
        wait(0, 1, 2)
        for r in range(0, width, 256):
            partial[:, r : r + 256] = (
                mm_bt(dkv[:, :part], w_a[r : r + 256, :]) + mm_bt(dkv[:, part:], w_b[r : r + 256, :])
            ).astype(BF)
        flush(0)

    return sectioned(
        body, core, flags, (), (dkv, *w), (spec((rows, width)),), [], 4 * rows * width * part, 0, deps
    )[0]


def self_backward(
    core, flags, terms, kept, gain, qkv, o, lse, seg, w_qkv, w_out, deps=(), sums=()
):
    packed, length = seg.shape
    rows, width = terms[0].shape
    heads = 2 * w_out[0].shape[0] // HD
    part = w_qkv[0].shape[1]
    k = len(terms)

    def body(flags, small, big, outs, extra, wait, flush):
        segq, segk, gain = small
        terms = big[:k]
        hat, inv, out_a, out_b, qkv, o, lse, qkv_a, qkv_b = big[k:]
        ds, n, dqkv, partial = outs
        do, mask, inner = extra
        wait(*range(k + 2))
        norm_back_rows(terms, hat, inv, gain, ds, n)
        flush(0, 1)
        wait(k + 2, k + 3)
        half = heads // 2 * HD
        matmul_bt_into(ds, out_a, do)
        matmul_bt_into(ds, out_b, do, half)
        wait(*range(k + 4, k + 7))
        attend_back(
            heads, length, 3 * HD, SELF_AT, HD, flags[0], qkv, qkv, segq, segk, o, lse, do, dqkv,
            dqkv, mask, inner,
        )
        flush(2)
        wait(k + 7, k + 8)
        for r in range(0, width, 256):
            partial[:, r : r + 256] = (
                mm_bt(dqkv[:, :part], qkv_a[r : r + 256, :])
                + mm_bt(dqkv[:, part:], qkv_b[r : r + 256, :])
            ).astype(BF)
        flush(3)

    return sectioned(
        body, core, flags, (seg, seg.reshape(rows, 1), gain),
        (*terms, *map(in_hbm, kept), *w_out, *map(in_hbm, (qkv, o, lse)), *w_qkv),
        (
            spec((rows, width)), Saved((2, 8, width), F32), Saved((rows, 2 * part)),
            spec((rows, width)),
        ),
        [
            pltpu.VMEM((rows, heads * HD), BF), pltpu.VMEM((length, length), F32),
            pltpu.VMEM((length, 128), F32),
        ],
        2 * rows * width * heads * HD * 4 + 40 * heads * rows * length * HD,
        heads * rows * length, deps, sums=sums,
    )


def weight_grads(flags, groups, deps=(), cuts=1, sums=()):
    lists = [
        in_hbm(array) for own in groups for lefts, rights, _ in own for array in (*lefts, *rights)
    ]
    live = [core for core in range(2) if groups[core]]
    some = groups[live[0]]
    height = some[0][0][0].shape[1] // (2 if some[0][2] else 1)
    widths = [
        [rights[0].shape[1] // (1 if split_left else 2) for _, rights, split_left in own]
        for own in groups
    ]
    piece = height // cuts
    counts = [sum(2 * len(lefts) for lefts, _, _ in own) for own in groups]

    def body(flags, small, big, outs, extra, wait, flush):
        def run(core):
            for i in reversed(range(2)):
                first, at = counts[0] * core, 0
                for g, (lefts, rights, split_left) in enumerate(groups[core]):
                    k = len(lefts)
                    if i == 1:
                        wait(*range(first, first + 2 * k))
                    i_m = i * height if split_left else 0
                    n = widths[core][g]
                    i_n = 0 if split_left else i * n
                    tile = min(256, piece)
                    for r in range(0, height, tile):
                        low = r % piece
                        outs[i * cuts + r // piece][low : low + tile, at : at + n] = sum(
                            mm_at(
                                big[first + j][:, i_m + r : i_m + r + tile],
                                big[first + k + j][:, i_n : i_n + n],
                            )
                            for j in range(k)
                        ).astype(BF)
                    first += 2 * k
                    at += n
                flush(*range(i * cuts, (i + 1) * cuts))

        if len(live) == 1:
            run(live[0])
        else:
            for core in live:
                pl.when(flags[0] == core)(lambda core=core: run(core))

    blocks = tuple(spec((piece, sum(widths[live[0]]))) for _ in range(2 * cuts))
    owners = [0] * counts[0] + [1] * counts[1]
    return sectioned(
        body, live[0] if len(live) == 1 else None, flags, (), lists, blocks, [], 0, 0, deps, owners,
        sums,
    )


def after(array, *deps):
    deps = in_order(deps)
    return note(pl.pallas_call(
        lambda *refs: None,
        out_shape=spec(array.shape, array.dtype),
        in_specs=[pl.BlockSpec(memory_space=pl.ANY)] * (1 + len(deps)),
        out_specs=pl.BlockSpec(memory_space=pl.ANY),
        input_output_aliases={0: 0},
        cost_estimate=LIGHT,
    )(array, *deps))


def pack_rows(flags, weights, deps=(), whole=False):
    deps = in_order(deps)
    halves = [w.shape[0] // (1 if whole else 2) for w in weights]
    out = spec((sum(halves), weights[0].shape[1]))

    def kernel(flags_ref, *refs):
        target, sem = refs[-2:]
        copies, at = [], 0
        for i, half in enumerate(halves):
            first = 0 if whole else pl.multiple_of(flags_ref[1] * half, half)
            copies.append(
                pltpu.make_async_copy(
                    refs[i].at[pl.ds(first, half), :], target.at[pl.ds(at, half), :], sem.at[i]
                )
            )
            at += half
        for copy in copies:
            copy.start()
        for copy in copies:
            copy.wait()

    return note(pl.pallas_call(
        kernel,
        out_shape=out,
        in_specs=[pl.BlockSpec(memory_space=pltpu.SMEM)]
        + [pl.BlockSpec(memory_space=pl.ANY)] * (len(weights) + len(deps)),
        out_specs=pl.BlockSpec(memory_space=pltpu.VMEM),
        scratch_shapes=[pltpu.SemaphoreType.DMA((len(weights),))],
        cost_estimate=LIGHT,
    )(flags, *weights, *deps))


def add_pairs(flags, pairs, deps=()):
    deps = in_order(deps)
    k = len(pairs)
    cuts = [4 if a.shape[0] % 64 == 0 else 1 for _, a, _ in pairs]

    def kernel(flags_ref, *refs):
        terms = refs[: 2 * k]
        outs = refs[2 * k + len(deps) : 3 * k + len(deps)]
        held = refs[3 * k + len(deps) : -2]
        in_sem, out_sem = refs[-2:]
        jobs = []
        for p, (core, a, _) in enumerate(pairs):
            live = flags_ref[0] >= 0 if core is None else flags_ref[0] == core
            chunk = a.shape[0] // cuts[p]
            for i in range(cuts[p]):
                at = pl.ds(i * chunk, chunk)
                loads = [
                    pltpu.make_async_copy(
                        terms[2 * p + j].at[at, :], held[2 * p + j].at[at, :], in_sem.at[2 * p + j, i]
                    )
                    for j in range(2)
                ]
                store = pltpu.make_async_copy(held[2 * p].at[at, :], outs[p].at[at, :], out_sem.at[p, i])
                jobs.append((live, at, held[2 * p], held[2 * p + 1], loads, store))
        for live, _, _, _, loads, _ in jobs:

            @pl.when(live)
            def _():
                for load in loads:
                    load.start()

        for live, at, a_ref, b_ref, loads, store in jobs:

            @pl.when(live)
            def _():
                for load in loads:
                    load.wait()
                a_ref[at, :] = (a_ref[at, :].astype(F32) + b_ref[at, :].astype(F32)).astype(BF)
                store.start()

        for live, _, _, _, _, store in jobs:
            pl.when(live)(store.wait)

    arrays = [array for _, a, b in pairs for array in (a, b)]
    return note(pl.pallas_call(
        kernel,
        out_shape=tuple(spec(a.shape) for _, a, _ in pairs),
        in_specs=[pl.BlockSpec(memory_space=pltpu.SMEM)]
        + [pl.BlockSpec(memory_space=pl.ANY)] * (2 * k + len(deps)),
        out_specs=tuple([pl.BlockSpec(memory_space=pl.ANY)] * k),
        scratch_shapes=[pltpu.VMEM(array.shape, BF) for array in arrays]
        + [pltpu.SemaphoreType.DMA((2 * k, 4)), pltpu.SemaphoreType.DMA((k, 4))],
        compiler_params=pltpu.CompilerParams(
            vmem_limit_bytes=sum(2 * array.size for array in arrays) + VMEM_SPARE
        ),
        cost_estimate=LIGHT,
    )(flags, *arrays, *deps))


def finish(flags, kept, got, columns, deps=()):
    deps = in_order(deps)
    sources = [kept[0], kept[1], got[0], got[1]]
    rows = sum(piece.shape[0] for piece in sources[0][0])
    cuts = 4 if rows % 64 == 0 else max(len(pieces) for pieces, _ in sources)
    chunk = rows // cuts
    flat = [piece for pieces, _ in sources for piece in pieces]

    def kernel(flags_ref, *refs):
        out_hbm, low_ref, out_ref, in_sem, out_sem = refs[len(flat) + len(deps) :]
        loads, stores = [], []
        for i in range(cuts):
            at = pl.ds(i * chunk, chunk)
            first_ref = 0
            for c, (pieces, first) in enumerate(sources):
                size = rows // len(pieces)
                load = pltpu.make_async_copy(
                    refs[first_ref + i * chunk // size].at[
                        pl.ds(i * chunk % size, chunk), pl.ds(first, columns)
                    ],
                    low_ref.at[at, :],
                    in_sem.at[i],
                )
                pl.when(flags_ref[0] + 2 * flags_ref[2] == c)(load.start)
                first_ref += len(pieces)
            loads.append(load)
            stores.append(pltpu.make_async_copy(out_ref.at[at, :], out_hbm.at[at, :], out_sem.at[i]))
        for i in range(cuts):
            at = pl.ds(i * chunk, chunk)
            loads[i].wait()
            out_ref[at, :] = low_ref[at, :].astype(F32)
            stores[i].start()
        for store in stores:
            store.wait()

    out = spec((rows, columns), F32)
    return note(pl.pallas_call(
        kernel,
        out_shape=out,
        in_specs=[pl.BlockSpec(memory_space=pltpu.SMEM)]
        + [pl.BlockSpec(memory_space=pl.ANY)] * (len(flat) + len(deps)),
        out_specs=pl.BlockSpec(memory_space=pl.ANY),
        scratch_shapes=[
            pltpu.VMEM(out.shape, BF), pltpu.VMEM(out.shape, F32),
            pltpu.SemaphoreType.DMA((cuts,)), pltpu.SemaphoreType.DMA((cuts,)),
        ],
        compiler_params=pltpu.CompilerParams(vmem_limit_bytes=6 * rows * columns + VMEM_SPARE),
        cost_estimate=LIGHT,
    )(flags, *flat, *deps))


def norm_back(dy, kept, gain):
    hat, inv = kept
    t = dy * gain
    dv = (
        t
        - jnp.mean(t, axis=-1, keepdims=True)
        - hat * jnp.mean(t * hat, axis=-1, keepdims=True)
    ) * inv
    return dv, jnp.stack([jnp.sum(dy * hat, axis=0), jnp.sum(dy, axis=0)])


def on_device(
    layer_in, segments, cotangent, self_qkv, self_out, cross_proj, ffn_up, ffn_down,
    norm_gain, norm_bias,
):
    ORDER.clear()
    STRICT[-1] = True
    sec = lax.axis_index("section")
    n = lax.axis_size("tensor")
    zs = lax.axis_size("dp")
    z = lax.axis_index("dp")
    t = lax.axis_index("tensor")
    tp = n // 2
    bits = tp.bit_length() - 1
    x = t % tp
    fs = t // tp
    micro, share, width = layer_in.shape[1:]
    packed, length = segments.shape[2:]
    rows = packed * length
    assert micro == 4 and zs == 4
    is0 = sec == 0
    gain, bias = norm_gain[0], norm_bias[0]

    def to_core(v, core):
        return lax.ppermute(v, "section", [(1 - core, core)])

    def flip(v, bit, core=None):
        if core is None:
            return lax.ppermute(v, "tensor", [(i, i ^ (1 << bit)) for i in range(n)])
        return lax.ppermute(
            v,
            ("section", "tensor"),
            [(core * n + i, core * n + (i ^ (1 << bit))) for i in range(n)],
        )

    def z_on(v, core, pairs):
        if core is None:
            return lax.ppermute(v, "dp", pairs)
        if core is None:
            return lax.ppermute(v, "dp", pairs)
        if core is None:
            return lax.ppermute(v, "dp", pairs)
        return lax.ppermute(v, ("section", "dp"), [(core * zs + a, core * zs + b) for a, b in pairs])

    def tp_sum(v, core=None):
        for bit in range(bits):
            got = flip(v, bit, core)
            if bit < bits - 1:
                v = (v.astype(F32) + got.astype(F32)).astype(BF)
        return v, got

    def tp_scatter(v, core):
        cur = v.reshape(2, tp, share, width)
        for bit in reversed(range(bits)):
            half = 1 << bit
            bit_on = (x >> bit) & 1
            parts = cur.reshape(2, 2, half, share, width)
            give = lax.dynamic_index_in_dim(parts, 1 - bit_on, 1, keepdims=False)
            keep = lax.dynamic_index_in_dim(parts, bit_on, 1, keepdims=False)
            total = keep.astype(F32) + flip(give, bit, core).astype(F32)
            cur = total.astype(BF)
        return total.reshape(2 * share, width)

    def own_rows(v):
        return lax.dynamic_index_in_dim(
            v.reshape(2, tp, share, v.shape[-1]), x, 1, keepdims=False
        ).reshape(2 * share, v.shape[-1])

    def ordered(is_first, own, other, axis=0):
        first = jnp.where(is_first, own, other)
        second = jnp.where(is_first, other, own)
        return jnp.stack([first, second], axis=axis)

    def gather_micro(keep, got, core=None):
        count = keep.shape[0]
        cur = ordered(fs == 0, keep, got, axis=1)[:, :, None]
        for bit in range(bits):
            got = flip(cur, bit, core)
            cur = ordered((x >> bit) & 1 == 0, cur, got, axis=2).reshape(
                count, 2, 2 << bit, share, width
            )
        return cur.reshape(count, rows, width)

    def scatter_micro(streams):
        blocks = jnp.stack([v.reshape(2, share, width) for v in streams], axis=1)
        keep = lax.dynamic_index_in_dim(blocks, fs, 0, keepdims=False)
        give = lax.dynamic_index_in_dim(blocks, 1 - fs, 0, keepdims=False)
        return ordered(fs == 0, keep, flip(give, bits)).reshape(1, micro, share, width)

    class Reduction:
        def __init__(self, core, own, near):
            self.core, self.value, self.step = core, own, 0
            self.got = None if near is None else flip(near, bits, core)

        def forward(self, value):
            self.value = value
            inward, middle, outward = ((0, 1), (3, 2)), ((1, 2), (2, 1)), ((1, 0), (2, 3))
            self.got = z_on(self.value, self.core, (inward, middle, outward)[self.step])
            self.step += 1
            return self.value

    def z_sum(g, core):
        half = zs // 2
        for k in range(half - 1):
            got = z_on(g, core, [(k, k + 1), (zs - 1 - k, zs - 2 - k)])
            g = (g.astype(F32) + got.astype(F32)).astype(g.dtype)
        got = z_on(g, core, [(half - 1, half), (half, half - 1)])
        g = (g.astype(F32) + got.astype(F32)).astype(g.dtype)
        for k in reversed(range(half - 1)):
            got = z_on(g, core, [(k + 1, k), (zs - 2 - k, zs - 1 - k)])
            g = jnp.where((z == k) | (z == zs - 1 - k), got, g)
        return g

    streams = range(2)
    by_slot = layer_in[0].reshape(2, 2, share, width)
    src_keep = lax.dynamic_index_in_dim(by_slot, fs, 0, keepdims=False)
    src_give = lax.dynamic_index_in_dim(by_slot, 1 - fs, 0, keepdims=False)
    src_got = flip(src_give, bits)
    src = [gather_micro(src_keep[j : j + 1], src_got[j : j + 1])[0] for j in streams]
    segs = lax.dynamic_index_in_dim(
        segments.reshape(2, 2, 2, packed, length), fs, 1, keepdims=False
    )
    seg_e = [segs[0, j] for j in streams]
    seg_d = [segs[1, j] for j in streams]
    seg_own = [jnp.where(is0, e, d) for e, d in zip(seg_e, seg_d)]
    outer = (z == 0) | (z == zs - 1)
    flags = jnp.stack([sec, z % 2, outer]).astype(jnp.int32)

    def fetch(weights, core=None, deps=()):
        if len({w.shape[1] for w in weights}) > 1:
            return [fetch([w], core, deps)[0] for w in weights]
        p = flip(pack_rows(flags, weights, deps), bits, core)
        q = z_on(p, core, [(i, i ^ 1) for i in range(zs)])
        pairs, at = [], 0
        for w in weights:
            pairs.append((w, Near(w.shape, p, q, at)))
            at += w.shape[0] // 2
        return pairs

    STRICT[-1] = False
    (w_qkv,) = fetch([self_qkv[0]])
    (w_out,) = fetch([self_out[0]])
    early = [fetch([w[0]], 0, [src_got])[0] for w in (ffn_up, ffn_down)]
    (w_cross,) = fetch([cross_proj[0]], None, [src[1]])
    late = fetch([ffn_up[0], ffn_down[0]], 1, [src[1]])

    def row(v, i):
        return v[i : i + 1]

    def ln(i):
        return row(gain, i), row(bias, i)

    STRICT[-1] = True
    start, kept_in, sa, keep_s = ([None] * 2 for _ in range(4))
    for j in streams:
        start[j], *kept_in[j], qkv, o, lse, part = self_forward(
            flags, src[j], seg_own[j], *ln(1), w_qkv, w_out
        )
        keep_s[j] = (qkv, o, lse)
        sa[j] = tp_sum(part)
    mid, kept_e1, keep_fe, ff = ([None] * 2 for _ in range(4))
    for j in streams:
        mid[j], *kept_e1[j], hidden, slope, part = ffn_forward(
            0, flags, start[j], sa[j], *ln(0), *early
        )
        keep_fe[j] = (hidden, slope)
        ff[j] = tp_sum(part, 0)
    memory, kept_mem, kv, d1, kept_d1, q, ca, keep_c = ([None] * 2 for _ in range(8))
    for j in streams:
        d1[j], *kept_d1[j], q[j] = norm_project(1, flags, start[j], sa[j], *ln(0), w_cross)
        memory[j], *kept_mem[j], kv[j] = norm_project(0, flags, mid[j], ff[j], *ln(2), w_cross)
        kv[j] = to_core(kv[j], 1)
    cot_by_slot = cotangent.reshape(2, 2, share, width)
    cot_keep = lax.dynamic_index_in_dim(cot_by_slot, fs, 0, keepdims=False)
    cot_give = lax.dynamic_index_in_dim(cot_by_slot, 1 - fs, 0, keepdims=False)
    for j in streams:
        *keep_c[j], part = cross_forward(1, flags, q[j], kv[j], seg_d[j], seg_e[j], w_cross)
        ca[j] = tp_sum(part, 1)
    cot = gather_micro(cot_keep, flip(after(cot_give, keep_c[0][0]), bits, 1), 1)
    d2, kept_d2, keep_fd = ([None] * 2 for _ in range(3))
    for j in streams:
        d2[j], *kept_d2[j], hidden, slope, part = ffn_forward(
            1, flags, d1[j], ca[j], *ln(1), *late
        )
        keep_fd[j] = (hidden, slope)
        ff[j] = tp_sum(part, 1)

    STRICT[-1] = False
    def pick(items, i):
        return [item[i] for item in items]

    def height(group):
        return group[0][0].shape[1] // (2 if group[2] else 1)

    def reduced(enc, dec, cuts=1, sums=()):
        heights = {height(g) for g in (*enc, *dec)}
        widths = {sum(g[1][0].shape[1] // (1 if g[2] else 2) for g in own) for own in (enc, dec) if own}
        if len(heights) > 1 or len(widths) > 1:
            advance((sums, 0))
            return [reduced([g], [], cuts)[0] for g in enc] + [
                reduced([], [g], cuts)[0] for g in dec
            ]
        core = None if enc and dec else 0 if enc else 1
        blocks = weight_grads(flags, (enc, dec), (), cuts, sums)
        chains = [Reduction(core, *pair) for pair in zip(blocks[:cuts], blocks[cuts:])]
        places = []
        for own in (enc, dec):
            at = 0
            for lefts, rights, split_left in own:
                places.append((chains, at))
                at += rights[0].shape[1] // (1 if split_left else 2)
        return places

    def chains_of(places):
        return list({id(chain): chain for place in places for chain in place[0]}.values())

    def advance(*places, deps=()):
        chains = [chain for chain in chains_of(places) if chain.step < 3]
        if chains:
            pairs = [(chain.core, chain.value, chain.got) for chain in chains]
            for chain, value in zip(chains, add_pairs(flags, pairs, deps)):
                chain.forward(value)
        return chains

    def arrived(*places):
        return [chain.got for chain in chains_of(places)]

    def soon(pair):
        return (pair[0], after(pair[1]))

    decoded, df, du, back, n_out, n_d2, n_d1, n_mem, n_e1, n_in = ([None] * 2 for _ in range(10))
    for j in streams:
        decoded[j], df[j], n_out[j], du[j], part = top_backward(
            1, flags, d2[j], ff[j], cot[j], *ln(2), keep_fd[j][1], *late
        )
        back[j] = tp_sum(part, 1)

    dca, dq, dkv, dmem, ds, dqkv, grad_d, grad_e, dfe, due, backe = ([None] * 2 for _ in range(11))
    es, eqkv = ([None] * 2 for _ in range(2))

    def cross_step(j):
        dca[j], n_d2[j], dq[j], grad, part = cross_backward(
            1, flags, (df[j], *back[j]), kept_d2[j], row(gain, 1), q[j], kv[j], seg_d[j], seg_e[j],
            *keep_c[j], w_cross,
        )
        dkv[j] = to_core(grad, 0)
        dmem[j] = tp_sum(memory_backward(0, flags, dkv[j], w_cross), 0)
        back[j] = tp_sum(part, 1)

    def ffn_step(j):
        dfe[j], n_mem[j], due[j], part = ffn_backward(
            0, flags, dmem[j], kept_mem[j], row(gain, 2), keep_fe[j][1], *early,
        )
        backe[j] = tp_sum(part, 0)

    def dec_step(j, sums):
        ds[j], n_d1[j], dqkv[j], part = self_backward(
            1, flags, (dca[j], *back[j]), kept_d1[j], row(gain, 0), *keep_s[j], seg_own[j], w_qkv,
            w_out, sums=sums,
        )
        grad_d[j] = own_rows(ds[j]).astype(F32) + tp_scatter(part, 1)

    def enc_step(j):
        es[j], n_e1[j], eqkv[j], part = self_backward(
            0, flags, (dfe[j], *backe[j]), kept_e1[j], row(gain, 0), *keep_s[j], seg_own[j], w_qkv,
            w_out,
        )
        dy = own_rows(es[j]).astype(F32) + tp_scatter(part, 0)
        hat = own_rows(kept_in[j][0]).astype(F32)
        dv, n_in[j] = norm_back(dy, (hat, own_rows(kept_in[j][1])[:, :1]), gain[1])
        grad_e[j] = dv.astype(BF)

    cross_step(0)
    cross_step(1)
    (gd_down,) = reduced([], [(pick(keep_fd, 0), df, True)])
    ffn_step(0)
    (gd_up,) = reduced([], [(d2, du, False)])
    ffn_step(1)
    dec_step(0, [])
    enc_step(0)
    dec_step(1, gd_down[0])
    ge_cross, ge_down, gd_cross, gd_qkv, gd_out = reduced(
        [(memory, dkv, False), (pick(keep_fe, 0), dfe, True)],
        [
            ((*d1, *dca), (*dq, *pick(keep_c, 0)), False),
            (start, dqkv, False),
            (ds, pick(keep_s, 1), False),
        ],
        2,
    )
    STRICT[-1] = True
    enc_step(1)
    advance(gd_up, gd_down)
    ge_up, ge_qkv, ge_out = reduced(
        [(mid, due, False), (start, eqkv, False), (es, pick(keep_s, 1), False)], [], 2
    )
    layer_out = scatter_micro([own_rows(jnp.where(is0, m, d)) for m, d in zip(memory, decoded)])

    def part(place, i):
        return ([place[0][i % len(place[0])]], 0)

    p1a, p1b = part(ge_cross, 0), part(ge_cross, 1)
    p2a, p2b = part(ge_up, 0), part(ge_up, 1)
    advance(p1a, gd_down, gd_up, deps=[layer_out])

    once = 1.0 / tp
    norms = jnp.where(
        is0,
        jnp.stack([sum(n_e1).sum(1) * once, sum(n_in), sum(n_mem).sum(1) * once], axis=1),
        jnp.stack([sum(n_d1), sum(n_d2), sum(n_out)], axis=1).sum(2) * once,
    )

    def total(enc, dec, columns, turned=False):
        kept, got = (
            [([getattr(chain, name) for chain in chains], at) for chains, at in (enc, dec)]
            for name in ("value", "got")
        )
        if columns % 128 == 0 and enc[1] % 128 == 0 and dec[1] % 128 == 0 and not turned:
            return finish(flags, kept, got, columns)[None]
        kept, got = (
            jnp.where(is0, *(jnp.concatenate(rows)[:, at : at + columns] for rows, at in pair))
            for pair in (kept, got)
        )
        kept = jnp.where(outer, got, kept)
        return (jnp.transpose(kept) if turned else kept).astype(F32)[None]

    def norms_step(norms, bit):
        bit_on = (t >> bit) & 1
        parts = norms.reshape(2, 3, 2, -1)
        return lax.dynamic_index_in_dim(parts, bit_on, 2, keepdims=False) + flip(
            lax.dynamic_index_in_dim(parts, 1 - bit_on, 2, keepdims=False), bit
        )

    for bit in reversed(range(bits + 1)):
        norms = norms_step(norms, bit)
    input_grad = scatter_micro([jnp.where(is0, e, d.astype(BF)) for e, d in zip(grad_e, grad_d)])
    norms_sum = Reduction(None, norms, None)
    advance(p1b, gd_up, p1a, deps=[*arrived(gd_down), input_grad, norms])
    norms_sum.forward(norms)
    advance(p2a, p1b, p1a, deps=[*arrived(gd_up), norms_sum.got])
    norms_sum.forward(norms_sum.value + norms_sum.got)
    advance(p2b, p2a, p1b, deps=[*arrived(p1a), norms_sum.got])
    norms_sum.forward(norms_sum.value + norms_sum.got)
    advance(p2b, p2a, deps=[*arrived(p1b), norms_sum.got])
    advance(p2b, deps=arrived(p2a))
    everything = (
        ge_cross, ge_down, gd_cross, gd_qkv, gd_out, ge_up, ge_qkv, ge_out, gd_down, gd_up
    )
    while advance(*everything):
        pass
    g_cross = total(ge_cross, gd_cross, cross_proj.shape[2])
    g_down = total(ge_down, gd_down, width)
    norms = jnp.where(outer, norms_sum.got, norms_sum.value)
    totals = (
        total(ge_qkv, gd_qkv, self_qkv.shape[2]),
        total(ge_out, gd_out, self_out.shape[1], True),
        g_cross, total(ge_up, gd_up, ffn_up.shape[2]), g_down,
    )
    return (layer_out, input_grad, *totals, norms[0][None], norms[1][None])


def solution(mesh):
    return jax.shard_map(
        on_device,
        mesh=mesh,
        in_specs=(
            P("section", None, ("dp", "tensor"), None),
            P(None, None, "dp", None),
            P(None, ("dp", "tensor"), None),
            P("section", None, "tensor"),
            P("section", "tensor", None),
            P("section", None, "tensor"),
            P("section", None, "tensor"),
            P("section", "tensor", None),
            P("section", None, None),
            P("section", None, None),
        ),
        out_specs=(
            P("section", None, ("dp", "tensor"), None),
            P("section", None, ("dp", "tensor"), None),
            P("section", None, "tensor"),
            P("section", "tensor", None),
            P("section", None, "tensor"),
            P("section", None, "tensor"),
            P("section", "tensor", None),
            P("section", None, "tensor"),
            P("section", None, "tensor"),
        ),
        check_vma=False,
    )
```

time: 2370 us -> 727 us (0.31)
  waiting for transfers between devices: 1700 us -> 281 us
  matrix products: 351 us -> 0 us
  Pallas kernels: 0 us -> 218 us
  other arithmetic: 155 us -> 21.5 us
  starting transfers between devices: 23.4 us -> 134 us
  local copies, waits for them, and re-layouts: 102 us -> 55.3 us
    reduce_scatter x30 -> x0, waiting for transfers between devices: 745 us -> none  [the longest x15 413 us: sum_rows(): lax.psum_scatter(partial_term(jnp.int32(0), share_rows * lax.axis_size('t...]
    all_gather x30 -> x0, waiting for transfers between devices: 650 us -> none  [the longest x15 363 us: gather_rows(): return lax.all_gather(rows_low, 'tensor', axis=0, tiled=True)]
    dot_general x150 -> x0, matrix products: 351 us -> none  [the longest x30 92.7 us: rows_product(): lax.dot_general(left, right, (((0,), (0,)), ((), ())), preferred_element_...]
    ppermute x10 -> x72, waiting for transfers between devices: 13.5 us -> 281 us  [the longest x4 98.1 us: to_core(): return lax.ppermute(v, 'section', [(1 - core, core)])]
    psum x1 -> x0, waiting for transfers between devices: 247 us -> none  [on_device(): lax.psum(grad_qkv.astype(jnp.bfloat16), 'dp').astype(jnp.float32)]
    pallas_call x0 -> x46, Pallas kernels: none -> 218 us  [the longest x28 162 us: sectioned(): pl.pallas_call(kernel, out_shape=tuple((pltpu.HBM(a.shape, a.dtype) if is...]
    ppermute x10 -> x72, starting transfers between devices: 17.5 us -> 134 us  [the longest x27 58.4 us: flip(): lax.ppermute(v, ('section', 'tensor'), [(core * n + i, core * n + (i ^ 1...]
    reduce_sum x52 -> x4, other arithmetic: 70.1 us -> 3.58 us  [the longest x1 3.45 us: norm_back(): return (dv, jnp.stack([jnp.sum(dy * hat, axis=0), jnp.sum(dy, axis=0)]))]
  transfers between devices with their start and end apart: 73 -> 72, of which waited for: 68 -> 17; matrix products, arithmetic and copies ran while one was open for 12% -> 4% of each run, Pallas kernels for 0% -> 28%
where the time goes in v1:
time: 727 us; the launch traced here: 714 us
  waiting for transfers between devices  281 us (39%)
  Pallas kernels  218 us (30%)
  starting transfers between devices  134 us (18%)
  local copies, waits for them, and re-layouts  55.3 us (8%)
  other arithmetic  21.5 us (3%)
    pallas_call x28, Pallas kernels, sectioned(): pl.pallas_call(kernel, out_shape=tuple((pltpu.HBM(a.shape, a.dtype) if is...  162 us
    ppermute x4, waiting for transfers between devices, to_core(): return lax.ppermute(v, 'section', [(1 - core, core)])  98.1 us
    ppermute x12, waiting for transfers between devices, z_on(): return lax.ppermute(v, 'dp', pairs)  90.4 us
    ppermute x27, starting transfers between devices, flip(): lax.ppermute(v, ('section', 'tensor'), [(core * n + i, core * n + (i ^ 1...  58.4 us
    ppermute x15, waiting for transfers between devices, z_on(): lax.ppermute(v, ('section', 'dp'), [(core * zs + a, core * zs + b) for a,...  51.1 us
    unnamed x346, local copies, waits for them, and re-layouts  45.4 us
    ppermute x14, waiting for transfers between devices, flip(): return lax.ppermute(v, 'tensor', [(i, i ^ 1 << bit) for i in range(n)])  31.5 us
    ppermute x15, starting transfers between devices, z_on(): lax.ppermute(v, ('section', 'dp'), [(core * zs + a, core * zs + b) for a,...  31.1 us
  transfers between devices with their start and end apart: 72, of which 17 were waited for; matrix products, arithmetic and copies ran while one was open for 4% of the time, Pallas kernels for 28%

profile of v1, /device:TPU:0, one launch (start us, length us, event | category | flops | bytes accessed | tf_op | source)
XLA Modules:
  0.0 713.7 jit_solution(4229326875914636865)
XLA Ops:
  1.8 3.0 collective-permute-start
  5.5 2.8 shard_map.169
  14.3 3.3 collective-permute-done.refs_1_
  22.8 2.9 shard_map.173
  25.7 4.1 collective-permute-start.8
  29.8 2.9 shard_map.174
  32.6 6.6 collective-permute-done.4.refs_9_
  39.2 3.6 collective-permute-start.10
  49.5 3.7 shard_map.171.refs_11_
  53.4 12.0 %collective-permute-done.3.refs_7_.refs_16_ = bf16[512,768]{1,0:T(8,128)(2,1)S(1)} collective-permute-done((bf16[512,768]{1,0:T(8,128)(2,1)S(1)}, bf16[512,768]{1,0:T(8,128)(2,1)S(1)}, u32[]{:S(2)}, u32[]{:S(2)}) %collective-permute-start.3) | collective-permute-done | bytes 786464 | tf_op jit(solution)/shard_map/ppermute | solution.py:933
  65.5 13.5 %shard_map.172 = (bf16[512,1024]{1,0:T(8,128)(2,1)S(1)}, bf16[512,1024]{1,0:T(8,128)(2,1)}, f32[512,128]{1,0:T(8,128)}, bf16[512,1536]{1,0:T(8,128)(2,1)}, bf16[...) custom-call(s32[3]{0:T(128)S(1)} %copy-done.117, s32[512,1]{1,0:T(8,128)S(1)} %copy-done.80, ...), custom_call_target="tpu_custom_call" | custom-call | flops 1024 | bytes 1024 | tf_op jit(solution)/shard_map/pallas_call | solution.py:183
  80.5 3.5 collective-permute-start.9
  86.5 13.7 %shard_map.175 = (bf16[512,1024]{1,0:T(8,128)(2,1)S(1)}, bf16[512,1024]{1,0:T(8,128)(2,1)}, f32[512,128]{1,0:T(8,128)}, bf16[512,1536]{1,0:T(8,128)(2,1)}, bf16[...) custom-call(s32[3]{0:T(128)S(1)} %copy-done.117, ...), custom_call_target="tpu_custom_call" | custom-call | flops 1024 | bytes 1024 | tf_op jit(solution)/shard_map/pallas_call | solution.py:183
  103.8 2.5 shard_map.177
  111.6 11.2 %shard_map.176 = (bf16[512,1024]{1,0:T(8,128)(2,1)S(1)}, bf16[512,1024]{1,0:T(8,128)(2,1)}, f32[512,128]{1,0:T(8,128)}, bf16[512,2048]{1,0:T(8,128)(2,1)}, bf16[...) custom-call(s32[3]{0:T(128)S(1)} %copy-done.118, f32[1,1024]{1,0:T(1,128)S(1)} %get-tuple-element.337.refs_0_.refs_2_, ...), custom_call_target="tpu_custom_call" | custom-call | flops 1024 | bytes 1024 | tf_op jit(solution)/shard_map/pallas_call | solution.py:183
  122.9 2.5 collective-permute-start.12
  125.5 11.1 %shard_map.178 = (bf16[512,1024]{1,0:T(8,128)(2,1)S(1)}, bf16[512,1024]{1,0:T(8,128)(2,1)}, f32[512,128]{1,0:T(8,128)}, bf16[512,2048]{1,0:T(8,128)(2,1)}, bf16[...) custom-call(s32[3]{0:T(128)S(1)} %copy-done.118, f32[1,1024]{1,0:T(1,128)S(1)} %get-tuple-element.337.refs_0_.refs_2_, ...), custom_call_target="tpu_custom_call" | custom-call | flops 1024 | bytes 1024 | tf_op jit(solution)/shard_map/pallas_call | solution.py:183
  136.5 3.3 collective-permute-start.17
  141.5 7.6 %collective-permute-done.14.refs_7_.refs_6_.refs_10_.refs_3_ = bf16[512,512]{1,0:T(8,128)(2,1)S(1)} collective-permute-done((bf16[512,512]{1,0:T(8,128)(2,1)S(1)}, bf16[512,512]{1,0:T(8,128)(2,1)S(1)}, u32[]{:S(2)}, u32[]{:S(2)}) %collective-permute-start.14) | collective-permute-done | bytes 524320 | tf_op jit(solution)/shard_map/ppermute | solution.py:933
  149.8 4.2 shard_map.180
  156.1 3.8 shard_map.182
  179.5 5.8 shard_map.189
  201.8 6.3 shard_map.190
  214.7 87.6 %collective-permute-done.36.refs_0_.refs_3_ = bf16[512,1024]{1,0:T(8,128)(2,1)} collective-permute-done((bf16[512,1024]{1,0:T(8,128)(2,1)}, bf16[512,1024]{1,0:T(8,128)(2,1)}, u32[]{:S(2)}, u32[]{:S(2)}) %collective-permute-start.36) | collective-permute-done | bytes 1048608 | tf_op jit(solution)/shard_map/ppermute | solution.py:920
  304.4 3.4 shard_map.196.refs_1_
  307.8 3.4 collective-permute-start.37
  311.2 10.5 %collective-permute-done.29.refs_0_.refs_2_ = bf16[512,1024]{1,0:T(8,128)(2,1)} collective-permute-done((bf16[512,1024]{1,0:T(8,128)(2,1)}, bf16[512,1024]{1,0:T(8,128)(2,1)}, u32[]{:S(2)}, u32[]{:S(2)}) %collective-permute-start.29) | collective-permute-done | bytes 1048608 | tf_op jit(solution)/shard_map/ppermute | solution.py:920
  321.7 3.3 shard_map.191.refs_1_
  324.9 3.3 collective-permute-start.30
  338.9 9.8 %shard_map.197 = (bf16[512,1024]{1,0:T(8,128)(2,1)S(1)}, f32[2,8,1024]{2,1,0:T(8,128)}, bf16[512,2048]{1,0:T(8,128)(2,1)}, bf16[512,1024]{1,0:T(8,128)(2,1)}) custom-call(s32[3]{0:T(128)S(1)} %copy-done.118, f32[1,1024]{1,0:T(1,128)S(1)} %get-tuple-element.336.refs_0_, bf16[512,1024]{1,0:T(8,128)(2,1)S(1)} %shard_map.196.refs_1_, ...), custom_call_target="tpu_custom_call" | custom-call | flops 1024 | bytes 1024 | tf_op jit(solution)/shard_map/pallas_call | solution.py:183
  349.7 2.6 collective-permute-start.38
  352.4 9.5 %shard_map.192 = (bf16[512,1024]{1,0:T(8,128)(2,1)S(1)}, f32[2,8,1024]{2,1,0:T(8,128)}, bf16[512,2048]{1,0:T(8,128)(2,1)}, bf16[512,1024]{1,0:T(8,128)(2,1)}) custom-call(s32[3]{0:T(128)S(1)} %copy-done.118, f32[1,1024]{1,0:T(1,128)S(1)} %get-tuple-element.336.refs_0_, bf16[512,1024]{1,0:T(8,128)(2,1)S(1)} %shard_map.191.refs_1_, ...), custom_call_target="tpu_custom_call" | custom-call | flops 1024 | bytes 1024 | tf_op jit(solution)/shard_map/pallas_call | solution.py:183
  361.9 3.3 collective-permute-start.31
  371.9 11.8 %shard_map.200 = (bf16[512,1536]{1,0:T(8,128)(2,1)S(1)}, bf16[512,1536]{1,0:T(8,128)(2,1)S(1)}, bf16[512,1536]{1,0:T(8,128)(2,1)}, bf16[512,1536]{1,0:T(8,128)(2,1)S(1)}) custom-call(s32[3]{0:T(128)S(1)} %copy-done.118, bf16[512,1024]{1,0:T(8,128)(2,1)} %copy-done.50, bf16[512,1024]{1,0:T(8,128)(2,1)} %copy-done.52, ...), custom_call_target="tpu_custom_call" | custom-call | flops 1024 | bytes 1024 | tf_op jit(solution)/shard_map/pallas_call | solution.py:183
  386.8 16.1 %shard_map.201 = (bf16[512,1024]{1,0:T(8,128)(2,1)S(1)}, f32[2,8,1024]{2,1,0:T(8,128)}, bf16[512,1536]{1,0:T(8,128)(2,1)}, bf16[512,1024]{1,0:T(8,128)(2,1)S(1)}) custom-call(s32[3]{0:T(128)S(1)} %copy-done.118, s32[1,512]{1,0:T(1,128)S(1)} %get-tuple-element.351.refs_1_.refs_0_, s32[512,1]{1,0:T(8,128)S(1)} %copy-done.70, ...), custom_call_target="tpu_custom_call" | custom-call | flops 1024 | bytes 1024 | tf_op jit(solution)/shard_map/pallas_call | solution.py:183
  403.9 2.6 collective-permute-start.41
  406.5 15.9 %shard_map.193 = (bf16[512,1024]{1,0:T(8,128)(2,1)S(1)}, f32[2,8,1024]{2,1,0:T(8,128)}, bf16[512,1536]{1,0:T(8,128)(2,1)}, bf16[512,1024]{1,0:T(8,128)(2,1)S(1)}) custom-call(s32[3]{0:T(128)S(1)} %copy-done.118, s32[1,512]{1,0:T(1,128)S(1)} %get-tuple-element.352.refs_1_.refs_0_, s32[512,1]{1,0:T(8,128)S(1)} %copy-done.82, ...), custom_call_target="tpu_custom_call" | custom-call | flops 1024 | bytes 1024 | tf_op jit(solution)/shard_map/pallas_call | solution.py:183
  428.7 3.3 collective-permute-start.32
  432.2 13.9 %shard_map.204 = (bf16[512,2048]{1,0:T(8,128)(2,1)S(1)}, bf16[512,2048]{1,0:T(8,128)(2,1)S(1)}, bf16[512,2048]{1,0:T(8,128)(2,1)S(1)}, bf16[512,2048]{1,0:T(8,128)(2,1)S(1)}) custom-call(s32[3]{0:T(128)S(1)} %copy-done.118, bf16[512,1024]{1,0:T(8,128)(2,1)} %copy-done.54, bf16[512,1024]{1,0:T(8,128)(2,1)} %copy-done.44, ...), custom_call_target="tpu_custom_call" | custom-call | flops 1024 | bytes 1024 | tf_op jit(solution)/shard_map/pallas_call | solution.py:183
  450.9 3.5 fusion.9
  458.3 4.1 shard_map.205
  468.4 3.6 collective-permute-start.53
  473.5 4.1 collective-permute-done.55
  477.8 3.6 collective-permute-done.56
  482.2 14.0 %collective-permute-done.43 = bf16[2,128,1024]{2,1,0:T(8,128)(2,1)S(1)} collective-permute-done((bf16[2,128,1024]{2,1,0:T(8,128)(2,1)S(1)}, bf16[2,128,1024]{2,1,0:T(8,128)(2,1)S(1)}, u32[]{:S(2)}, u32[]{:S(2)}) %collective-permute-start.43) | collective-permute-done | bytes 524320 | tf_op jit(solution)/shard_map/ppermute | solution.py:924
  496.2 2.9 collective-permute-start.47
  499.4 5.6 shard_map.206
  505.9 3.8 collective-permute-start.57
  510.5 5.0 collective-permute-start.60
  515.6 25.5 %collective-permute-done.60.refs_7_ = f32[2,3,256]{2,1,0:T(4,128)S(1)} collective-permute-done((f32[2,3,256]{2,1,0:T(4,128)S(1)}, f32[2,3,256]{2,1,0:T(4,128)S(1)}, u32[]{:S(2)}, u32[]{:S(2)}) %collective-permute-start.60) | collective-permute-done | bytes 6176 | tf_op jit(solution)/shard_map/ppermute | solution.py:933
  541.0 3.7 collective-permute-start.46
  544.8 7.1 shard_map.207
  551.9 4.5 collective-permute-start.61
  559.2 9.9 %collective-permute-done.46.refs_1_ = bf16[512,2048]{1,0:T(8,128)(2,1)S(1)} collective-permute-done((bf16[512,2048]{1,0:T(8,128)(2,1)S(1)}, bf16[512,2048]{1,0:T(8,128)(2,1)S(1)}, u32[]{:S(2)}, u32[]{:S(2)}) %collective-permute-start.46) | collective-permute-done | bytes 2097184 | tf_op jit(solution)/shard_map/ppermute | solution.py:925
  569.1 18.5 %collective-permute-done.63.refs_6_.refs_4_.refs_3_ = bf16[512,1536]{1,0:T(8,128)(2,1)S(1)} collective-permute-done((bf16[512,1536]{1,0:T(8,128)(2,1)S(1)}, bf16[512,1536]{1,0:T(8,128)(2,1)S(1)}, u32[]{:S(2)}, u32[]{:S(2)}) %collective-permute-start.63) | collective-permute-done | bytes 1572896 | tf_op jit(solution)/shard_map/ppermute | solution.py:933
  588.9 5.4 shard_map.208
  594.3 4.7 collective-permute-start.65
  602.5 26.8 %collective-permute-done.68.refs_5_ = f32[2,3,256]{2,1,0:T(4,128)S(1)} collective-permute-done((f32[2,3,256]{2,1,0:T(4,128)S(1)}, f32[2,3,256]{2,1,0:T(4,128)S(1)}, u32[]{:S(2)}, u32[]{:S(2)}) %collective-permute-start.68) | collective-permute-done | bytes 6176 | tf_op jit(solution)/shard_map/ppermute | solution.py:933
  629.3 2.7 shard_map.209
  634.1 30.1 %collective-permute-done.70.refs_2_.refs_4_.refs_3_ = bf16[512,2048]{1,0:T(8,128)(2,1)S(1)} collective-permute-done((bf16[512,2048]{1,0:T(8,128)(2,1)S(1)}, bf16[512,2048]{1,0:T(8,128)(2,1)S(1)}, u32[]{:S(2)}, u32[]{:S(2)}) %collective-permute-start.70) | collective-permute-done | bytes 2097184 | tf_op jit(solution)/shard_map/ppermute | solution.py:938
  672.0 2.9 shard_map.212.refs_8_
  675.0 18.7 %collective-permute-done.71.refs_5_.refs_4_ = bf16[512,2048]{1,0:T(8,128)(2,1)S(1)} collective-permute-done((bf16[512,2048]{1,0:T(8,128)(2,1)S(1)}, bf16[512,2048]{1,0:T(8,128)(2,1)S(1)}, u32[]{:S(2)}, u32[]{:S(2)}) %collective-permute-start.71) | collective-permute-done | bytes 2097184 | tf_op jit(solution)/shard_map/ppermute | solution.py:938
  696.7 2.6 shard_map.213.refs_6_
  710.4 3.0 shard_map.214
  (554 shorter events, 159.4 us)
Async XLA Ops:
  1.8 15.8 %collective-permute-start = (bf16[2,128,1024]{2,1,0:T(8,128)(2,1)S(1)}, bf16[2,128,1024]{2,1,0:T(8,128)(2,1)S(1)}, u32[]{:S(2)}, u32[]{:S(2)}) collective-permute-start(bf16[2,128,1024]{2,1,0:T(8,128)(2,1)S(1)} %dynamic-slice_bitcast_fusion.5), channel_id=1, source_target_pairs={{0,2},{1,3},{2,0},{3,1},{4,6},{5,7},{6,4},{7,5},{8,10},{9,11},{10,... | collective-permute-start | bytes 1572872 | tf_op jit(solution)/shard_map/ppermute | solution.py:924
  8.3 34.6 %collective-permute-start.2 = (bf16[512,768]{1,0:T(8,128)(2,1)}, bf16[512,768]{1,0:T(8,128)(2,1)S(1)}, u32[]{:S(2)}, u32[]{:S(2)}) collective-permute-start(bf16[512,768]{1,0:T(8,128)(2,1)} %shard_map.169), channel_id=1, source_target_pairs={{0,2},{1,3},{2,0},{3,1},{4,6},{5,7},{6,4},{7,5},{8,10},{9,11},{10,... | collective-permute-start | bytes 2359304 | tf_op jit(solution)/shard_map/ppermute | solution.py:924
  10.7 28.5 %collective-permute-start.4 = (bf16[128,1024]{1,0:T(8,128)(2,1)}, bf16[128,1024]{1,0:T(8,128)(2,1)S(1)}, u32[]{:S(2)}, u32[]{:S(2)}) collective-permute-start(bf16[128,1024]{1,0:T(8,128)(2,1)} %shard_map.170), channel_id=1, source_target_pairs={{0,2},{1,3},{2,0},{3,1},{4,6},{5,7},{6,4},{7,5},{8,10},{9,11},{10,... | collective-permute-start | bytes 786440 | tf_op jit(solution)/shard_map/ppermute | solution.py:924
  19.9 24.7 %collective-permute-start.1 = (bf16[1,2,1,128,1024]{4,3,1,2,0:T(8,128)(2,1)}, bf16[1,2,1,128,1024]{4,3,1,2,0:T(8,128)(2,1)}, u32[]{:S(2)}, u32[]{:S(2)}) collective-permute-start(bf16[1,2,1,128,1024]{4,3,1,2,0:T(8,128)(2,1)} %maximum_bitcast_fusion.1), channel_id=1, source_target_pairs={{0,1},{1,0},{2,3},{3,2},{4,5},{5,4},{6,7},{7,6},{8,9},{9,8},{10,11... | collective-permute-start | bytes 1572872 | tf_op jit(solution)/shard_map/ppermute | solution.py:924
  22.7 24.4 %collective-permute-start.6 = (bf16[1,2,1,128,1024]{4,3,1,2,0:T(8,128)(2,1)}, bf16[1,2,1,128,1024]{4,3,1,2,0:T(8,128)(2,1)}, u32[]{:S(2)}, u32[]{:S(2)}) collective-permute-start(bf16[1,2,1,128,1024]{4,3,1,2,0:T(8,128)(2,1)} %maximum_bitcast_fusion.2), channel_id=1, source_target_pairs={{0,1},{1,0},{2,3},{3,2},{4,5},{5,4},{6,7},{7,6},{8,9},{9,8},{10,11... | collective-permute-start | bytes 1572872 | tf_op jit(solution)/shard_map/ppermute | solution.py:924
  25.7 54.9 %collective-permute-start.8 = (bf16[512,1024]{1,0:T(8,128)(2,1)}, bf16[512,1024]{1,0:T(8,128)(2,1)}, u32[]{:S(2)}, u32[]{:S(2)}) collective-permute-start(bf16[512,1024]{1,0:T(8,128)(2,1)} %shard_map.173), channel_id=1, source_target_pairs={{0,2},{1,3},{2,0},{3,1},{4,6},{5,7},{6,4},{7,5},{8,10},{9,11},{10,... | collective-permute-start | bytes 3145736 | tf_op jit(solution)/shard_map/ppermute | solution.py:925
  39.2 44.8 %collective-permute-start.10 = (bf16[512,1024]{1,0:T(8,128)(2,1)}, bf16[512,1024]{1,0:T(8,128)(2,1)}, u32[]{:S(2)}, u32[]{:S(2)}) collective-permute-start(bf16[512,1024]{1,0:T(8,128)(2,1)} %shard_map.174), channel_id=1, source_target_pairs={{0,2},{1,3},{2,0},{3,1},{4,6},{5,7},{6,4},{7,5},{8,10},{9,11},{10,... | collective-permute-start | bytes 3145736 | tf_op jit(solution)/shard_map/ppermute | solution.py:925
  42.9 10.5 %collective-permute-start.5 = (bf16[128,1024]{1,0:T(8,128)(2,1)S(1)}, bf16[128,1024]{1,0:T(8,128)(2,1)S(1)}, u32[]{:S(2)}, u32[]{:S(2)}) collective-permute-start(bf16[128,1024]{1,0:T(8,128)(2,1)S(1)} %collective-permute-done.4.refs_9_), channel_id=1, source_target_pairs={{0,4},{4,0},{8,12},{12,8},{1,5},{5,1},{9,13},{13,9},{2,6},{6,2},{1... | collective-permute-start | bytes 786440 | tf_op jit(solution)/shard_map/ppermute | solution.py:933
  44.6 20.9 %collective-permute-start.3 = (bf16[512,768]{1,0:T(8,128)(2,1)S(1)}, bf16[512,768]{1,0:T(8,128)(2,1)S(1)}, u32[]{:S(2)}, u32[]{:S(2)}) collective-permute-start(bf16[512,768]{1,0:T(8,128)(2,1)S(1)} %collective-permute-done.2.refs_6_.refs_15_), channel_id=1, source_target_pairs={{0,4},{4,0},{8,12},{12,8},{1,5},{5,1},{9,13},{13,9},{2,6},{6,2},{1... | collective-permute-start | bytes 2359304 | tf_op jit(solution)/shard_map/ppermute | solution.py:933
  79.1 27.2 %collective-permute-start.7 = (bf16[512,1024]{1,0:T(8,128)(2,1)}, bf16[512,1024]{1,0:T(8,128)(2,1)}, u32[]{:S(2)}, u32[]{:S(2)}) collective-permute-start(bf16[512,1024]{1,0:T(8,128)(2,1)} %get-tuple-element.143.refs_3_), channel_id=1, source_target_pairs={{0,1},{1,0},{2,3},{3,2},{4,5},{5,4},{6,7},{7,6},{8,9},{9,8},{10,11... | collective-permute-start | bytes 3145736 | tf_op jit(solution)/shard_map/ppermute | solution.py:924
  80.5 27.4 %collective-permute-start.9 = (bf16[512,1024]{1,0:T(8,128)(2,1)}, bf16[512,1024]{1,0:T(8,128)(2,1)}, u32[]{:S(2)}, u32[]{:S(2)}) collective-permute-start(bf16[512,1024]{1,0:T(8,128)(2,1)} %collective-permute-done.8.refs_6_.refs_7_), channel_id=1, source_target_pairs={{0,4},{4,0},{8,12},{12,8},{1,5},{5,1},{9,13},{13,9},{2,6},{6,2},{1... | collective-permute-start | bytes 3145736 | tf_op jit(solution)/shard_map/ppermute | solution.py:938
  84.0 24.7 %collective-permute-start.11 = (bf16[512,1024]{1,0:T(8,128)(2,1)}, bf16[512,1024]{1,0:T(8,128)(2,1)}, u32[]{:S(2)}, u32[]{:S(2)}) collective-permute-start(bf16[512,1024]{1,0:T(8,128)(2,1)} %collective-permute-done.10.refs_9_.refs_10_), channel_id=1, source_target_pairs={{0,4},{4,0},{8,12},{12,8},{1,5},{5,1},{9,13},{13,9},{2,6},{6,2},{1... | collective-permute-start | bytes 3145736 | tf_op jit(solution)/shard_map/ppermute | solution.py:938
  101.2 24.3 %collective-permute-start.15 = (bf16[512,1024]{1,0:T(8,128)(2,1)}, bf16[512,1024]{1,0:T(8,128)(2,1)}, u32[]{:S(2)}, u32[]{:S(2)}) collective-permute-start(bf16[512,1024]{1,0:T(8,128)(2,1)} %get-tuple-element.147.refs_3_), channel_id=1, source_target_pairs={{0,1},{1,0},{2,3},{3,2},{4,5},{5,4},{6,7},{7,6},{8,9},{9,8},{10,11... | collective-permute-start | bytes 3145736 | tf_op jit(solution)/shard_map/ppermute | solution.py:924
  101.8 59.5 %collective-permute-start.19 = (bf16[1024,1024]{1,0:T(8,128)(2,1)}, bf16[1024,1024]{1,0:T(8,128)(2,1)}, u32[]{:S(2)}, u32[]{:S(2)}) collective-permute-start(bf16[1024,1024]{1,0:T(8,128)(2,1)} %shard_map.171.refs_11_), channel_id=1, source_target_pairs={{16,18},{17,19},{18,16},{19,17},{20,22},{21,23},{22,20},{23,21},{2... | collective-permute-start | bytes 6291464 | tf_op jit(solution)/shard_map/ppermute | solution.py:925
  106.3 33.5 %collective-permute-start.13 = (bf16[512,512]{1,0:T(8,128)(2,1)}, bf16[512,512]{1,0:T(8,128)(2,1)S(1)}, u32[]{:S(2)}, u32[]{:S(2)}) collective-permute-start(bf16[512,512]{1,0:T(8,128)(2,1)} %shard_map.177), channel_id=1, source_target_pairs={{0,2},{1,3},{2,0},{3,1},{4,6},{5,7},{6,4},{7,5},{8,10},{9,11},{10,... | collective-permute-start | bytes 1572872 | tf_op jit(solution)/shard_map/ppermute | solution.py:924
  122.9 26.9 %collective-permute-start.12 = (bf16[512,1024]{1,0:T(8,128)(2,1)S(1)}, bf16[512,1024]{1,0:T(8,128)(2,1)S(1)}, u32[]{:S(2)}, u32[]{:S(2)}) collective-permute-start(bf16[512,1024]{1,0:T(8,128)(2,1)S(1)} %get-tuple-element.146.refs_3_), channel_id=1, source_target_pairs={{0,1},{1,0},{2,3},{3,2},{4,5},{5,4},{6,7},{7,6},{8,9},{9,8},{10,11... | collective-permute-start | bytes 3145736 | tf_op jit(solution)/shard_map/ppermute | solution.py:925
  136.5 19.5 %collective-permute-start.17 = (bf16[512,1024]{1,0:T(8,128)(2,1)S(1)}, bf16[512,1024]{1,0:T(8,128)(2,1)S(1)}, u32[]{:S(2)}, u32[]{:S(2)}) collective-permute-start(bf16[512,1024]{1,0:T(8,128)(2,1)S(1)} %get-tuple-element.153.refs_3_), channel_id=1, source_target_pairs={{0,1},{1,0},{2,3},{3,2},{4,5},{5,4},{6,7},{7,6},{8,9},{9,8},{10,11... | collective-permute-start | bytes 3145736 | tf_op jit(solution)/shard_map/ppermute | solution.py:925
  139.9 9.2 %collective-permute-start.14 = (bf16[512,512]{1,0:T(8,128)(2,1)S(1)}, bf16[512,512]{1,0:T(8,128)(2,1)S(1)}, u32[]{:S(2)}, u32[]{:S(2)}) collective-permute-start(bf16[512,512]{1,0:T(8,128)(2,1)S(1)} %collective-permute-done.13.refs_6_.refs_5_.refs_9_.refs_2_), channel_id=1, source_target_pairs={{0,4},{4,0},{8,12},{12,8},{1,5},{5,1},{9,13},{13,9},{2,6},{6,2},{1... | collective-permute-start | bytes 1572872 | tf_op jit(solution)/shard_map/ppermute | solution.py:933
  154.0 10.1 %collective-permute-start.16 = (bf16[512,1024]{1,0:T(8,128)(2,1)S(1)}, bf16[512,1024]{1,0:T(8,128)(2,1)S(1)}, u32[]{:S(2)}, u32[]{:S(2)}) collective-permute-start(bf16[512,1024]{1,0:T(8,128)(2,1)S(1)} %get-tuple-element.152), channel_id=1, source_target_pairs={{0,16},{1,17},{2,18},{3,19},{4,20},{5,21},{6,22},{7,23},{8,24},{9,... | collective-permute-start | bytes 3145736 | tf_op jit(solution)/shard_map/ppermute | solution.py:920
  161.3 12.3 %collective-permute-start.20 = (bf16[1024,1024]{1,0:T(8,128)(2,1)}, bf16[1024,1024]{1,0:T(8,128)(2,1)}, u32[]{:S(2)}, u32[]{:S(2)}) collective-permute-start(bf16[1024,1024]{1,0:T(8,128)(2,1)} %collective-permute-done.19.refs_6_.refs_9_.refs_8_.refs_11_), channel_id=1, source_target_pairs={{16,20},{20,16},{24,28},{28,24},{17,21},{21,17},{25,29},{29,25},{1... | collective-permute-start | bytes 6291464 | tf_op jit(solution)/shard_map/ppermute | solution.py:938
  170.4 5.4 collective-permute-start.25
  177.3 10.7 %collective-permute-start.22 = (bf16[512,1024]{1,0:T(8,128)(2,1)S(1)}, bf16[512,1024]{1,0:T(8,128)(2,1)S(1)}, u32[]{:S(2)}, u32[]{:S(2)}) collective-permute-start(bf16[512,1024]{1,0:T(8,128)(2,1)S(1)} %get-tuple-element.162.refs_3_), channel_id=1, source_target_pairs={{16,17},{17,16},{18,19},{19,18},{20,21},{21,20},{22,23},{23,22},{2... | collective-permute-start | bytes 3145736 | tf_op jit(solution)/shard_map/ppermute | solution.py:925
  185.2 10.0 %collective-permute-start.35 = (bf16[512,1024]{1,0:T(8,128)(2,1)}, bf16[512,1024]{1,0:T(8,128)(2,1)}, u32[]{:S(2)}, u32[]{:S(2)}) collective-permute-start(bf16[512,1024]{1,0:T(8,128)(2,1)} %get-tuple-element.197.refs_4_), channel_id=1, source_target_pairs={{16,17},{17,16},{18,19},{19,18},{20,21},{21,20},{22,23},{23,22},{2... | collective-permute-start | bytes 3145736 | tf_op jit(solution)/shard_map/ppermute | solution.py:925
  189.7 12.1 %collective-permute-start.28 = (bf16[512,1024]{1,0:T(8,128)(2,1)}, bf16[512,1024]{1,0:T(8,128)(2,1)}, u32[]{:S(2)}, u32[]{:S(2)}) collective-permute-start(bf16[512,1024]{1,0:T(8,128)(2,1)} %get-tuple-element.171.refs_4_), channel_id=1, source_target_pairs={{16,17},{17,16},{18,19},{19,18},{20,21},{21,20},{22,23},{23,22},{2... | collective-permute-start | bytes 3145736 | tf_op jit(solution)/shard_map/ppermute | solution.py:925
  193.3 139.2 %collective-permute-start.40 = (bf16[1024,1024]{1,0:T(8,128)(2,1)}, bf16[1024,1024]{1,0:T(8,128)(2,1)}, u32[]{:S(2)}, u32[]{:S(2)}) collective-permute-start(bf16[1024,1024]{1,0:T(8,128)(2,1)} %get-tuple-element.224), channel_id=1, source_target_pairs={{16,18},{17,19},{18,16},{19,17},{20,22},{21,23},{22,20},{23,21},{2... | collective-permute-start | bytes 6291464 | tf_op jit(solution)/shard_map/ppermute | solution.py:925
  200.5 101.8 %collective-permute-start.36 = (bf16[512,1024]{1,0:T(8,128)(2,1)}, bf16[512,1024]{1,0:T(8,128)(2,1)}, u32[]{:S(2)}, u32[]{:S(2)}) collective-permute-start(bf16[512,1024]{1,0:T(8,128)(2,1)} %get-tuple-element.201), channel_id=1, source_target_pairs={{16,0},{17,1},{18,2},{19,3},{20,4},{21,5},{22,6},{23,7},{24,8},{25... | collective-permute-start | bytes 3145736 | tf_op jit(solution)/shard_map/ppermute | solution.py:920
  208.1 113.5 %collective-permute-start.29 = (bf16[512,1024]{1,0:T(8,128)(2,1)}, bf16[512,1024]{1,0:T(8,128)(2,1)}, u32[]{:S(2)}, u32[]{:S(2)}) collective-permute-start(bf16[512,1024]{1,0:T(8,128)(2,1)} %get-tuple-element.175), channel_id=1, source_target_pairs={{16,0},{17,1},{18,2},{19,3},{20,4},{21,5},{22,6},{23,7},{24,8},{25... | collective-permute-start | bytes 3145736 | tf_op jit(solution)/shard_map/ppermute | solution.py:920
  209.6 120.8 %collective-permute-start.39 = (bf16[512,1024]{1,0:T(8,128)(2,1)}, bf16[512,1024]{1,0:T(8,128)(2,1)}, u32[]{:S(2)}, u32[]{:S(2)}) collective-permute-start(bf16[512,1024]{1,0:T(8,128)(2,1)} %get-tuple-element.218.refs_4_), channel_id=1, source_target_pairs={{16,17},{17,16},{18,19},{19,18},{20,21},{21,20},{22,23},{23,22},{2... | collective-permute-start | bytes 3145736 | tf_op jit(solution)/shard_map/ppermute | solution.py:925
  213.2 122.3 %collective-permute-start.27 = (bf16[2,128,1024]{2,1,0:T(8,128)(2,1)}, bf16[2,128,1024]{2,1,0:T(8,128)(2,1)}, u32[]{:S(2)}, u32[]{:S(2)}) collective-permute-start(bf16[2,128,1024]{2,1,0:T(8,128)(2,1)} %fusion.24), channel_id=1, source_target_pairs={{0,2},{1,3},{2,0},{3,1},{4,6},{5,7},{6,4},{7,5},{8,10},{9,11},{10,... | collective-permute-start | bytes 1572872 | tf_op jit(solution)/shard_map/ppermute | solution.py:924
  307.8 31.1 %collective-permute-start.37 = (bf16[512,1024]{1,0:T(8,128)(2,1)S(1)}, bf16[512,1024]{1,0:T(8,128)(2,1)S(1)}, u32[]{:S(2)}, u32[]{:S(2)}) collective-permute-start(bf16[512,1024]{1,0:T(8,128)(2,1)S(1)} %shard_map.196.refs_1_), channel_id=1, source_target_pairs={{0,1},{1,0},{2,3},{3,2},{4,5},{5,4},{6,7},{7,6},{8,9},{9,8},{10,11... | collective-permute-start | bytes 3145736 | tf_op jit(solution)/shard_map/ppermute | solution.py:925
  324.9 27.4 %collective-permute-start.30 = (bf16[512,1024]{1,0:T(8,128)(2,1)S(1)}, bf16[512,1024]{1,0:T(8,128)(2,1)S(1)}, u32[]{:S(2)}, u32[]{:S(2)}) collective-permute-start(bf16[512,1024]{1,0:T(8,128)(2,1)S(1)} %shard_map.191.refs_1_), channel_id=1, source_target_pairs={{0,1},{1,0},{2,3},{3,2},{4,5},{5,4},{6,7},{7,6},{8,9},{9,8},{10,11... | collective-permute-start | bytes 3145736 | tf_op jit(solution)/shard_map/ppermute | solution.py:925
  330.4 93.0 %collective-permute-start.44 = (bf16[1024,1024]{1,0:T(8,128)(2,1)}, bf16[1024,1024]{1,0:T(8,128)(2,1)}, u32[]{:S(2)}, u32[]{:S(2)}) collective-permute-start(bf16[1024,1024]{1,0:T(8,128)(2,1)} %get-tuple-element.240), channel_id=1, source_target_pairs={{16,18},{17,19},{18,16},{19,17},{20,22},{21,23},{22,20},{23,21},{2... | collective-permute-start | bytes 6291464 | tf_op jit(solution)/shard_map/ppermute | solution.py:925
  333.4 90.0 %collective-permute-start.45 = (bf16[1024,1024]{1,0:T(8,128)(2,1)}, bf16[1024,1024]{1,0:T(8,128)(2,1)}, u32[]{:S(2)}, u32[]{:S(2)}) collective-permute-start(bf16[1024,1024]{1,0:T(8,128)(2,1)} %get-tuple-element.241.refs_2_), channel_id=1, source_target_pairs={{16,20},{28,24},{17,21},{29,25},{18,22},{30,26},{19,23},{31,27}} | collective-permute-start | bytes 6291464 | tf_op jit(solution)/shard_map/ppermute | solution.py:938
  335.5 29.7 %collective-permute-start.33 = (bf16[512,1024]{1,0:T(8,128)(2,1)S(1)}, bf16[512,1024]{1,0:T(8,128)(2,1)S(1)}, u32[]{:S(2)}, u32[]{:S(2)}) collective-permute-start(bf16[512,1024]{1,0:T(8,128)(2,1)S(1)} %copy-done.120), channel_id=1, source_target_pairs={{16,17},{17,16},{18,19},{19,18},{20,21},{21,20},{22,23},{23,22},{2... | collective-permute-start | bytes 3145736 | tf_op jit(solution)/shard_map/ppermute | solution.py:925
  349.7 36.9 %collective-permute-start.38 = (bf16[512,1024]{1,0:T(8,128)(2,1)}, bf16[512,1024]{1,0:T(8,128)(2,1)}, u32[]{:S(2)}, u32[]{:S(2)}) collective-permute-start(bf16[512,1024]{1,0:T(8,128)(2,1)} %get-tuple-element.206.refs_4_), channel_id=1, source_target_pairs={{0,1},{1,0},{2,3},{3,2},{4,5},{5,4},{6,7},{7,6},{8,9},{9,8},{10,11... | collective-permute-start | bytes 3145736 | tf_op jit(solution)/shard_map/ppermute | solution.py:925
  361.9 44.6 %collective-permute-start.31 = (bf16[512,1024]{1,0:T(8,128)(2,1)}, bf16[512,1024]{1,0:T(8,128)(2,1)S(1)}, u32[]{:S(2)}, u32[]{:S(2)}) collective-permute-start(bf16[512,1024]{1,0:T(8,128)(2,1)} %get-tuple-element.180.refs_4_), channel_id=1, source_target_pairs={{0,1},{1,0},{2,3},{3,2},{4,5},{5,4},{6,7},{7,6},{8,9},{9,8},{10,11... | collective-permute-start | bytes 3145736 | tf_op jit(solution)/shard_map/ppermute | solution.py:925
  384.9 69.7 %collective-permute-start.49 = (bf16[512,1536]{1,0:T(8,128)(2,1)}, bf16[512,1536]{1,0:T(8,128)(2,1)}, u32[]{:S(2)}, u32[]{:S(2)}) collective-permute-start(bf16[512,1536]{1,0:T(8,128)(2,1)} %get-tuple-element.249), channel_id=1, source_target_pairs={{0,2},{1,3},{2,0},{3,1},{4,6},{5,7},{6,4},{7,5},{8,10},{9,11},{10,... | collective-permute-start | bytes 4718600 | tf_op jit(solution)/shard_map/ppermute | solution.py:924
  403.9 43.6 %collective-permute-start.41 = (bf16[2,1,128,1024]{3,2,0,1:T(8,128)(2,1)}, bf16[2,1,128,1024]{3,2,0,1:T(8,128)(2,1)}, u32[]{:S(2)}, u32[]{:S(2)}) collective-permute-start(bf16[2,1,128,1024]{3,2,0,1:T(8,128)(2,1)} %dynamic-slice_bitcast_fusion.1), channel_id=1, source_target_pairs={{0,1},{1,0},{2,3},{3,2},{4,5},{5,4},{6,7},{7,6},{8,9},{9,8},{10,11... | collective-permute-start | bytes 1572872 | tf_op jit(solution)/shard_map/ppermute | solution.py:925
  424.6 30.6 %collective-permute-start.50 = (bf16[1024,1024]{1,0:T(8,128)(2,1)}, bf16[1024,1024]{1,0:T(8,128)(2,1)}, u32[]{:S(2)}, u32[]{:S(2)}) collective-permute-start(bf16[1024,1024]{1,0:T(8,128)(2,1)} %get-tuple-element.250.refs_2_), channel_id=1, source_target_pairs={{20,24},{24,20},{21,25},{25,21},{22,26},{26,22},{23,27},{27,23}} | collective-permute-start | bytes 6291464 | tf_op jit(solution)/shard_map/ppermute | solution.py:938
  426.6 28.6 %collective-permute-start.51 = (bf16[1024,1024]{1,0:T(8,128)(2,1)S(1)}, bf16[1024,1024]{1,0:T(8,128)(2,1)}, u32[]{:S(2)}, u32[]{:S(2)}) collective-permute-start(bf16[1024,1024]{1,0:T(8,128)(2,1)S(1)} %get-tuple-element.242.refs_12_.refs_4_), channel_id=1, source_target_pairs={{16,20},{28,24},{17,21},{29,25},{18,22},{30,26},{19,23},{31,27}} | collective-permute-start | bytes 6291464 | tf_op jit(solution)/shard_map/ppermute | solution.py:938
  428.7 20.7 %collective-permute-start.32 = (bf16[2,1,128,1024]{3,2,0,1:T(8,128)(2,1)S(1)}, bf16[2,1,128,1024]{3,2,0,1:T(8,128)(2,1)S(1)}, u32[]{:S(2)}, u32[]{:S(2)}) collective-permute-start(bf16[2,1,128,1024]{3,2,0,1:T(8,128)(2,1)S(1)} %dynamic-slice_bitcast_fusion.3), channel_id=1, source_target_pairs={{0,1},{1,0},{2,3},{3,2},{4,5},{5,4},{6,7},{7,6},{8,9},{9,8},{10,11... | collective-permute-start | bytes 1572872 | tf_op jit(solution)/shard_map/ppermute | solution.py:925
  447.5 17.9 %collective-permute-start.34 = (bf16[2,1,128,1024]{3,2,0,1:T(8,128)(2,1)}, bf16[2,1,128,1024]{3,2,0,1:T(8,128)(2,1)}, u32[]{:S(2)}, u32[]{:S(2)}) collective-permute-start(bf16[2,1,128,1024]{3,2,0,1:T(8,128)(2,1)} %dynamic-slice_bitcast_fusion.2), channel_id=1, source_target_pairs={{16,17},{17,16},{18,19},{19,18},{20,21},{21,20},{22,23},{23,22},{2... | collective-permute-start | bytes 1572872 | tf_op jit(solution)/shard_map/ppermute | solution.py:925
  449.4 19.0 %collective-permute-start.42 = (bf16[2,1,128,1024]{3,2,0,1:T(8,128)(2,1)}, bf16[2,1,128,1024]{3,2,0,1:T(8,128)(2,1)}, u32[]{:S(2)}, u32[]{:S(2)}) collective-permute-start(bf16[2,1,128,1024]{3,2,0,1:T(8,128)(2,1)} %dynamic-slice_bitcast_fusion), channel_id=1, source_target_pairs={{16,17},{17,16},{18,19},{19,18},{20,21},{21,20},{22,23},{23,22},{2... | collective-permute-start | bytes 1572872 | tf_op jit(solution)/shard_map/ppermute | solution.py:925
  454.6 44.7 %collective-permute-start.48 = (bf16[512,1536]{1,0:T(8,128)(2,1)}, bf16[512,1536]{1,0:T(8,128)(2,1)}, u32[]{:S(2)}, u32[]{:S(2)}) collective-permute-start(bf16[512,1536]{1,0:T(8,128)(2,1)} %copy-done.136), channel_id=1, source_target_pairs={{0,2},{1,3},{2,0},{3,1},{4,6},{5,7},{6,4},{7,5},{8,10},{9,11},{10,... | collective-permute-start | bytes 4718600 | tf_op jit(solution)/shard_map/ppermute | solution.py:924
  462.4 37.0 %collective-permute-start.52 = (bf16[1024,1024]{1,0:T(8,128)(2,1)}, bf16[1024,1024]{1,0:T(8,128)(2,1)}, u32[]{:S(2)}, u32[]{:S(2)}) collective-permute-start(bf16[1024,1024]{1,0:T(8,128)(2,1)} %get-tuple-element.251.refs_2_), channel_id=1, source_target_pairs={{20,24},{24,20},{21,25},{25,21},{22,26},{26,22},{23,27},{27,23}} | collective-permute-start | bytes 6291464 | tf_op jit(solution)/shard_map/ppermute | solution.py:938
  464.5 34.8 %collective-permute-start.54 = (bf16[1024,1024]{1,0:T(8,128)(2,1)}, bf16[1024,1024]{1,0:T(8,128)(2,1)S(1)}, u32[]{:S(2)}, u32[]{:S(2)}) collective-permute-start(bf16[1024,1024]{1,0:T(8,128)(2,1)} %get-tuple-element.253.refs_2_), channel_id=1, source_target_pairs={{20,16},{24,28},{21,17},{25,29},{22,18},{26,30},{23,19},{27,31}} | collective-permute-start | bytes 6291464 | tf_op jit(solution)/shard_map/ppermute | solution.py:938
  465.3 12.2 %collective-permute-start.55 = (f32[2,3,512]{2,0,1:T(2,128)S(1)}, f32[2,3,512]{2,0,1:T(2,128)S(1)}, u32[]{:S(2)}, u32[]{:S(2)}) collective-permute-start(f32[2,3,512]{2,0,1:T(2,128)S(1)} %bitcast.330), channel_id=1, source_target_pairs={{0,2},{1,3},{2,0},{3,1},{4,6},{5,7},{6,4},{7,5},{8,10},{9,11},{10,... | collective-permute-start | bytes 36872 | tf_op jit(solution)/shard_map/ppermute | solution.py:924
  468.4 31.0 %collective-permute-start.53 = (bf16[512,1536]{1,0:T(8,128)(2,1)}, bf16[512,1536]{1,0:T(8,128)(2,1)}, u32[]{:S(2)}, u32[]{:S(2)}) collective-permute-start(bf16[512,1536]{1,0:T(8,128)(2,1)} %get-tuple-element.252.refs_4_.refs_9_), channel_id=1, source_target_pairs={{0,4},{12,8},{1,5},{13,9},{2,6},{14,10},{3,7},{15,11},{16,20},{28,... | collective-permute-start | bytes 4718600 | tf_op jit(solution)/shard_map/ppermute | solution.py:933
  481.4 14.9 %collective-permute-start.43 = (bf16[2,128,1024]{2,1,0:T(8,128)(2,1)S(1)}, bf16[2,128,1024]{2,1,0:T(8,128)(2,1)S(1)}, u32[]{:S(2)}, u32[]{:S(2)}) collective-permute-start(bf16[2,128,1024]{2,1,0:T(8,128)(2,1)S(1)} %fusion.20), channel_id=1, source_target_pairs={{0,2},{1,3},{2,0},{3,1},{4,6},{5,7},{6,4},{7,5},{8,10},{9,11},{10,... | collective-permute-start | bytes 1572872 | tf_op jit(solution)/shard_map/ppermute | solution.py:924
  496.2 48.5 %collective-permute-start.47 = (bf16[512,2048]{1,0:T(8,128)(2,1)}, bf16[512,2048]{1,0:T(8,128)(2,1)S(1)}, u32[]{:S(2)}, u32[]{:S(2)}) collective-permute-start(bf16[512,2048]{1,0:T(8,128)(2,1)} %copy-done.135), channel_id=1, source_target_pairs={{0,2},{1,3},{2,0},{3,1},{4,6},{5,7},{6,4},{7,5},{8,10},{9,11},{10,... | collective-permute-start | bytes 6291464 | tf_op jit(solution)/shard_map/ppermute | solution.py:925
  505.1 39.7 %collective-permute-start.59 = (bf16[1024,1024]{1,0:T(8,128)(2,1)S(1)}, bf16[1024,1024]{1,0:T(8,128)(2,1)S(1)}, u32[]{:S(2)}, u32[]{:S(2)}) collective-permute-start(bf16[1024,1024]{1,0:T(8,128)(2,1)S(1)} %get-tuple-element.266.refs_2_), channel_id=1, source_target_pairs={{20,16},{24,28},{21,17},{25,29},{22,18},{26,30},{23,19},{27,31}} | collective-permute-start | bytes 6291464 | tf_op jit(solution)/shard_map/ppermute | solution.py:938
  505.9 38.9 %collective-permute-start.57 = (bf16[512,1536]{1,0:T(8,128)(2,1)S(1)}, bf16[512,1536]{1,0:T(8,128)(2,1)S(1)}, u32[]{:S(2)}, u32[]{:S(2)}) collective-permute-start(bf16[512,1536]{1,0:T(8,128)(2,1)S(1)} %get-tuple-element.264.refs_2_.refs_8_), channel_id=1, source_target_pairs={{0,4},{12,8},{1,5},{13,9},{2,6},{14,10},{3,7},{15,11},{16,20},{28,... | collective-permute-start | bytes 4718600 | tf_op jit(solution)/shard_map/ppermute | solution.py:933
  509.8 35.0 %collective-permute-start.58 = (bf16[512,1536]{1,0:T(8,128)(2,1)S(1)}, bf16[512,1536]{1,0:T(8,128)(2,1)S(1)}, u32[]{:S(2)}, u32[]{:S(2)}) collective-permute-start(bf16[512,1536]{1,0:T(8,128)(2,1)S(1)} %get-tuple-element.265.refs_4_), channel_id=1, source_target_pairs={{4,8},{8,4},{5,9},{9,5},{6,10},{10,6},{7,11},{11,7},{20,24},{24,20... | collective-permute-start | bytes 4718600 | tf_op jit(solution)/shard_map/ppermute | solution.py:933
  510.5 30.5 %collective-permute-start.60 = (f32[2,3,256]{2,1,0:T(4,128)S(1)}, f32[2,3,256]{2,1,0:T(4,128)S(1)}, u32[]{:S(2)}, u32[]{:S(2)}) collective-permute-start(f32[2,3,256]{2,1,0:T(4,128)S(1)} %bitcast_add_fusion.1.refs_8_), channel_id=1, source_target_pairs={{0,4},{12,8},{1,5},{13,9},{2,6},{14,10},{3,7},{15,11},{16,20},{28,... | collective-permute-start | bytes 18440 | tf_op jit(solution)/shard_map/ppermute | solution.py:933
  541.0 28.0 %collective-permute-start.46 = (bf16[512,2048]{1,0:T(8,128)(2,1)S(1)}, bf16[512,2048]{1,0:T(8,128)(2,1)S(1)}, u32[]{:S(2)}, u32[]{:S(2)}) collective-permute-start(bf16[512,2048]{1,0:T(8,128)(2,1)S(1)} %copy-done.134), channel_id=1, source_target_pairs={{0,2},{1,3},{2,0},{3,1},{4,6},{5,7},{6,4},{7,5},{8,10},{9,11},{10,... | collective-permute-start | bytes 6291464 | tf_op jit(solution)/shard_map/ppermute | solution.py:925
  551.9 37.0 %collective-permute-start.61 = (bf16[512,2048]{1,0:T(8,128)(2,1)S(1)}, bf16[512,2048]{1,0:T(8,128)(2,1)S(1)}, u32[]{:S(2)}, u32[]{:S(2)}) collective-permute-start(bf16[512,2048]{1,0:T(8,128)(2,1)S(1)} %get-tuple-element.267.refs_2_.refs_8_), channel_id=1, source_target_pairs={{0,4},{12,8},{1,5},{13,9},{2,6},{14,10},{3,7},{15,11}} | collective-permute-start | bytes 6291464 | tf_op jit(solution)/shard_map/ppermute | solution.py:938
  556.4 12.6 %collective-permute-start.62 = (bf16[512,1536]{1,0:T(8,128)(2,1)S(1)}, bf16[512,1536]{1,0:T(8,128)(2,1)S(1)}, u32[]{:S(2)}, u32[]{:S(2)}) collective-permute-start(bf16[512,1536]{1,0:T(8,128)(2,1)S(1)} %get-tuple-element.268.refs_4_), channel_id=1, source_target_pairs={{4,8},{8,4},{5,9},{9,5},{6,10},{10,6},{7,11},{11,7},{20,24},{24,20... | collective-permute-start | bytes 4718600 | tf_op jit(solution)/shard_map/ppermute | solution.py:933
  557.2 30.3 %collective-permute-start.63 = (bf16[512,1536]{1,0:T(8,128)(2,1)S(1)}, bf16[512,1536]{1,0:T(8,128)(2,1)S(1)}, u32[]{:S(2)}, u32[]{:S(2)}) collective-permute-start(bf16[512,1536]{1,0:T(8,128)(2,1)S(1)} %get-tuple-element.269.refs_0_.refs_2_), channel_id=1, source_target_pairs={{4,0},{8,12},{5,1},{9,13},{6,2},{10,14},{7,3},{11,15},{20,16},{24,... | collective-permute-start | bytes 4718600 | tf_op jit(solution)/shard_map/ppermute | solution.py:933
  594.3 34.9 %collective-permute-start.65 = (bf16[512,2048]{1,0:T(8,128)(2,1)S(1)}, bf16[512,2048]{1,0:T(8,128)(2,1)S(1)}, u32[]{:S(2)}, u32[]{:S(2)}) collective-permute-start(bf16[512,2048]{1,0:T(8,128)(2,1)S(1)} %get-tuple-element.270.refs_0_.refs_6_), channel_id=1, source_target_pairs={{0,4},{12,8},{1,5},{13,9},{2,6},{14,10},{3,7},{15,11}} | collective-permute-start | bytes 6291464 | tf_op jit(solution)/shard_map/ppermute | solution.py:938
  599.1 30.2 %collective-permute-start.66 = (bf16[512,2048]{1,0:T(8,128)(2,1)S(1)}, bf16[512,2048]{1,0:T(8,128)(2,1)S(1)}, u32[]{:S(2)}, u32[]{:S(2)}) collective-permute-start(bf16[512,2048]{1,0:T(8,128)(2,1)S(1)} %get-tuple-element.271.refs_2_), channel_id=1, source_target_pairs={{4,8},{8,4},{5,9},{9,5},{6,10},{10,6},{7,11},{11,7}} | collective-permute-start | bytes 6291464 | tf_op jit(solution)/shard_map/ppermute | solution.py:938
  599.9 29.4 %collective-permute-start.67 = (bf16[512,1536]{1,0:T(8,128)(2,1)S(1)}, bf16[512,1536]{1,0:T(8,128)(2,1)S(1)}, u32[]{:S(2)}, u32[]{:S(2)}) collective-permute-start(bf16[512,1536]{1,0:T(8,128)(2,1)S(1)} %get-tuple-element.272.refs_1_.refs_3_), channel_id=1, source_target_pairs={{4,0},{8,12},{5,1},{9,13},{6,2},{10,14},{7,3},{11,15},{20,16},{24,... | collective-permute-start | bytes 4718600 | tf_op jit(solution)/shard_map/ppermute | solution.py:933
  601.2 28.1 %collective-permute-start.68 = (f32[2,3,256]{2,1,0:T(4,128)S(1)}, f32[2,3,256]{2,1,0:T(4,128)S(1)}, u32[]{:S(2)}, u32[]{:S(2)}) collective-permute-start(f32[2,3,256]{2,1,0:T(4,128)S(1)} %add.170), channel_id=1, source_target_pairs={{4,0},{8,12},{5,1},{9,13},{6,2},{10,14},{7,3},{11,15},{20,16},{24,... | collective-permute-start | bytes 18440 | tf_op jit(solution)/shard_map/ppermute | solution.py:933
  632.8 31.4 %collective-permute-start.70 = (bf16[512,2048]{1,0:T(8,128)(2,1)S(1)}, bf16[512,2048]{1,0:T(8,128)(2,1)S(1)}, u32[]{:S(2)}, u32[]{:S(2)}) collective-permute-start(bf16[512,2048]{1,0:T(8,128)(2,1)S(1)} %get-tuple-element.273.refs_0_), channel_id=1, source_target_pairs={{4,0},{8,12},{5,1},{9,13},{6,2},{10,14},{7,3},{11,15}} | collective-permute-start | bytes 6291464 | tf_op jit(solution)/shard_map/ppermute | solution.py:938
  665.8 27.9 %collective-permute-start.71 = (bf16[512,2048]{1,0:T(8,128)(2,1)S(1)}, bf16[512,2048]{1,0:T(8,128)(2,1)S(1)}, u32[]{:S(2)}, u32[]{:S(2)}) collective-permute-start(bf16[512,2048]{1,0:T(8,128)(2,1)S(1)} %shard_map.210.refs_8_.refs_1_), channel_id=1, source_target_pairs={{4,0},{8,12},{5,1},{9,13},{6,2},{10,14},{7,3},{11,15}} | collective-permute-start | bytes 6291464 | tf_op jit(solution)/shard_map/ppermute | solution.py:938
  (179 other events, 1739.3 us)

commit v2 on v1

--- a/solution.py
+++ b/solution.py
@@ -1171,9 +1171,9 @@
     ffn_step(0)
     (gd_up,) = reduced([], [(d2, du, False)])
     ffn_step(1)
-    dec_step(0, [])
+    dec_step(0, gd_down[0])
     enc_step(0)
-    dec_step(1, gd_down[0])
+    dec_step(1, gd_down[0] + gd_up[0])
     ge_cross, ge_down, gd_cross, gd_qkv, gd_out = reduced(
         [(memory, dkv, False), (pick(keep_fe, 0), dfe, True)],
         [
@@ -1226,18 +1226,20 @@
             lax.dynamic_index_in_dim(parts, 1 - bit_on, 2, keepdims=False), bit
         )
 
-    for bit in reversed(range(bits + 1)):
+    hops = reversed(range(bits + 1))
+    norms = norms_step(norms, next(hops))
+    input_grad = scatter_micro([jnp.where(is0, e, d.astype(BF)) for e, d in zip(grad_e, grad_d)])
+    advance(p1b, gd_up, p1a, deps=[*arrived(gd_down), norms])
+    for bit in hops:
         norms = norms_step(norms, bit)
-    input_grad = scatter_micro([jnp.where(is0, e, d.astype(BF)) for e, d in zip(grad_e, grad_d)])
     norms_sum = Reduction(None, norms, None)
-    advance(p1b, gd_up, p1a, deps=[*arrived(gd_down), input_grad, norms])
+    advance(p2a, p1b, p1a, deps=[*arrived(gd_up), norms, input_grad])
     norms_sum.forward(norms)
-    advance(p2a, p1b, p1a, deps=[*arrived(gd_up), norms_sum.got])
-    norms_sum.forward(norms_sum.value + norms_sum.got)
     advance(p2b, p2a, p1b, deps=[*arrived(p1a), norms_sum.got])
     norms_sum.forward(norms_sum.value + norms_sum.got)
     advance(p2b, p2a, deps=[*arrived(p1b), norms_sum.got])
-    advance(p2b, deps=arrived(p2a))
+    norms_sum.forward(norms_sum.value + norms_sum.got)
+    advance(p2b, deps=[*arrived(p2a), norms_sum.got])
     everything = (
         ge_cross, ge_down, gd_cross, gd_qkv, gd_out, ge_up, ge_qkv, ge_out, gd_down, gd_up
     )

time: 727 us -> 712 us (0.979)
  local copies, waits for them, and re-layouts: 55.3 us -> 43 us
  starting transfers between devices: 134 us -> 122 us
    ppermute x15, waiting for transfers between devices: 51.1 us -> 19.6 us  [z_on(): lax.ppermute(v, ('section', 'dp'), [(core * zs + a, core * zs + b) for a,...]
    ppermute x4, waiting for transfers between devices: 98.1 us -> 126 us  [to_core(): return lax.ppermute(v, 'section', [(1 - core, core)])]
    ppermute x12, waiting for transfers between devices: 90.4 us -> 105 us  [z_on(): return lax.ppermute(v, 'dp', pairs)]
    unnamed x346 -> x301, local copies, waits for them, and re-layouts: 45.4 us -> 31.4 us
    ppermute x14, waiting for transfers between devices: 31.5 us -> 21.8 us  [flip(): return lax.ppermute(v, 'tensor', [(i, i ^ 1 << bit) for i in range(n)])]
    pallas_call x28, Pallas kernels: 162 us -> 172 us  [sectioned(): pl.pallas_call(kernel, out_shape=tuple((pltpu.HBM(a.shape, a.dtype) if is...]
    ppermute x27, starting transfers between devices: 58.4 us -> 49.4 us  [flip(): lax.ppermute(v, ('section', 'tensor'), [(core * n + i, core * n + (i ^ 1...]
  transfers between devices with their start and end apart: 72 -> 72, of which waited for: 17 -> 20; matrix products, arithmetic and copies ran while one was open for 4% -> 5% of each run, Pallas kernels for 28% -> 30%
where the time goes in v2:
time: 712 us; the launch traced here: 702 us
  waiting for transfers between devices  282 us (40%)
  Pallas kernels  225 us (32%)
  starting transfers between devices  122 us (17%)
  local copies, waits for them, and re-layouts  43 us (6%)
  other arithmetic  25.1 us (4%)
    pallas_call x28, Pallas kernels, sectioned(): pl.pallas_call(kernel, out_shape=tuple((pltpu.HBM(a.shape, a.dtype) if is...  172 us
    ppermute x4, waiting for transfers between devices, to_core(): return lax.ppermute(v, 'section', [(1 - core, core)])  126 us
    ppermute x12, waiting for transfers between devices, z_on(): return lax.ppermute(v, 'dp', pairs)  105 us
    ppermute x27, starting transfers between devices, flip(): lax.ppermute(v, ('section', 'tensor'), [(core * n + i, core * n + (i ^ 1...  49.4 us
    unnamed x301, local copies, waits for them, and re-layouts  31.4 us
    ppermute x15, starting transfers between devices, z_on(): lax.ppermute(v, ('section', 'dp'), [(core * zs + a, core * zs + b) for a,...  30.2 us
    pallas_call x7, Pallas kernels, add_pairs(): pl.pallas_call(kernel, out_shape=tuple((spec(a.shape) for _, a, _ in pair...  25.8 us
    ppermute x12, starting transfers between devices, z_on(): return lax.ppermute(v, 'dp', pairs)  22.7 us
  transfers between devices with their start and end apart: 72, of which 20 were waited for; matrix products, arithmetic and copies ran while one was open for 5% of the time, Pallas kernels for 30%

profile of v2, /device:TPU:0, one launch (start us, length us, event | category | flops | bytes accessed | tf_op | source)
XLA Modules:
  0.0 701.7 jit_solution(6046453961620147469)
XLA Ops:
  1.8 3.0 collective-permute-start
  5.4 2.8 shard_map.169
  14.2 3.3 collective-permute-done.refs_1_
  22.7 2.9 shard_map.173
  25.6 4.1 collective-permute-start.8
  29.7 2.9 shard_map.174
  32.6 6.6 collective-permute-done.4.refs_9_
  39.2 3.6 collective-permute-start.10
  49.4 3.5 shard_map.171.refs_11_
  54.5 10.9 %collective-permute-done.3.refs_7_.refs_16_ = bf16[512,768]{1,0:T(8,128)(2,1)S(1)} collective-permute-done((bf16[512,768]{1,0:T(8,128)(2,1)S(1)}, bf16[512,768]{1,0:T(8,128)(2,1)S(1)}, u32[]{:S(2)}, u32[]{:S(2)}) %collective-permute-start.3) | collective-permute-done | bytes 786464 | tf_op jit(solution)/shard_map/ppermute | solution.py:933
  65.4 13.5 %shard_map.172 = (bf16[512,1024]{1,0:T(8,128)(2,1)S(1)}, bf16[512,1024]{1,0:T(8,128)(2,1)}, f32[512,128]{1,0:T(8,128)}, bf16[512,1536]{1,0:T(8,128)(2,1)}, bf16[...) custom-call(s32[3]{0:T(128)S(1)} %copy-done.106, ...), custom_call_target="tpu_custom_call" | custom-call | flops 1024 | bytes 1024 | tf_op jit(solution)/shard_map/pallas_call | solution.py:183
  80.5 3.5 collective-permute-start.9
  86.4 13.9 %shard_map.175 = (bf16[512,1024]{1,0:T(8,128)(2,1)S(1)}, bf16[512,1024]{1,0:T(8,128)(2,1)}, f32[512,128]{1,0:T(8,128)}, bf16[512,1536]{1,0:T(8,128)(2,1)}, bf16[...) custom-call(s32[3]{0:T(128)S(1)} %copy-done.106, s32[512,1]{1,0:T(8,128)S(1)} %copy-done.68, ...), custom_call_target="tpu_custom_call" | custom-call | flops 1024 | bytes 1024 | tf_op jit(solution)/shard_map/pallas_call | solution.py:183
  111.5 11.6 %shard_map.176 = (bf16[512,1024]{1,0:T(8,128)(2,1)S(1)}, bf16[512,1024]{1,0:T(8,128)(2,1)}, f32[512,128]{1,0:T(8,128)}, bf16[512,2048]{1,0:T(8,128)(2,1)}, bf16[...) custom-call(s32[3]{0:T(128)S(1)} %copy-done.107, f32[1,1024]{1,0:T(1,128)S(1)} %get-tuple-element.337.refs_0_.refs_2_, ...), custom_call_target="tpu_custom_call" | custom-call | flops 1024 | bytes 1024 | tf_op jit(solution)/shard_map/pallas_call | solution.py:183
  123.1 2.6 collective-permute-start.12
  125.8 11.1 %shard_map.178 = (bf16[512,1024]{1,0:T(8,128)(2,1)S(1)}, bf16[512,1024]{1,0:T(8,128)(2,1)}, f32[512,128]{1,0:T(8,128)}, bf16[512,2048]{1,0:T(8,128)(2,1)}, bf16[...) custom-call(s32[3]{0:T(128)S(1)} %copy-done.107, f32[1,1024]{1,0:T(1,128)S(1)} %get-tuple-element.337.refs_0_.refs_2_, ...), custom_call_target="tpu_custom_call" | custom-call | flops 1024 | bytes 1024 | tf_op jit(solution)/shard_map/pallas_call | solution.py:183
  136.8 3.2 collective-permute-start.17
  141.8 7.6 %collective-permute-done.14.refs_7_.refs_6_.refs_10_.refs_3_ = bf16[512,512]{1,0:T(8,128)(2,1)S(1)} collective-permute-done((bf16[512,512]{1,0:T(8,128)(2,1)S(1)}, bf16[512,512]{1,0:T(8,128)(2,1)S(1)}, u32[]{:S(2)}, u32[]{:S(2)}) %collective-permute-start.14) | collective-permute-done | bytes 524320 | tf_op jit(solution)/shard_map/ppermute | solution.py:933
  150.1 3.9 shard_map.180
  156.1 3.8 shard_map.182
  180.8 4.7 shard_map.187
  189.7 4.3 shard_map.190
  195.5 9.1 %shard_map.199 = (bf16[1024,1024]{1,0:T(8,128)(2,1)S(1)}, bf16[1024,1024]{1,0:T(8,128)(2,1)S(1)}) custom-call(s32[3]{0:T(128)S(1)} %copy-done.107, bf16[512,1024]{1,0:T(8,128)(2,1)} %copy-done.50, bf16[512,1024]{1,0:T(8,128)(2,1)} %copy-done.75, bf16[512,2048]{1,0:T(8,128)(2,1)} %get-tuple-element.226.refs_2_, bf16[512,2048]{1,0:T(8,128)(2,1)} %get-tuple-element.227.refs_3_), custom_call_target="tpu_custom_call" | custom-call | flops 1024 | bytes 1024 | tf_op jit(solution)/shard_map/pallas_call | solution.py:183
  208.1 5.0 shard_map.196
  216.7 125.6 %collective-permute-done.37.refs_0_.refs_3_ = bf16[512,1024]{1,0:T(8,128)(2,1)S(1)} collective-permute-done((bf16[512,1024]{1,0:T(8,128)(2,1)S(1)}, bf16[512,1024]{1,0:T(8,128)(2,1)S(1)}, u32[]{:S(2)}, u32[]{:S(2)}) %collective-permute-start.37) | collective-permute-done | bytes 1048608 | tf_op jit(solution)/shard_map/ppermute | solution.py:920
  342.3 3.3 shard_map.197.refs_1_
  345.6 2.8 collective-permute-start.38
  357.7 3.6 shard_map.191.refs_1_
  361.3 3.0 collective-permute-start.30
  364.6 2.7 collective-permute-done.38.refs_2_
  367.3 9.5 %shard_map.198 = (bf16[512,1024]{1,0:T(8,128)(2,1)S(1)}, f32[2,8,1024]{2,1,0:T(8,128)}, bf16[512,2048]{1,0:T(8,128)(2,1)}, bf16[512,1024]{1,0:T(8,128)(2,1)S(1)}) custom-call(s32[3]{0:T(128)S(1)} %copy-done.107, f32[1,1024]{1,0:T(1,128)S(1)} %get-tuple-element.336.refs_0_, bf16[512,1024]{1,0:T(8,128)(2,1)} %shard_map.197.refs_1_, ...), custom_call_target="tpu_custom_call" | custom-call | flops 1024 | bytes 1024 | tf_op jit(solution)/shard_map/pallas_call | solution.py:183
  376.8 2.9 collective-permute-start.39
  380.5 9.4 %shard_map.192 = (bf16[512,1024]{1,0:T(8,128)(2,1)S(1)}, f32[2,8,1024]{2,1,0:T(8,128)}, bf16[512,2048]{1,0:T(8,128)(2,1)}, bf16[512,1024]{1,0:T(8,128)(2,1)}) custom-call(s32[3]{0:T(128)S(1)} %copy-done.107, f32[1,1024]{1,0:T(1,128)S(1)} %get-tuple-element.336.refs_0_, bf16[512,1024]{1,0:T(8,128)(2,1)S(1)} %shard_map.191.refs_1_, ...), custom_call_target="tpu_custom_call" | custom-call | flops 1024 | bytes 1024 | tf_op jit(solution)/shard_map/pallas_call | solution.py:183
  389.9 3.0 collective-permute-start.31
  394.2 11.3 %shard_map.201 = (bf16[512,1536]{1,0:T(8,128)(2,1)S(1)}, bf16[512,1536]{1,0:T(8,128)(2,1)S(1)}, bf16[512,1536]{1,0:T(8,128)(2,1)}, bf16[512,1536]{1,0:T(8,128)(2,1)S(1)}) custom-call(s32[3]{0:T(128)S(1)} %copy-done.107, bf16[512,1024]{1,0:T(8,128)(2,1)} %copy-done.51, bf16[512,1024]{1,0:T(8,128)(2,1)} %copy-done.52, ...), custom_call_target="tpu_custom_call" | custom-call | flops 1024 | bytes 1024 | tf_op jit(solution)/shard_map/pallas_call | solution.py:183
  405.6 16.2 %shard_map.202 = (bf16[512,1024]{1,0:T(8,128)(2,1)S(1)}, f32[2,8,1024]{2,1,0:T(8,128)}, bf16[512,1536]{1,0:T(8,128)(2,1)}, bf16[512,1024]{1,0:T(8,128)(2,1)S(1)}) custom-call(s32[3]{0:T(128)S(1)} %copy-done.107, s32[1,512]{1,0:T(1,128)S(1)} %get-tuple-element.351.refs_1_.refs_0_, s32[512,1]{1,0:T(8,128)S(1)} %copy-done.70, ...), custom_call_target="tpu_custom_call" | custom-call | flops 1024 | bytes 1024 | tf_op jit(solution)/shard_map/pallas_call | solution.py:183
  433.3 16.1 %shard_map.193 = (bf16[512,1024]{1,0:T(8,128)(2,1)S(1)}, f32[2,8,1024]{2,1,0:T(8,128)}, bf16[512,1536]{1,0:T(8,128)(2,1)}, bf16[512,1024]{1,0:T(8,128)(2,1)S(1)}) custom-call(s32[3]{0:T(128)S(1)} %copy-done.107, s32[1,512]{1,0:T(1,128)S(1)} %get-tuple-element.352.refs_1_.refs_0_, s32[512,1]{1,0:T(8,128)S(1)} %copy-done.67, ...), custom_call_target="tpu_custom_call" | custom-call | flops 1024 | bytes 1024 | tf_op jit(solution)/shard_map/pallas_call | solution.py:183
  450.3 2.9 collective-permute-start.32
  454.1 3.0 collective-permute-start.43
  458.2 3.6 collective-permute-done.32
  464.0 3.4 collective-permute-done.43
  469.1 4.1 fusion.9
  473.3 13.8 %shard_map.204 = (bf16[512,2048]{1,0:T(8,128)(2,1)S(1)}, bf16[512,2048]{1,0:T(8,128)(2,1)S(1)}, bf16[512,2048]{1,0:T(8,128)(2,1)}, bf16[512,2048]{1,0:T(8,128)(2,1)S(1)}) custom-call(s32[3]{0:T(128)S(1)} %copy-done.107, bf16[512,1024]{1,0:T(8,128)(2,1)} %copy-done.54, bf16[512,1024]{1,0:T(8,128)(2,1)} %copy-done.45, ...), custom_call_target="tpu_custom_call" | custom-call | flops 1024 | bytes 1024 | tf_op jit(solution)/shard_map/pallas_call | solution.py:183
  487.9 4.7 shard_map.205
  492.7 3.8 collective-permute-start.53
  500.4 2.5 collective-permute-start.49
  504.9 10.9 %collective-permute-done.53.refs_3_ = bf16[512,1536]{1,0:T(8,128)(2,1)S(1)} collective-permute-done((bf16[512,1536]{1,0:T(8,128)(2,1)S(1)}, bf16[512,1536]{1,0:T(8,128)(2,1)S(1)}, u32[]{:S(2)}, u32[]{:S(2)}) %collective-permute-start.53) | collective-permute-done | bytes 1572896 | tf_op jit(solution)/shard_map/ppermute | solution.py:933
  515.9 5.1 shard_map.206
  521.0 4.5 collective-permute-start.56
  531.4 9.2 %collective-permute-done.45 = bf16[2,128,1024]{2,1,0:T(8,128)(2,1)S(1)} collective-permute-done((bf16[2,128,1024]{2,1,0:T(8,128)(2,1)S(1)}, bf16[2,128,1024]{2,1,0:T(8,128)(2,1)S(1)}, u32[]{:S(2)}, u32[]{:S(2)}) %collective-permute-start.45) | collective-permute-done | bytes 524320 | tf_op jit(solution)/shard_map/ppermute | solution.py:924
  544.0 4.1 collective-permute-done.56.refs_3_
  548.1 5.4 shard_map.207
  553.6 7.0 collective-permute-start.60
  562.6 4.6 collective-permute-start.63
  567.3 16.8 %collective-permute-done.63.refs_7_ = f32[2,3,256]{2,1,0:T(4,128)S(1)} collective-permute-done((f32[2,3,256]{2,1,0:T(4,128)S(1)}, f32[2,3,256]{2,1,0:T(4,128)S(1)}, u32[]{:S(2)}, u32[]{:S(2)}) %collective-permute-start.63) | collective-permute-done | bytes 6176 | tf_op jit(solution)/shard_map/ppermute | solution.py:933
  584.1 5.5 collective-permute-done.62.refs_6_.refs_4_.refs_3_
  589.6 5.4 shard_map.208
  599.4 20.4 %collective-permute-done.66.refs_4_.refs_5_.refs_7_ = bf16[512,1536]{1,0:T(8,128)(2,1)S(1)} collective-permute-done((bf16[512,1536]{1,0:T(8,128)(2,1)S(1)}, bf16[512,1536]{1,0:T(8,128)(2,1)S(1)}, u32[]{:S(2)}, u32[]{:S(2)}) %collective-permute-start.66) | collective-permute-done | bytes 1572896 | tf_op jit(solution)/shard_map/ppermute | solution.py:933
  620.0 2.7 shard_map.209
  626.0 29.2 %collective-permute-done.70.refs_3_ = f32[2,3,256]{2,1,0:T(4,128)S(1)} collective-permute-done((f32[2,3,256]{2,1,0:T(4,128)S(1)}, f32[2,3,256]{2,1,0:T(4,128)S(1)}, u32[]{:S(2)}, u32[]{:S(2)}) %collective-permute-start.70) | collective-permute-done | bytes 6176 | tf_op jit(solution)/shard_map/ppermute | solution.py:933
  663.4 2.9 shard_map.212.refs_8_
  666.3 18.7 %collective-permute-done.71.refs_5_.refs_4_ = bf16[512,2048]{1,0:T(8,128)(2,1)S(1)} collective-permute-done((bf16[512,2048]{1,0:T(8,128)(2,1)S(1)}, bf16[512,2048]{1,0:T(8,128)(2,1)S(1)}, u32[]{:S(2)}, u32[]{:S(2)}) %collective-permute-start.71) | collective-permute-done | bytes 2097184 | tf_op jit(solution)/shard_map/ppermute | solution.py:938
  688.0 2.6 shard_map.213.refs_6_
  698.5 2.9 shard_map.214
  (510 shorter events, 146.9 us)
Async XLA Ops:
  1.8 15.8 %collective-permute-start = (bf16[2,128,1024]{2,1,0:T(8,128)(2,1)S(1)}, bf16[2,128,1024]{2,1,0:T(8,128)(2,1)S(1)}, u32[]{:S(2)}, u32[]{:S(2)}) collective-permute-start(bf16[2,128,1024]{2,1,0:T(8,128)(2,1)S(1)} %dynamic-slice_bitcast_fusion.5), channel_id=1, source_target_pairs={{0,2},{1,3},{2,0},{3,1},{4,6},{5,7},{6,4},{7,5},{8,10},{9,11},{10,... | collective-permute-start | bytes 1572872 | tf_op jit(solution)/shard_map/ppermute | solution.py:924
  8.3 34.6 %collective-permute-start.2 = (bf16[512,768]{1,0:T(8,128)(2,1)}, bf16[512,768]{1,0:T(8,128)(2,1)S(1)}, u32[]{:S(2)}, u32[]{:S(2)}) collective-permute-start(bf16[512,768]{1,0:T(8,128)(2,1)} %shard_map.169), channel_id=1, source_target_pairs={{0,2},{1,3},{2,0},{3,1},{4,6},{5,7},{6,4},{7,5},{8,10},{9,11},{10,... | collective-permute-start | bytes 2359304 | tf_op jit(solution)/shard_map/ppermute | solution.py:924
  10.7 28.5 %collective-permute-start.4 = (bf16[128,1024]{1,0:T(8,128)(2,1)}, bf16[128,1024]{1,0:T(8,128)(2,1)S(1)}, u32[]{:S(2)}, u32[]{:S(2)}) collective-permute-start(bf16[128,1024]{1,0:T(8,128)(2,1)} %shard_map.170), channel_id=1, source_target_pairs={{0,2},{1,3},{2,0},{3,1},{4,6},{5,7},{6,4},{7,5},{8,10},{9,11},{10,... | collective-permute-start | bytes 786440 | tf_op jit(solution)/shard_map/ppermute | solution.py:924
  19.8 24.7 %collective-permute-start.1 = (bf16[1,2,1,128,1024]{4,3,1,2,0:T(8,128)(2,1)}, bf16[1,2,1,128,1024]{4,3,1,2,0:T(8,128)(2,1)}, u32[]{:S(2)}, u32[]{:S(2)}) collective-permute-start(bf16[1,2,1,128,1024]{4,3,1,2,0:T(8,128)(2,1)} %maximum_bitcast_fusion.1), channel_id=1, source_target_pairs={{0,1},{1,0},{2,3},{3,2},{4,5},{5,4},{6,7},{7,6},{8,9},{9,8},{10,11... | collective-permute-start | bytes 1572872 | tf_op jit(solution)/shard_map/ppermute | solution.py:924
  22.7 24.4 %collective-permute-start.6 = (bf16[1,2,1,128,1024]{4,3,1,2,0:T(8,128)(2,1)}, bf16[1,2,1,128,1024]{4,3,1,2,0:T(8,128)(2,1)}, u32[]{:S(2)}, u32[]{:S(2)}) collective-permute-start(bf16[1,2,1,128,1024]{4,3,1,2,0:T(8,128)(2,1)} %maximum_bitcast_fusion.2), channel_id=1, source_target_pairs={{0,1},{1,0},{2,3},{3,2},{4,5},{5,4},{6,7},{7,6},{8,9},{9,8},{10,11... | collective-permute-start | bytes 1572872 | tf_op jit(solution)/shard_map/ppermute | solution.py:924
  25.6 54.8 %collective-permute-start.8 = (bf16[512,1024]{1,0:T(8,128)(2,1)}, bf16[512,1024]{1,0:T(8,128)(2,1)}, u32[]{:S(2)}, u32[]{:S(2)}) collective-permute-start(bf16[512,1024]{1,0:T(8,128)(2,1)} %shard_map.173), channel_id=1, source_target_pairs={{0,2},{1,3},{2,0},{3,1},{4,6},{5,7},{6,4},{7,5},{8,10},{9,11},{10,... | collective-permute-start | bytes 3145736 | tf_op jit(solution)/shard_map/ppermute | solution.py:925
  39.2 44.8 %collective-permute-start.10 = (bf16[512,1024]{1,0:T(8,128)(2,1)}, bf16[512,1024]{1,0:T(8,128)(2,1)}, u32[]{:S(2)}, u32[]{:S(2)}) collective-permute-start(bf16[512,1024]{1,0:T(8,128)(2,1)} %shard_map.174), channel_id=1, source_target_pairs={{0,2},{1,3},{2,0},{3,1},{4,6},{5,7},{6,4},{7,5},{8,10},{9,11},{10,... | collective-permute-start | bytes 3145736 | tf_op jit(solution)/shard_map/ppermute | solution.py:925
  42.9 11.6 %collective-permute-start.5 = (bf16[128,1024]{1,0:T(8,128)(2,1)S(1)}, bf16[128,1024]{1,0:T(8,128)(2,1)S(1)}, u32[]{:S(2)}, u32[]{:S(2)}) collective-permute-start(bf16[128,1024]{1,0:T(8,128)(2,1)S(1)} %collective-permute-done.4.refs_9_), channel_id=1, source_target_pairs={{0,4},{4,0},{8,12},{12,8},{1,5},{5,1},{9,13},{13,9},{2,6},{6,2},{1... | collective-permute-start | bytes 786440 | tf_op jit(solution)/shard_map/ppermute | solution.py:933
  44.6 20.8 %collective-permute-start.3 = (bf16[512,768]{1,0:T(8,128)(2,1)S(1)}, bf16[512,768]{1,0:T(8,128)(2,1)S(1)}, u32[]{:S(2)}, u32[]{:S(2)}) collective-permute-start(bf16[512,768]{1,0:T(8,128)(2,1)S(1)} %collective-permute-done.2.refs_6_.refs_15_), channel_id=1, source_target_pairs={{0,4},{4,0},{8,12},{12,8},{1,5},{5,1},{9,13},{13,9},{2,6},{6,2},{1... | collective-permute-start | bytes 2359304 | tf_op jit(solution)/shard_map/ppermute | solution.py:933
  79.0 27.5 %collective-permute-start.7 = (bf16[512,1024]{1,0:T(8,128)(2,1)}, bf16[512,1024]{1,0:T(8,128)(2,1)}, u32[]{:S(2)}, u32[]{:S(2)}) collective-permute-start(bf16[512,1024]{1,0:T(8,128)(2,1)} %get-tuple-element.143.refs_3_), channel_id=1, source_target_pairs={{0,1},{1,0},{2,3},{3,2},{4,5},{5,4},{6,7},{7,6},{8,9},{9,8},{10,11... | collective-permute-start | bytes 3145736 | tf_op jit(solution)/shard_map/ppermute | solution.py:924
  80.5 27.6 %collective-permute-start.9 = (bf16[512,1024]{1,0:T(8,128)(2,1)}, bf16[512,1024]{1,0:T(8,128)(2,1)}, u32[]{:S(2)}, u32[]{:S(2)}) collective-permute-start(bf16[512,1024]{1,0:T(8,128)(2,1)} %collective-permute-done.8.refs_6_.refs_7_), channel_id=1, source_target_pairs={{0,4},{4,0},{8,12},{12,8},{1,5},{5,1},{9,13},{13,9},{2,6},{6,2},{1... | collective-permute-start | bytes 3145736 | tf_op jit(solution)/shard_map/ppermute | solution.py:938
  84.0 24.7 %collective-permute-start.11 = (bf16[512,1024]{1,0:T(8,128)(2,1)}, bf16[512,1024]{1,0:T(8,128)(2,1)}, u32[]{:S(2)}, u32[]{:S(2)}) collective-permute-start(bf16[512,1024]{1,0:T(8,128)(2,1)} %collective-permute-done.10.refs_9_.refs_10_), channel_id=1, source_target_pairs={{0,4},{4,0},{8,12},{12,8},{1,5},{5,1},{9,13},{13,9},{2,6},{6,2},{1... | collective-permute-start | bytes 3145736 | tf_op jit(solution)/shard_map/ppermute | solution.py:938
  101.3 24.4 %collective-permute-start.15 = (bf16[512,1024]{1,0:T(8,128)(2,1)}, bf16[512,1024]{1,0:T(8,128)(2,1)}, u32[]{:S(2)}, u32[]{:S(2)}) collective-permute-start(bf16[512,1024]{1,0:T(8,128)(2,1)} %get-tuple-element.147.refs_3_), channel_id=1, source_target_pairs={{0,1},{1,0},{2,3},{3,2},{4,5},{5,4},{6,7},{7,6},{8,9},{9,8},{10,11... | collective-permute-start | bytes 3145736 | tf_op jit(solution)/shard_map/ppermute | solution.py:924
  101.9 59.4 %collective-permute-start.19 = (bf16[1024,1024]{1,0:T(8,128)(2,1)}, bf16[1024,1024]{1,0:T(8,128)(2,1)}, u32[]{:S(2)}, u32[]{:S(2)}) collective-permute-start(bf16[1024,1024]{1,0:T(8,128)(2,1)} %shard_map.171.refs_11_), channel_id=1, source_target_pairs={{16,18},{17,19},{18,16},{19,17},{20,22},{21,23},{22,20},{23,21},{2... | collective-permute-start | bytes 6291464 | tf_op jit(solution)/shard_map/ppermute | solution.py:925
  106.5 33.6 %collective-permute-start.13 = (bf16[512,512]{1,0:T(8,128)(2,1)}, bf16[512,512]{1,0:T(8,128)(2,1)S(1)}, u32[]{:S(2)}, u32[]{:S(2)}) collective-permute-start(bf16[512,512]{1,0:T(8,128)(2,1)} %shard_map.177), channel_id=1, source_target_pairs={{0,2},{1,3},{2,0},{3,1},{4,6},{5,7},{6,4},{7,5},{8,10},{9,11},{10,... | collective-permute-start | bytes 1572872 | tf_op jit(solution)/shard_map/ppermute | solution.py:924
  123.1 26.9 %collective-permute-start.12 = (bf16[512,1024]{1,0:T(8,128)(2,1)S(1)}, bf16[512,1024]{1,0:T(8,128)(2,1)S(1)}, u32[]{:S(2)}, u32[]{:S(2)}) collective-permute-start(bf16[512,1024]{1,0:T(8,128)(2,1)S(1)} %get-tuple-element.146.refs_3_), channel_id=1, source_target_pairs={{0,1},{1,0},{2,3},{3,2},{4,5},{5,4},{6,7},{7,6},{8,9},{9,8},{10,11... | collective-permute-start | bytes 3145736 | tf_op jit(solution)/shard_map/ppermute | solution.py:925
  136.8 19.3 %collective-permute-start.17 = (bf16[512,1024]{1,0:T(8,128)(2,1)S(1)}, bf16[512,1024]{1,0:T(8,128)(2,1)S(1)}, u32[]{:S(2)}, u32[]{:S(2)}) collective-permute-start(bf16[512,1024]{1,0:T(8,128)(2,1)S(1)} %get-tuple-element.153.refs_3_), channel_id=1, source_target_pairs={{0,1},{1,0},{2,3},{3,2},{4,5},{5,4},{6,7},{7,6},{8,9},{9,8},{10,11... | collective-permute-start | bytes 3145736 | tf_op jit(solution)/shard_map/ppermute | solution.py:925
  140.1 9.2 %collective-permute-start.14 = (bf16[512,512]{1,0:T(8,128)(2,1)S(1)}, bf16[512,512]{1,0:T(8,128)(2,1)S(1)}, u32[]{:S(2)}, u32[]{:S(2)}) collective-permute-start(bf16[512,512]{1,0:T(8,128)(2,1)S(1)} %collective-permute-done.13.refs_6_.refs_5_.refs_9_.refs_2_), channel_id=1, source_target_pairs={{0,4},{4,0},{8,12},{12,8},{1,5},{5,1},{9,13},{13,9},{2,6},{6,2},{1... | collective-permute-start | bytes 1572872 | tf_op jit(solution)/shard_map/ppermute | solution.py:933
  154.0 10.2 %collective-permute-start.16 = (bf16[512,1024]{1,0:T(8,128)(2,1)S(1)}, bf16[512,1024]{1,0:T(8,128)(2,1)S(1)}, u32[]{:S(2)}, u32[]{:S(2)}) collective-permute-start(bf16[512,1024]{1,0:T(8,128)(2,1)S(1)} %get-tuple-element.152), channel_id=1, source_target_pairs={{0,16},{1,17},{2,18},{3,19},{4,20},{5,21},{6,22},{7,23},{8,24},{9,... | collective-permute-start | bytes 3145736 | tf_op jit(solution)/shard_map/ppermute | solution.py:920
  161.3 12.4 %collective-permute-start.20 = (bf16[1024,1024]{1,0:T(8,128)(2,1)}, bf16[1024,1024]{1,0:T(8,128)(2,1)}, u32[]{:S(2)}, u32[]{:S(2)}) collective-permute-start(bf16[1024,1024]{1,0:T(8,128)(2,1)} %collective-permute-done.19.refs_6_.refs_9_.refs_8_.refs_11_), channel_id=1, source_target_pairs={{16,20},{20,16},{24,28},{28,24},{17,21},{21,17},{25,29},{29,25},{1... | collective-permute-start | bytes 6291464 | tf_op jit(solution)/shard_map/ppermute | solution.py:938
  170.5 6.3 collective-permute-start.25
  172.9 5.5 collective-permute-start.24
  177.6 8.6 %collective-permute-start.26 = (bf16[512,1024]{1,0:T(8,128)(2,1)S(1)}, bf16[512,1024]{1,0:T(8,128)(2,1)S(1)}, u32[]{:S(2)}, u32[]{:S(2)}) collective-permute-start(bf16[512,1024]{1,0:T(8,128)(2,1)S(1)} %get-tuple-element.167.refs_3_), channel_id=1, source_target_pairs={{16,17},{17,16},{18,19},{19,18},{20,21},{21,20},{22,23},{23,22},{2... | collective-permute-start | bytes 3145736 | tf_op jit(solution)/shard_map/ppermute | solution.py:925
  188.7 16.7 %collective-permute-start.34 = (bf16[1024,1024]{1,0:T(8,128)(2,1)S(1)}, bf16[1024,1024]{1,0:T(8,128)(2,1)S(1)}, u32[]{:S(2)}, u32[]{:S(2)}) collective-permute-start(bf16[1024,1024]{1,0:T(8,128)(2,1)S(1)} %get-tuple-element.198), channel_id=1, source_target_pairs={{16,18},{17,19},{18,16},{19,17},{20,22},{21,23},{22,20},{23,21},{2... | collective-permute-start | bytes 6291464 | tf_op jit(solution)/shard_map/ppermute | solution.py:925
  194.0 11.4 %collective-permute-start.33 = (bf16[512,1024]{1,0:T(8,128)(2,1)S(1)}, bf16[512,1024]{1,0:T(8,128)(2,1)S(1)}, u32[]{:S(2)}, u32[]{:S(2)}) collective-permute-start(bf16[512,1024]{1,0:T(8,128)(2,1)S(1)} %get-tuple-element.191.refs_4_), channel_id=1, source_target_pairs={{16,17},{17,16},{18,19},{19,18},{20,21},{21,20},{22,23},{23,22},{2... | collective-permute-start | bytes 3145736 | tf_op jit(solution)/shard_map/ppermute | solution.py:925
  194.7 13.4 %collective-permute-start.36 = (bf16[512,1024]{1,0:T(8,128)(2,1)S(1)}, bf16[512,1024]{1,0:T(8,128)(2,1)S(1)}, u32[]{:S(2)}, u32[]{:S(2)}) collective-permute-start(bf16[512,1024]{1,0:T(8,128)(2,1)S(1)} %get-tuple-element.201.refs_4_), channel_id=1, source_target_pairs={{16,17},{17,16},{18,19},{19,18},{20,21},{21,20},{22,23},{23,22},{2... | collective-permute-start | bytes 3145736 | tf_op jit(solution)/shard_map/ppermute | solution.py:925
  204.6 143.8 %collective-permute-start.42 = (bf16[1024,1024]{1,0:T(8,128)(2,1)S(1)}, bf16[1024,1024]{1,0:T(8,128)(2,1)S(1)}, u32[]{:S(2)}, u32[]{:S(2)}) collective-permute-start(bf16[1024,1024]{1,0:T(8,128)(2,1)S(1)} %get-tuple-element.229), channel_id=1, source_target_pairs={{16,18},{17,19},{18,16},{19,17},{20,22},{21,23},{22,20},{23,21},{2... | collective-permute-start | bytes 6291464 | tf_op jit(solution)/shard_map/ppermute | solution.py:925
  207.3 141.1 %collective-permute-start.41 = (bf16[1024,1024]{1,0:T(8,128)(2,1)S(1)}, bf16[1024,1024]{1,0:T(8,128)(2,1)S(1)}, u32[]{:S(2)}, u32[]{:S(2)}) collective-permute-start(bf16[1024,1024]{1,0:T(8,128)(2,1)S(1)} %get-tuple-element.225.refs_17_), channel_id=1, source_target_pairs={{16,20},{28,24},{17,21},{29,25},{18,22},{30,26},{19,23},{31,27}} | collective-permute-start | bytes 6291464 | tf_op jit(solution)/shard_map/ppermute | solution.py:938
  213.2 129.1 %collective-permute-start.37 = (bf16[512,1024]{1,0:T(8,128)(2,1)S(1)}, bf16[512,1024]{1,0:T(8,128)(2,1)S(1)}, u32[]{:S(2)}, u32[]{:S(2)}) collective-permute-start(bf16[512,1024]{1,0:T(8,128)(2,1)S(1)} %get-tuple-element.205), channel_id=1, source_target_pairs={{16,0},{17,1},{18,2},{19,3},{20,4},{21,5},{22,6},{23,7},{24,8},{25... | collective-permute-start | bytes 3145736 | tf_op jit(solution)/shard_map/ppermute | solution.py:920
  214.5 133.9 %collective-permute-start.40 = (bf16[512,1024]{1,0:T(8,128)(2,1)S(1)}, bf16[512,1024]{1,0:T(8,128)(2,1)S(1)}, u32[]{:S(2)}, u32[]{:S(2)}) collective-permute-start(bf16[512,1024]{1,0:T(8,128)(2,1)S(1)} %get-tuple-element.222.refs_4_), channel_id=1, source_target_pairs={{16,17},{17,16},{18,19},{19,18},{20,21},{21,20},{22,23},{23,22},{2... | collective-permute-start | bytes 3145736 | tf_op jit(solution)/shard_map/ppermute | solution.py:925
  215.2 142.4 %collective-permute-start.29 = (bf16[512,1024]{1,0:T(8,128)(2,1)}, bf16[512,1024]{1,0:T(8,128)(2,1)}, u32[]{:S(2)}, u32[]{:S(2)}) collective-permute-start(bf16[512,1024]{1,0:T(8,128)(2,1)} %get-tuple-element.175), channel_id=1, source_target_pairs={{16,0},{17,1},{18,2},{19,3},{20,4},{21,5},{22,6},{23,7},{24,8},{25... | collective-permute-start | bytes 3145736 | tf_op jit(solution)/shard_map/ppermute | solution.py:920
  345.6 21.7 %collective-permute-start.38 = (bf16[512,1024]{1,0:T(8,128)(2,1)}, bf16[512,1024]{1,0:T(8,128)(2,1)}, u32[]{:S(2)}, u32[]{:S(2)}) collective-permute-start(bf16[512,1024]{1,0:T(8,128)(2,1)} %shard_map.197.refs_1_), channel_id=1, source_target_pairs={{0,1},{1,0},{2,3},{3,2},{4,5},{5,4},{6,7},{7,6},{8,9},{9,8},{10,11... | collective-permute-start | bytes 3145736 | tf_op jit(solution)/shard_map/ppermute | solution.py:925
  351.2 71.6 %collective-permute-start.46 = (bf16[1024,1024]{1,0:T(8,128)(2,1)}, bf16[1024,1024]{1,0:T(8,128)(2,1)}, u32[]{:S(2)}, u32[]{:S(2)}) collective-permute-start(bf16[1024,1024]{1,0:T(8,128)(2,1)} %get-tuple-element.242.refs_0_), channel_id=1, source_target_pairs={{16,20},{28,24},{17,21},{29,25},{18,22},{30,26},{19,23},{31,27}} | collective-permute-start | bytes 6291464 | tf_op jit(solution)/shard_map/ppermute | solution.py:938
  353.2 69.6 %collective-permute-start.47 = (bf16[1024,1024]{1,0:T(8,128)(2,1)}, bf16[1024,1024]{1,0:T(8,128)(2,1)}, u32[]{:S(2)}, u32[]{:S(2)}) collective-permute-start(bf16[1024,1024]{1,0:T(8,128)(2,1)} %get-tuple-element.243.refs_2_), channel_id=1, source_target_pairs={{20,24},{24,20},{21,25},{25,21},{22,26},{26,22},{23,27},{27,23}} | collective-permute-start | bytes 6291464 | tf_op jit(solution)/shard_map/ppermute | solution.py:938
  361.3 19.2 %collective-permute-start.30 = (bf16[512,1024]{1,0:T(8,128)(2,1)S(1)}, bf16[512,1024]{1,0:T(8,128)(2,1)S(1)}, u32[]{:S(2)}, u32[]{:S(2)}) collective-permute-start(bf16[512,1024]{1,0:T(8,128)(2,1)S(1)} %shard_map.191.refs_1_), channel_id=1, source_target_pairs={{0,1},{1,0},{2,3},{3,2},{4,5},{5,4},{6,7},{7,6},{8,9},{9,8},{10,11... | collective-permute-start | bytes 3145736 | tf_op jit(solution)/shard_map/ppermute | solution.py:925
  376.8 28.7 %collective-permute-start.39 = (bf16[512,1024]{1,0:T(8,128)(2,1)S(1)}, bf16[512,1024]{1,0:T(8,128)(2,1)S(1)}, u32[]{:S(2)}, u32[]{:S(2)}) collective-permute-start(bf16[512,1024]{1,0:T(8,128)(2,1)S(1)} %get-tuple-element.210.refs_4_), channel_id=1, source_target_pairs={{0,1},{1,0},{2,3},{3,2},{4,5},{5,4},{6,7},{7,6},{8,9},{9,8},{10,11... | collective-permute-start | bytes 3145736 | tf_op jit(solution)/shard_map/ppermute | solution.py:925
  379.9 13.1 %collective-permute-start.27 = (bf16[2,128,1024]{2,1,0:T(8,128)(2,1)S(1)}, bf16[2,128,1024]{2,1,0:T(8,128)(2,1)S(1)}, u32[]{:S(2)}, u32[]{:S(2)}) collective-permute-start(bf16[2,128,1024]{2,1,0:T(8,128)(2,1)S(1)} %fusion.24), channel_id=1, source_target_pairs={{0,2},{1,3},{2,0},{3,1},{4,6},{5,7},{6,4},{7,5},{8,10},{9,11},{10,... | collective-permute-start | bytes 1572872 | tf_op jit(solution)/shard_map/ppermute | solution.py:924
  389.9 39.2 %collective-permute-start.31 = (bf16[512,1024]{1,0:T(8,128)(2,1)}, bf16[512,1024]{1,0:T(8,128)(2,1)}, u32[]{:S(2)}, u32[]{:S(2)}) collective-permute-start(bf16[512,1024]{1,0:T(8,128)(2,1)} %get-tuple-element.180.refs_4_), channel_id=1, source_target_pairs={{0,1},{1,0},{2,3},{3,2},{4,5},{5,4},{6,7},{7,6},{8,9},{9,8},{10,11... | collective-permute-start | bytes 3145736 | tf_op jit(solution)/shard_map/ppermute | solution.py:925
  423.8 64.1 %collective-permute-start.52 = (bf16[1024,1024]{1,0:T(8,128)(2,1)}, bf16[1024,1024]{1,0:T(8,128)(2,1)}, u32[]{:S(2)}, u32[]{:S(2)}) collective-permute-start(bf16[1024,1024]{1,0:T(8,128)(2,1)} %get-tuple-element.244.refs_12_.refs_2_), channel_id=1, source_target_pairs={{20,24},{24,20},{21,25},{25,21},{22,26},{26,22},{23,27},{27,23}} | collective-permute-start | bytes 6291464 | tf_op jit(solution)/shard_map/ppermute | solution.py:938
  427.3 59.9 %collective-permute-start.51 = (bf16[512,1536]{1,0:T(8,128)(2,1)}, bf16[512,1536]{1,0:T(8,128)(2,1)}, u32[]{:S(2)}, u32[]{:S(2)}) collective-permute-start(bf16[512,1536]{1,0:T(8,128)(2,1)} %get-tuple-element.251), channel_id=1, source_target_pairs={{0,2},{1,3},{2,0},{3,1},{4,6},{5,7},{6,4},{7,5},{8,10},{9,11},{10,... | collective-permute-start | bytes 4718600 | tf_op jit(solution)/shard_map/ppermute | solution.py:924
  450.3 11.5 %collective-permute-start.32 = (bf16[2,1,128,1024]{3,2,0,1:T(8,128)(2,1)}, bf16[2,1,128,1024]{3,2,0,1:T(8,128)(2,1)}, u32[]{:S(2)}, u32[]{:S(2)}) collective-permute-start(bf16[2,1,128,1024]{3,2,0,1:T(8,128)(2,1)} %dynamic-slice_bitcast_fusion.3), channel_id=1, source_target_pairs={{0,1},{1,0},{2,3},{3,2},{4,5},{5,4},{6,7},{7,6},{8,9},{9,8},{10,11... | collective-permute-start | bytes 1572872 | tf_op jit(solution)/shard_map/ppermute | solution.py:925
  454.1 13.3 %collective-permute-start.43 = (bf16[2,1,128,1024]{3,2,0,1:T(8,128)(2,1)}, bf16[2,1,128,1024]{3,2,0,1:T(8,128)(2,1)}, u32[]{:S(2)}, u32[]{:S(2)}) collective-permute-start(bf16[2,1,128,1024]{3,2,0,1:T(8,128)(2,1)} %dynamic-slice_bitcast_fusion.1), channel_id=1, source_target_pairs={{0,1},{1,0},{2,3},{3,2},{4,5},{5,4},{6,7},{7,6},{8,9},{9,8},{10,11... | collective-permute-start | bytes 1572872 | tf_op jit(solution)/shard_map/ppermute | solution.py:925
  457.4 47.6 %collective-permute-start.54 = (bf16[1024,1024]{1,0:T(8,128)(2,1)}, bf16[1024,1024]{1,0:T(8,128)(2,1)S(1)}, u32[]{:S(2)}, u32[]{:S(2)}) collective-permute-start(bf16[1024,1024]{1,0:T(8,128)(2,1)} %get-tuple-element.253.refs_2_), channel_id=1, source_target_pairs={{20,16},{24,28},{21,17},{25,29},{22,18},{26,30},{23,19},{27,31}} | collective-permute-start | bytes 6291464 | tf_op jit(solution)/shard_map/ppermute | solution.py:938
  461.9 41.1 %collective-permute-start.50 = (bf16[512,1536]{1,0:T(8,128)(2,1)}, bf16[512,1536]{1,0:T(8,128)(2,1)}, u32[]{:S(2)}, u32[]{:S(2)}) collective-permute-start(bf16[512,1536]{1,0:T(8,128)(2,1)} %copy-done.122), channel_id=1, source_target_pairs={{0,2},{1,3},{2,0},{3,1},{4,6},{5,7},{6,4},{7,5},{8,10},{9,11},{10,... | collective-permute-start | bytes 4718600 | tf_op jit(solution)/shard_map/ppermute | solution.py:924
  467.5 29.1 %collective-permute-start.35 = (bf16[2,1,128,1024]{3,2,0,1:T(8,128)(2,1)}, bf16[2,1,128,1024]{3,2,0,1:T(8,128)(2,1)}, u32[]{:S(2)}, u32[]{:S(2)}) collective-permute-start(bf16[2,1,128,1024]{3,2,0,1:T(8,128)(2,1)} %dynamic-slice_bitcast_fusion.2), channel_id=1, source_target_pairs={{16,17},{17,16},{18,19},{19,18},{20,21},{21,20},{22,23},{23,22},{2... | collective-permute-start | bytes 1572872 | tf_op jit(solution)/shard_map/ppermute | solution.py:925
  487.2 39.1 %collective-permute-start.44 = (bf16[2,1,128,1024]{3,2,0,1:T(8,128)(2,1)S(1)}, bf16[2,1,128,1024]{3,2,0,1:T(8,128)(2,1)S(1)}, u32[]{:S(2)}, u32[]{:S(2)}) collective-permute-start(bf16[2,1,128,1024]{3,2,0,1:T(8,128)(2,1)S(1)} %copy-done.134), channel_id=1, source_target_pairs={{16,17},{17,16},{18,19},{19,18},{20,21},{21,20},{22,23},{23,22},{2... | collective-permute-start | bytes 1572872 | tf_op jit(solution)/shard_map/ppermute | solution.py:925
  492.7 23.2 %collective-permute-start.53 = (bf16[512,1536]{1,0:T(8,128)(2,1)S(1)}, bf16[512,1536]{1,0:T(8,128)(2,1)S(1)}, u32[]{:S(2)}, u32[]{:S(2)}) collective-permute-start(bf16[512,1536]{1,0:T(8,128)(2,1)S(1)} %get-tuple-element.252.refs_2_.refs_6_), channel_id=1, source_target_pairs={{0,4},{12,8},{1,5},{13,9},{2,6},{14,10},{3,7},{15,11},{16,20},{28,... | collective-permute-start | bytes 4718600 | tf_op jit(solution)/shard_map/ppermute | solution.py:933
  500.4 43.5 %collective-permute-start.49 = (bf16[512,2048]{1,0:T(8,128)(2,1)}, bf16[512,2048]{1,0:T(8,128)(2,1)}, u32[]{:S(2)}, u32[]{:S(2)}) collective-permute-start(bf16[512,2048]{1,0:T(8,128)(2,1)} %get-tuple-element.248), channel_id=1, source_target_pairs={{0,2},{1,3},{2,0},{3,1},{4,6},{5,7},{6,4},{7,5},{8,10},{9,11},{10,... | collective-permute-start | bytes 6291464 | tf_op jit(solution)/shard_map/ppermute | solution.py:925
  502.9 41.0 %collective-permute-start.58 = (bf16[1024,1024]{1,0:T(8,128)(2,1)}, bf16[1024,1024]{1,0:T(8,128)(2,1)}, u32[]{:S(2)}, u32[]{:S(2)}) collective-permute-start(bf16[1024,1024]{1,0:T(8,128)(2,1)} %get-tuple-element.266.refs_2_), channel_id=1, source_target_pairs={{20,16},{24,28},{21,17},{25,29},{22,18},{26,30},{23,19},{27,31}} | collective-permute-start | bytes 6291464 | tf_op jit(solution)/shard_map/ppermute | solution.py:938
  521.0 27.1 %collective-permute-start.56 = (bf16[512,1536]{1,0:T(8,128)(2,1)}, bf16[512,1536]{1,0:T(8,128)(2,1)S(1)}, u32[]{:S(2)}, u32[]{:S(2)}) collective-permute-start(bf16[512,1536]{1,0:T(8,128)(2,1)} %get-tuple-element.264.refs_2_.refs_9_), channel_id=1, source_target_pairs={{0,4},{12,8},{1,5},{13,9},{2,6},{14,10},{3,7},{15,11},{16,20},{28,... | collective-permute-start | bytes 4718600 | tf_op jit(solution)/shard_map/ppermute | solution.py:933
  525.5 22.6 %collective-permute-start.57 = (bf16[512,1536]{1,0:T(8,128)(2,1)}, bf16[512,1536]{1,0:T(8,128)(2,1)S(1)}, u32[]{:S(2)}, u32[]{:S(2)}) collective-permute-start(bf16[512,1536]{1,0:T(8,128)(2,1)} %get-tuple-element.265.refs_4_), channel_id=1, source_target_pairs={{4,8},{8,4},{5,9},{9,5},{6,10},{10,6},{7,11},{11,7},{20,24},{24,20... | collective-permute-start | bytes 4718600 | tf_op jit(solution)/shard_map/ppermute | solution.py:933
  531.4 9.2 %collective-permute-start.45 = (bf16[2,128,1024]{2,1,0:T(8,128)(2,1)S(1)}, bf16[2,128,1024]{2,1,0:T(8,128)(2,1)S(1)}, u32[]{:S(2)}, u32[]{:S(2)}) collective-permute-start(bf16[2,128,1024]{2,1,0:T(8,128)(2,1)S(1)} %fusion.20), channel_id=1, source_target_pairs={{0,2},{1,3},{2,0},{3,1},{4,6},{5,7},{6,4},{7,5},{8,10},{9,11},{10,... | collective-permute-start | bytes 1572872 | tf_op jit(solution)/shard_map/ppermute | solution.py:924
  542.0 42.1 %collective-permute-start.48 = (bf16[512,2048]{1,0:T(8,128)(2,1)S(1)}, bf16[512,2048]{1,0:T(8,128)(2,1)S(1)}, u32[]{:S(2)}, u32[]{:S(2)}) collective-permute-start(bf16[512,2048]{1,0:T(8,128)(2,1)S(1)} %copy-done.121), channel_id=1, source_target_pairs={{0,2},{1,3},{2,0},{3,1},{4,6},{5,7},{6,4},{7,5},{8,10},{9,11},{10,... | collective-permute-start | bytes 6291464 | tf_op jit(solution)/shard_map/ppermute | solution.py:925
  553.6 36.0 %collective-permute-start.60 = (bf16[512,2048]{1,0:T(8,128)(2,1)S(1)}, bf16[512,2048]{1,0:T(8,128)(2,1)S(1)}, u32[]{:S(2)}, u32[]{:S(2)}) collective-permute-start(bf16[512,2048]{1,0:T(8,128)(2,1)S(1)} %get-tuple-element.267.refs_2_.refs_8_), channel_id=1, source_target_pairs={{0,4},{12,8},{1,5},{13,9},{2,6},{14,10},{3,7},{15,11}} | collective-permute-start | bytes 6291464 | tf_op jit(solution)/shard_map/ppermute | solution.py:938
  560.6 23.5 %collective-permute-start.61 = (bf16[512,1536]{1,0:T(8,128)(2,1)S(1)}, bf16[512,1536]{1,0:T(8,128)(2,1)S(1)}, u32[]{:S(2)}, u32[]{:S(2)}) collective-permute-start(bf16[512,1536]{1,0:T(8,128)(2,1)S(1)} %get-tuple-element.268.refs_4_), channel_id=1, source_target_pairs={{4,8},{8,4},{5,9},{9,5},{6,10},{10,6},{7,11},{11,7},{20,24},{24,20... | collective-permute-start | bytes 4718600 | tf_op jit(solution)/shard_map/ppermute | solution.py:933
  561.3 28.2 %collective-permute-start.62 = (bf16[512,1536]{1,0:T(8,128)(2,1)S(1)}, bf16[512,1536]{1,0:T(8,128)(2,1)S(1)}, u32[]{:S(2)}, u32[]{:S(2)}) collective-permute-start(bf16[512,1536]{1,0:T(8,128)(2,1)S(1)} %get-tuple-element.269.refs_0_.refs_2_), channel_id=1, source_target_pairs={{4,0},{8,12},{5,1},{9,13},{6,2},{10,14},{7,3},{11,15},{20,16},{24,... | collective-permute-start | bytes 4718600 | tf_op jit(solution)/shard_map/ppermute | solution.py:933
  562.6 21.4 %collective-permute-start.63 = (f32[2,3,256]{2,1,0:T(4,128)S(1)}, f32[2,3,256]{2,1,0:T(4,128)S(1)}, u32[]{:S(2)}, u32[]{:S(2)}) collective-permute-start(f32[2,3,256]{2,1,0:T(4,128)S(1)} %fusion.33.refs_7_), channel_id=1, source_target_pairs={{0,4},{12,8},{1,5},{13,9},{2,6},{14,10},{3,7},{15,11},{16,20},{28,... | collective-permute-start | bytes 18440 | tf_op jit(solution)/shard_map/ppermute | solution.py:933
  595.0 25.0 %collective-permute-start.64 = (bf16[512,2048]{1,0:T(8,128)(2,1)S(1)}, bf16[512,2048]{1,0:T(8,128)(2,1)S(1)}, u32[]{:S(2)}, u32[]{:S(2)}) collective-permute-start(bf16[512,2048]{1,0:T(8,128)(2,1)S(1)} %get-tuple-element.270.refs_0_.refs_6_), channel_id=1, source_target_pairs={{0,4},{12,8},{1,5},{13,9},{2,6},{14,10},{3,7},{15,11}} | collective-permute-start | bytes 6291464 | tf_op jit(solution)/shard_map/ppermute | solution.py:938
  596.6 23.4 %collective-permute-start.65 = (bf16[512,2048]{1,0:T(8,128)(2,1)S(1)}, bf16[512,2048]{1,0:T(8,128)(2,1)S(1)}, u32[]{:S(2)}, u32[]{:S(2)}) collective-permute-start(bf16[512,2048]{1,0:T(8,128)(2,1)S(1)} %get-tuple-element.271.refs_2_), channel_id=1, source_target_pairs={{4,8},{8,4},{5,9},{9,5},{6,10},{10,6},{7,11},{11,7}} | collective-permute-start | bytes 6291464 | tf_op jit(solution)/shard_map/ppermute | solution.py:938
  597.4 22.4 %collective-permute-start.66 = (bf16[512,1536]{1,0:T(8,128)(2,1)S(1)}, bf16[512,1536]{1,0:T(8,128)(2,1)S(1)}, u32[]{:S(2)}, u32[]{:S(2)}) collective-permute-start(bf16[512,1536]{1,0:T(8,128)(2,1)S(1)} %get-tuple-element.272.refs_1_.refs_3_), channel_id=1, source_target_pairs={{4,0},{8,12},{5,1},{9,13},{6,2},{10,14},{7,3},{11,15},{20,16},{24,... | collective-permute-start | bytes 4718600 | tf_op jit(solution)/shard_map/ppermute | solution.py:933
  622.6 32.7 %collective-permute-start.68 = (bf16[512,2048]{1,0:T(8,128)(2,1)S(1)}, bf16[512,2048]{1,0:T(8,128)(2,1)S(1)}, u32[]{:S(2)}, u32[]{:S(2)}) collective-permute-start(bf16[512,2048]{1,0:T(8,128)(2,1)S(1)} %get-tuple-element.274.refs_0_.refs_4_), channel_id=1, source_target_pairs={{4,8},{8,4},{5,9},{9,5},{6,10},{10,6},{7,11},{11,7}} | collective-permute-start | bytes 6291464 | tf_op jit(solution)/shard_map/ppermute | solution.py:938
  623.4 31.9 %collective-permute-start.69 = (bf16[512,2048]{1,0:T(8,128)(2,1)S(1)}, bf16[512,2048]{1,0:T(8,128)(2,1)S(1)}, u32[]{:S(2)}, u32[]{:S(2)}) collective-permute-start(bf16[512,2048]{1,0:T(8,128)(2,1)S(1)} %get-tuple-element.273.refs_0_), channel_id=1, source_target_pairs={{4,0},{8,12},{5,1},{9,13},{6,2},{10,14},{7,3},{11,15}} | collective-permute-start | bytes 6291464 | tf_op jit(solution)/shard_map/ppermute | solution.py:938
  624.7 30.5 %collective-permute-start.70 = (f32[2,3,256]{2,1,0:T(4,128)S(1)}, f32[2,3,256]{2,1,0:T(4,128)S(1)}, u32[]{:S(2)}, u32[]{:S(2)}) collective-permute-start(f32[2,3,256]{2,1,0:T(4,128)S(1)} %add.170), channel_id=1, source_target_pairs={{4,0},{8,12},{5,1},{9,13},{6,2},{10,14},{7,3},{11,15},{20,16},{24,... | collective-permute-start | bytes 18440 | tf_op jit(solution)/shard_map/ppermute | solution.py:933
  657.1 27.9 %collective-permute-start.71 = (bf16[512,2048]{1,0:T(8,128)(2,1)S(1)}, bf16[512,2048]{1,0:T(8,128)(2,1)S(1)}, u32[]{:S(2)}, u32[]{:S(2)}) collective-permute-start(bf16[512,2048]{1,0:T(8,128)(2,1)S(1)} %shard_map.210.refs_8_.refs_1_), channel_id=1, source_target_pairs={{4,0},{8,12},{5,1},{9,13},{6,2},{10,14},{7,3},{11,15}} | collective-permute-start | bytes 6291464 | tf_op jit(solution)/shard_map/ppermute | solution.py:938
  (157 other events, 1691.8 us)

commit v3 on v2

--- a/solution.py
+++ b/solution.py
@@ -838,7 +838,7 @@
     rows = sum(piece.shape[0] for piece in sources[0][0])
     cuts = 4 if rows % 64 == 0 else max(len(pieces) for pieces, _ in sources)
     chunk = rows // cuts
-    flat = [piece for pieces, _ in sources for piece in pieces]
+    flat = [in_hbm(piece) for pieces, _ in sources for piece in pieces]
 
     def kernel(flags_ref, *refs):
         out_hbm, low_ref, out_ref, in_sem, out_sem = refs[len(flat) + len(deps) :]
@@ -1239,14 +1239,19 @@
     norms_sum.forward(norms_sum.value + norms_sum.got)
     advance(p2b, p2a, deps=[*arrived(p1b), norms_sum.got])
     norms_sum.forward(norms_sum.value + norms_sum.got)
+    early_ends = all(chain.step == 3 for chain in chains_of([ge_cross, gd_cross, ge_down, gd_down]))
+    if early_ends:
+        g_cross = total(ge_cross, gd_cross, cross_proj.shape[2])
+        g_down = total(ge_down, gd_down, width)
     advance(p2b, deps=[*arrived(p2a), norms_sum.got])
     everything = (
         ge_cross, ge_down, gd_cross, gd_qkv, gd_out, ge_up, ge_qkv, ge_out, gd_down, gd_up
     )
     while advance(*everything):
         pass
-    g_cross = total(ge_cross, gd_cross, cross_proj.shape[2])
-    g_down = total(ge_down, gd_down, width)
+    if not early_ends:
+        g_cross = total(ge_cross, gd_cross, cross_proj.shape[2])
+        g_down = total(ge_down, gd_down, width)
     norms = jnp.where(outer, norms_sum.got, norms_sum.value)
     totals = (
         total(ge_qkv, gd_qkv, self_qkv.shape[2]),

time: 712 us -> 712 us (level)
    ppermute x12, waiting for transfers between devices: 105 us -> 97 us  [z_on(): return lax.ppermute(v, 'dp', pairs)]
    unnamed x301 -> x313, local copies, waits for them, and re-layouts: 31.4 us -> 27.3 us
where the time goes in v3:
time: 712 us; the launch traced here: 701 us
  waiting for transfers between devices  282 us (40%)
  Pallas kernels  227 us (32%)
  starting transfers between devices  123 us (17%)
  local copies, waits for them, and re-layouts  38.8 us (5%)
  other arithmetic  27.2 us (4%)
    pallas_call x28, Pallas kernels, sectioned(): pl.pallas_call(kernel, out_shape=tuple((pltpu.HBM(a.shape, a.dtype) if is...  171 us
    ppermute x4, waiting for transfers between devices, to_core(): return lax.ppermute(v, 'section', [(1 - core, core)])  127 us
    ppermute x12, waiting for transfers between devices, z_on(): return lax.ppermute(v, 'dp', pairs)  97 us
    ppermute x27, starting transfers between devices, flip(): lax.ppermute(v, ('section', 'tensor'), [(core * n + i, core * n + (i ^ 1...  49.3 us
    ppermute x15, starting transfers between devices, z_on(): lax.ppermute(v, ('section', 'dp'), [(core * zs + a, core * zs + b) for a,...  30 us
    unnamed x313, local copies, waits for them, and re-layouts  27.3 us
    ppermute x15, waiting for transfers between devices, z_on(): lax.ppermute(v, ('section', 'dp'), [(core * zs + a, core * zs + b) for a,...  26.3 us
    pallas_call x7, Pallas kernels, add_pairs(): pl.pallas_call(kernel, out_shape=tuple((spec(a.shape) for _, a, _ in pair...  25.6 us
  transfers between devices with their start and end apart: 72, of which 20 were waited for; matrix products, arithmetic and copies ran while one was open for 5% of the time, Pallas kernels for 30%

profile of v3, /device:TPU:0, one launch (start us, length us, event | category | flops | bytes accessed | tf_op | source)
XLA Modules:
  0.0 701.2 jit_solution(6973608866984709166)
XLA Ops:
  1.8 3.0 collective-permute-start
  5.5 2.8 shard_map.169
  14.3 3.3 collective-permute-done.refs_1_
  22.7 2.9 shard_map.173
  25.6 4.1 collective-permute-start.8
  29.7 2.9 shard_map.174
  32.6 6.6 collective-permute-done.4.refs_9_
  39.2 3.6 collective-permute-start.10
  49.4 3.5 shard_map.171.refs_11_
  54.5 10.9 %collective-permute-done.3.refs_7_.refs_16_ = bf16[512,768]{1,0:T(8,128)(2,1)S(1)} collective-permute-done((bf16[512,768]{1,0:T(8,128)(2,1)S(1)}, bf16[512,768]{1,0:T(8,128)(2,1)S(1)}, u32[]{:S(2)}, u32[]{:S(2)}) %collective-permute-start.3) | collective-permute-done | bytes 786464 | tf_op jit(solution)/shard_map/ppermute | solution.py:933
  65.5 13.5 %shard_map.172 = (bf16[512,1024]{1,0:T(8,128)(2,1)S(1)}, bf16[512,1024]{1,0:T(8,128)(2,1)}, f32[512,128]{1,0:T(8,128)}, bf16[512,1536]{1,0:T(8,128)(2,1)}, bf16[...) custom-call(s32[3]{0:T(128)S(1)} %copy-done.111, ...), custom_call_target="tpu_custom_call" | custom-call | flops 1024 | bytes 1024 | tf_op jit(solution)/shard_map/pallas_call | solution.py:183
  80.5 3.5 collective-permute-start.9
  86.4 13.9 %shard_map.175 = (bf16[512,1024]{1,0:T(8,128)(2,1)S(1)}, bf16[512,1024]{1,0:T(8,128)(2,1)}, f32[512,128]{1,0:T(8,128)}, bf16[512,1536]{1,0:T(8,128)(2,1)}, bf16[...) custom-call(s32[3]{0:T(128)S(1)} %copy-done.111, s32[512,1]{1,0:T(8,128)S(1)} %copy-done.73, ...), custom_call_target="tpu_custom_call" | custom-call | flops 1024 | bytes 1024 | tf_op jit(solution)/shard_map/pallas_call | solution.py:183
  111.5 11.6 %shard_map.176 = (bf16[512,1024]{1,0:T(8,128)(2,1)S(1)}, bf16[512,1024]{1,0:T(8,128)(2,1)}, f32[512,128]{1,0:T(8,128)}, bf16[512,2048]{1,0:T(8,128)(2,1)}, bf16[...) custom-call(s32[3]{0:T(128)S(1)} %copy-done.112, f32[1,1024]{1,0:T(1,128)S(1)} %get-tuple-element.337.refs_0_.refs_2_, ...), custom_call_target="tpu_custom_call" | custom-call | flops 1024 | bytes 1024 | tf_op jit(solution)/shard_map/pallas_call | solution.py:183
  123.1 2.6 collective-permute-start.12
  125.8 11.1 %shard_map.178 = (bf16[512,1024]{1,0:T(8,128)(2,1)S(1)}, bf16[512,1024]{1,0:T(8,128)(2,1)}, f32[512,128]{1,0:T(8,128)}, bf16[512,2048]{1,0:T(8,128)(2,1)}, bf16[...) custom-call(s32[3]{0:T(128)S(1)} %copy-done.112, f32[1,1024]{1,0:T(1,128)S(1)} %get-tuple-element.337.refs_0_.refs_2_, ...), custom_call_target="tpu_custom_call" | custom-call | flops 1024 | bytes 1024 | tf_op jit(solution)/shard_map/pallas_call | solution.py:183
  136.9 3.2 collective-permute-start.17
  141.8 7.6 %collective-permute-done.14.refs_7_.refs_6_.refs_10_.refs_3_ = bf16[512,512]{1,0:T(8,128)(2,1)S(1)} collective-permute-done((bf16[512,512]{1,0:T(8,128)(2,1)S(1)}, bf16[512,512]{1,0:T(8,128)(2,1)S(1)}, u32[]{:S(2)}, u32[]{:S(2)}) %collective-permute-start.14) | collective-permute-done | bytes 524320 | tf_op jit(solution)/shard_map/ppermute | solution.py:933
  150.1 3.9 shard_map.180
  156.1 3.8 shard_map.182
  180.8 4.7 shard_map.187
  189.6 4.3 shard_map.190
  195.5 9.1 %shard_map.199 = (bf16[1024,1024]{1,0:T(8,128)(2,1)S(1)}, bf16[1024,1024]{1,0:T(8,128)(2,1)S(1)}) custom-call(s32[3]{0:T(128)S(1)} %copy-done.112, bf16[512,1024]{1,0:T(8,128)(2,1)} %copy-done.56, bf16[512,1024]{1,0:T(8,128)(2,1)} %copy-done.80, bf16[512,2048]{1,0:T(8,128)(2,1)} %get-tuple-element.226.refs_2_, bf16[512,2048]{1,0:T(8,128)(2,1)} %get-tuple-element.227.refs_3_), custom_call_target="tpu_custom_call" | custom-call | flops 1024 | bytes 1024 | tf_op jit(solution)/shard_map/pallas_call | solution.py:183
  209.1 4.1 shard_map.196
  216.6 126.7 %collective-permute-done.37.refs_0_.refs_3_ = bf16[512,1024]{1,0:T(8,128)(2,1)S(1)} collective-permute-done((bf16[512,1024]{1,0:T(8,128)(2,1)S(1)}, bf16[512,1024]{1,0:T(8,128)(2,1)S(1)}, u32[]{:S(2)}, u32[]{:S(2)}) %collective-permute-start.37) | collective-permute-done | bytes 1048608 | tf_op jit(solution)/shard_map/ppermute | solution.py:920
  343.3 3.2 shard_map.197.refs_1_
  346.5 2.8 collective-permute-start.38
  358.6 3.6 shard_map.191.refs_1_
  362.2 3.1 collective-permute-start.30
  365.5 2.7 collective-permute-done.38.refs_2_
  368.3 9.5 %shard_map.198 = (bf16[512,1024]{1,0:T(8,128)(2,1)S(1)}, f32[2,8,1024]{2,1,0:T(8,128)}, bf16[512,2048]{1,0:T(8,128)(2,1)}, bf16[512,1024]{1,0:T(8,128)(2,1)S(1)}) custom-call(s32[3]{0:T(128)S(1)} %copy-done.112, f32[1,1024]{1,0:T(1,128)S(1)} %get-tuple-element.336.refs_0_, bf16[512,1024]{1,0:T(8,128)(2,1)} %shard_map.197.refs_1_, ...), custom_call_target="tpu_custom_call" | custom-call | flops 1024 | bytes 1024 | tf_op jit(solution)/shard_map/pallas_call | solution.py:183
  377.8 2.9 collective-permute-start.39
  381.5 9.4 %shard_map.192 = (bf16[512,1024]{1,0:T(8,128)(2,1)S(1)}, f32[2,8,1024]{2,1,0:T(8,128)}, bf16[512,2048]{1,0:T(8,128)(2,1)}, bf16[512,1024]{1,0:T(8,128)(2,1)}) custom-call(s32[3]{0:T(128)S(1)} %copy-done.112, f32[1,1024]{1,0:T(1,128)S(1)} %get-tuple-element.336.refs_0_, bf16[512,1024]{1,0:T(8,128)(2,1)S(1)} %shard_map.191.refs_1_, ...), custom_call_target="tpu_custom_call" | custom-call | flops 1024 | bytes 1024 | tf_op jit(solution)/shard_map/pallas_call | solution.py:183
  390.9 3.1 collective-permute-start.31
  395.2 11.3 %shard_map.201 = (bf16[512,1536]{1,0:T(8,128)(2,1)S(1)}, bf16[512,1536]{1,0:T(8,128)(2,1)S(1)}, bf16[512,1536]{1,0:T(8,128)(2,1)}, bf16[512,1536]{1,0:T(8,128)(2,1)S(1)}) custom-call(s32[3]{0:T(128)S(1)} %copy-done.112, bf16[512,1024]{1,0:T(8,128)(2,1)} %copy-done.57, bf16[512,1024]{1,0:T(8,128)(2,1)} %copy-done.58, ...), custom_call_target="tpu_custom_call" | custom-call | flops 1024 | bytes 1024 | tf_op jit(solution)/shard_map/pallas_call | solution.py:183
  406.6 16.2 %shard_map.202 = (bf16[512,1024]{1,0:T(8,128)(2,1)S(1)}, f32[2,8,1024]{2,1,0:T(8,128)}, bf16[512,1536]{1,0:T(8,128)(2,1)}, bf16[512,1024]{1,0:T(8,128)(2,1)S(1)}) custom-call(s32[3]{0:T(128)S(1)} %copy-done.112, s32[1,512]{1,0:T(1,128)S(1)} %get-tuple-element.351.refs_1_.refs_0_, s32[512,1]{1,0:T(8,128)S(1)} %copy-done.75, ...), custom_call_target="tpu_custom_call" | custom-call | flops 1024 | bytes 1024 | tf_op jit(solution)/shard_map/pallas_call | solution.py:183
  433.6 16.1 %shard_map.193 = (bf16[512,1024]{1,0:T(8,128)(2,1)S(1)}, f32[2,8,1024]{2,1,0:T(8,128)}, bf16[512,1536]{1,0:T(8,128)(2,1)}, bf16[512,1024]{1,0:T(8,128)(2,1)S(1)}) custom-call(s32[3]{0:T(128)S(1)} %copy-done.112, s32[1,512]{1,0:T(1,128)S(1)} %get-tuple-element.352.refs_1_.refs_0_, s32[512,1]{1,0:T(8,128)S(1)} %copy-done.72, ...), custom_call_target="tpu_custom_call" | custom-call | flops 1024 | bytes 1024 | tf_op jit(solution)/shard_map/pallas_call | solution.py:183
  450.7 2.9 collective-permute-start.32
  454.4 3.0 collective-permute-start.43
  458.6 3.6 collective-permute-done.32
  464.3 3.4 collective-permute-done.43
  469.5 4.1 fusion.9
  473.7 13.8 %shard_map.204 = (bf16[512,2048]{1,0:T(8,128)(2,1)S(1)}, bf16[512,2048]{1,0:T(8,128)(2,1)S(1)}, bf16[512,2048]{1,0:T(8,128)(2,1)}, bf16[512,2048]{1,0:T(8,128)(2,1)S(1)}) custom-call(s32[3]{0:T(128)S(1)} %copy-done.112, bf16[512,1024]{1,0:T(8,128)(2,1)} %copy-done.60, bf16[512,1024]{1,0:T(8,128)(2,1)} %copy-done.51, ...), custom_call_target="tpu_custom_call" | custom-call | flops 1024 | bytes 1024 | tf_op jit(solution)/shard_map/pallas_call | solution.py:183
  488.3 4.7 shard_map.205
  493.0 4.0 collective-permute-start.53
  505.5 11.0 %collective-permute-done.53.refs_3_ = bf16[512,1536]{1,0:T(8,128)(2,1)S(1)} collective-permute-done((bf16[512,1536]{1,0:T(8,128)(2,1)S(1)}, bf16[512,1536]{1,0:T(8,128)(2,1)S(1)}, u32[]{:S(2)}, u32[]{:S(2)}) %collective-permute-start.53) | collective-permute-done | bytes 1572896 | tf_op jit(solution)/shard_map/ppermute | solution.py:933
  516.6 5.1 shard_map.206
  521.7 4.5 collective-permute-start.56
  532.1 9.2 %collective-permute-done.45 = bf16[2,128,1024]{2,1,0:T(8,128)(2,1)S(1)} collective-permute-done((bf16[2,128,1024]{2,1,0:T(8,128)(2,1)S(1)}, bf16[2,128,1024]{2,1,0:T(8,128)(2,1)S(1)}, u32[]{:S(2)}, u32[]{:S(2)}) %collective-permute-start.45) | collective-permute-done | bytes 524320 | tf_op jit(solution)/shard_map/ppermute | solution.py:924
  544.7 4.0 collective-permute-done.56.refs_3_
  548.6 5.4 shard_map.207
  554.1 6.8 collective-permute-start.60
  563.0 4.6 collective-permute-start.63
  567.7 16.8 %collective-permute-done.63.refs_7_ = f32[2,3,256]{2,1,0:T(4,128)S(1)} collective-permute-done((f32[2,3,256]{2,1,0:T(4,128)S(1)}, f32[2,3,256]{2,1,0:T(4,128)S(1)}, u32[]{:S(2)}, u32[]{:S(2)}) %collective-permute-start.63) | collective-permute-done | bytes 6176 | tf_op jit(solution)/shard_map/ppermute | solution.py:933
  584.5 5.5 collective-permute-done.62.refs_6_.refs_4_.refs_3_
  589.9 5.4 shard_map.208
  599.8 20.4 %collective-permute-done.66.refs_4_.refs_5_.refs_7_ = bf16[512,1536]{1,0:T(8,128)(2,1)S(1)} collective-permute-done((bf16[512,1536]{1,0:T(8,128)(2,1)S(1)}, bf16[512,1536]{1,0:T(8,128)(2,1)S(1)}, u32[]{:S(2)}, u32[]{:S(2)}) %collective-permute-start.66) | collective-permute-done | bytes 1572896 | tf_op jit(solution)/shard_map/ppermute | solution.py:933
  620.4 2.7 shard_map.209
  626.6 2.9 shard_map.210.refs_6_
  631.2 3.7 shard_map.211.refs_4_
  634.9 20.8 %collective-permute-done.70.refs_3_ = f32[2,3,256]{2,1,0:T(4,128)S(1)} collective-permute-done((f32[2,3,256]{2,1,0:T(4,128)S(1)}, f32[2,3,256]{2,1,0:T(4,128)S(1)}, u32[]{:S(2)}, u32[]{:S(2)}) %collective-permute-start.70) | collective-permute-done | bytes 6176 | tf_op jit(solution)/shard_map/ppermute | solution.py:933
  662.1 25.4 %collective-permute-done.71.refs_5_.refs_4_ = bf16[512,2048]{1,0:T(8,128)(2,1)S(1)} collective-permute-done((bf16[512,2048]{1,0:T(8,128)(2,1)S(1)}, bf16[512,2048]{1,0:T(8,128)(2,1)S(1)}, u32[]{:S(2)}, u32[]{:S(2)}) %collective-permute-start.71) | collective-permute-done | bytes 2097184 | tf_op jit(solution)/shard_map/ppermute | solution.py:938
  688.8 3.3 shard_map.213.refs_6_
  697.2 3.7 shard_map.214
  (522 shorter events, 145.2 us)
Async XLA Ops:
  1.8 15.8 %collective-permute-start = (bf16[2,128,1024]{2,1,0:T(8,128)(2,1)S(1)}, bf16[2,128,1024]{2,1,0:T(8,128)(2,1)S(1)}, u32[]{:S(2)}, u32[]{:S(2)}) collective-permute-start(bf16[2,128,1024]{2,1,0:T(8,128)(2,1)S(1)} %dynamic-slice_bitcast_fusion.5), channel_id=1, source_target_pairs={{0,2},{1,3},{2,0},{3,1},{4,6},{5,7},{6,4},{7,5},{8,10},{9,11},{10,... | collective-permute-start | bytes 1572872 | tf_op jit(solution)/shard_map/ppermute | solution.py:924
  8.3 34.6 %collective-permute-start.2 = (bf16[512,768]{1,0:T(8,128)(2,1)}, bf16[512,768]{1,0:T(8,128)(2,1)S(1)}, u32[]{:S(2)}, u32[]{:S(2)}) collective-permute-start(bf16[512,768]{1,0:T(8,128)(2,1)} %shard_map.169), channel_id=1, source_target_pairs={{0,2},{1,3},{2,0},{3,1},{4,6},{5,7},{6,4},{7,5},{8,10},{9,11},{10,... | collective-permute-start | bytes 2359304 | tf_op jit(solution)/shard_map/ppermute | solution.py:924
  10.7 28.5 %collective-permute-start.4 = (bf16[128,1024]{1,0:T(8,128)(2,1)}, bf16[128,1024]{1,0:T(8,128)(2,1)S(1)}, u32[]{:S(2)}, u32[]{:S(2)}) collective-permute-start(bf16[128,1024]{1,0:T(8,128)(2,1)} %shard_map.170), channel_id=1, source_target_pairs={{0,2},{1,3},{2,0},{3,1},{4,6},{5,7},{6,4},{7,5},{8,10},{9,11},{10,... | collective-permute-start | bytes 786440 | tf_op jit(solution)/shard_map/ppermute | solution.py:924
  19.8 24.8 %collective-permute-start.1 = (bf16[1,2,1,128,1024]{4,3,1,2,0:T(8,128)(2,1)}, bf16[1,2,1,128,1024]{4,3,1,2,0:T(8,128)(2,1)}, u32[]{:S(2)}, u32[]{:S(2)}) collective-permute-start(bf16[1,2,1,128,1024]{4,3,1,2,0:T(8,128)(2,1)} %maximum_bitcast_fusion.1), channel_id=1, source_target_pairs={{0,1},{1,0},{2,3},{3,2},{4,5},{5,4},{6,7},{7,6},{8,9},{9,8},{10,11... | collective-permute-start | bytes 1572872 | tf_op jit(solution)/shard_map/ppermute | solution.py:924
  22.7 24.4 %collective-permute-start.6 = (bf16[1,2,1,128,1024]{4,3,1,2,0:T(8,128)(2,1)}, bf16[1,2,1,128,1024]{4,3,1,2,0:T(8,128)(2,1)}, u32[]{:S(2)}, u32[]{:S(2)}) collective-permute-start(bf16[1,2,1,128,1024]{4,3,1,2,0:T(8,128)(2,1)} %maximum_bitcast_fusion.2), channel_id=1, source_target_pairs={{0,1},{1,0},{2,3},{3,2},{4,5},{5,4},{6,7},{7,6},{8,9},{9,8},{10,11... | collective-permute-start | bytes 1572872 | tf_op jit(solution)/shard_map/ppermute | solution.py:924
  25.6 54.9 %collective-permute-start.8 = (bf16[512,1024]{1,0:T(8,128)(2,1)}, bf16[512,1024]{1,0:T(8,128)(2,1)}, u32[]{:S(2)}, u32[]{:S(2)}) collective-permute-start(bf16[512,1024]{1,0:T(8,128)(2,1)} %shard_map.173), channel_id=1, source_target_pairs={{0,2},{1,3},{2,0},{3,1},{4,6},{5,7},{6,4},{7,5},{8,10},{9,11},{10,... | collective-permute-start | bytes 3145736 | tf_op jit(solution)/shard_map/ppermute | solution.py:925
  39.2 44.8 %collective-permute-start.10 = (bf16[512,1024]{1,0:T(8,128)(2,1)}, bf16[512,1024]{1,0:T(8,128)(2,1)}, u32[]{:S(2)}, u32[]{:S(2)}) collective-permute-start(bf16[512,1024]{1,0:T(8,128)(2,1)} %shard_map.174), channel_id=1, source_target_pairs={{0,2},{1,3},{2,0},{3,1},{4,6},{5,7},{6,4},{7,5},{8,10},{9,11},{10,... | collective-permute-start | bytes 3145736 | tf_op jit(solution)/shard_map/ppermute | solution.py:925
  42.9 11.6 %collective-permute-start.5 = (bf16[128,1024]{1,0:T(8,128)(2,1)S(1)}, bf16[128,1024]{1,0:T(8,128)(2,1)S(1)}, u32[]{:S(2)}, u32[]{:S(2)}) collective-permute-start(bf16[128,1024]{1,0:T(8,128)(2,1)S(1)} %collective-permute-done.4.refs_9_), channel_id=1, source_target_pairs={{0,4},{4,0},{8,12},{12,8},{1,5},{5,1},{9,13},{13,9},{2,6},{6,2},{1... | collective-permute-start | bytes 786440 | tf_op jit(solution)/shard_map/ppermute | solution.py:933
  44.6 20.9 %collective-permute-start.3 = (bf16[512,768]{1,0:T(8,128)(2,1)S(1)}, bf16[512,768]{1,0:T(8,128)(2,1)S(1)}, u32[]{:S(2)}, u32[]{:S(2)}) collective-permute-start(bf16[512,768]{1,0:T(8,128)(2,1)S(1)} %collective-permute-done.2.refs_6_.refs_15_), channel_id=1, source_target_pairs={{0,4},{4,0},{8,12},{12,8},{1,5},{5,1},{9,13},{13,9},{2,6},{6,2},{1... | collective-permute-start | bytes 2359304 | tf_op jit(solution)/shard_map/ppermute | solution.py:933
  79.0 27.4 %collective-permute-start.7 = (bf16[512,1024]{1,0:T(8,128)(2,1)}, bf16[512,1024]{1,0:T(8,128)(2,1)}, u32[]{:S(2)}, u32[]{:S(2)}) collective-permute-start(bf16[512,1024]{1,0:T(8,128)(2,1)} %get-tuple-element.143.refs_3_), channel_id=1, source_target_pairs={{0,1},{1,0},{2,3},{3,2},{4,5},{5,4},{6,7},{7,6},{8,9},{9,8},{10,11... | collective-permute-start | bytes 3145736 | tf_op jit(solution)/shard_map/ppermute | solution.py:924
  80.5 27.6 %collective-permute-start.9 = (bf16[512,1024]{1,0:T(8,128)(2,1)}, bf16[512,1024]{1,0:T(8,128)(2,1)}, u32[]{:S(2)}, u32[]{:S(2)}) collective-permute-start(bf16[512,1024]{1,0:T(8,128)(2,1)} %collective-permute-done.8.refs_6_.refs_7_), channel_id=1, source_target_pairs={{0,4},{4,0},{8,12},{12,8},{1,5},{5,1},{9,13},{13,9},{2,6},{6,2},{1... | collective-permute-start | bytes 3145736 | tf_op jit(solution)/shard_map/ppermute | solution.py:938
  84.0 24.7 %collective-permute-start.11 = (bf16[512,1024]{1,0:T(8,128)(2,1)}, bf16[512,1024]{1,0:T(8,128)(2,1)}, u32[]{:S(2)}, u32[]{:S(2)}) collective-permute-start(bf16[512,1024]{1,0:T(8,128)(2,1)} %collective-permute-done.10.refs_9_.refs_10_), channel_id=1, source_target_pairs={{0,4},{4,0},{8,12},{12,8},{1,5},{5,1},{9,13},{13,9},{2,6},{6,2},{1... | collective-permute-start | bytes 3145736 | tf_op jit(solution)/shard_map/ppermute | solution.py:938
  101.3 24.5 %collective-permute-start.15 = (bf16[512,1024]{1,0:T(8,128)(2,1)}, bf16[512,1024]{1,0:T(8,128)(2,1)}, u32[]{:S(2)}, u32[]{:S(2)}) collective-permute-start(bf16[512,1024]{1,0:T(8,128)(2,1)} %get-tuple-element.147.refs_3_), channel_id=1, source_target_pairs={{0,1},{1,0},{2,3},{3,2},{4,5},{5,4},{6,7},{7,6},{8,9},{9,8},{10,11... | collective-permute-start | bytes 3145736 | tf_op jit(solution)/shard_map/ppermute | solution.py:924
  101.9 59.4 %collective-permute-start.19 = (bf16[1024,1024]{1,0:T(8,128)(2,1)}, bf16[1024,1024]{1,0:T(8,128)(2,1)}, u32[]{:S(2)}, u32[]{:S(2)}) collective-permute-start(bf16[1024,1024]{1,0:T(8,128)(2,1)} %shard_map.171.refs_11_), channel_id=1, source_target_pairs={{16,18},{17,19},{18,16},{19,17},{20,22},{21,23},{22,20},{23,21},{2... | collective-permute-start | bytes 6291464 | tf_op jit(solution)/shard_map/ppermute | solution.py:925
  106.4 33.7 %collective-permute-start.13 = (bf16[512,512]{1,0:T(8,128)(2,1)}, bf16[512,512]{1,0:T(8,128)(2,1)S(1)}, u32[]{:S(2)}, u32[]{:S(2)}) collective-permute-start(bf16[512,512]{1,0:T(8,128)(2,1)} %shard_map.177), channel_id=1, source_target_pairs={{0,2},{1,3},{2,0},{3,1},{4,6},{5,7},{6,4},{7,5},{8,10},{9,11},{10,... | collective-permute-start | bytes 1572872 | tf_op jit(solution)/shard_map/ppermute | solution.py:924
  123.1 26.9 %collective-permute-start.12 = (bf16[512,1024]{1,0:T(8,128)(2,1)S(1)}, bf16[512,1024]{1,0:T(8,128)(2,1)S(1)}, u32[]{:S(2)}, u32[]{:S(2)}) collective-permute-start(bf16[512,1024]{1,0:T(8,128)(2,1)S(1)} %get-tuple-element.146.refs_3_), channel_id=1, source_target_pairs={{0,1},{1,0},{2,3},{3,2},{4,5},{5,4},{6,7},{7,6},{8,9},{9,8},{10,11... | collective-permute-start | bytes 3145736 | tf_op jit(solution)/shard_map/ppermute | solution.py:925
  136.9 19.2 %collective-permute-start.17 = (bf16[512,1024]{1,0:T(8,128)(2,1)S(1)}, bf16[512,1024]{1,0:T(8,128)(2,1)S(1)}, u32[]{:S(2)}, u32[]{:S(2)}) collective-permute-start(bf16[512,1024]{1,0:T(8,128)(2,1)S(1)} %get-tuple-element.153.refs_3_), channel_id=1, source_target_pairs={{0,1},{1,0},{2,3},{3,2},{4,5},{5,4},{6,7},{7,6},{8,9},{9,8},{10,11... | collective-permute-start | bytes 3145736 | tf_op jit(solution)/shard_map/ppermute | solution.py:925
  140.1 9.2 %collective-permute-start.14 = (bf16[512,512]{1,0:T(8,128)(2,1)S(1)}, bf16[512,512]{1,0:T(8,128)(2,1)S(1)}, u32[]{:S(2)}, u32[]{:S(2)}) collective-permute-start(bf16[512,512]{1,0:T(8,128)(2,1)S(1)} %collective-permute-done.13.refs_6_.refs_5_.refs_9_.refs_2_), channel_id=1, source_target_pairs={{0,4},{4,0},{8,12},{12,8},{1,5},{5,1},{9,13},{13,9},{2,6},{6,2},{1... | collective-permute-start | bytes 1572872 | tf_op jit(solution)/shard_map/ppermute | solution.py:933
  154.0 10.2 %collective-permute-start.16 = (bf16[512,1024]{1,0:T(8,128)(2,1)S(1)}, bf16[512,1024]{1,0:T(8,128)(2,1)S(1)}, u32[]{:S(2)}, u32[]{:S(2)}) collective-permute-start(bf16[512,1024]{1,0:T(8,128)(2,1)S(1)} %get-tuple-element.152), channel_id=1, source_target_pairs={{0,16},{1,17},{2,18},{3,19},{4,20},{5,21},{6,22},{7,23},{8,24},{9,... | collective-permute-start | bytes 3145736 | tf_op jit(solution)/shard_map/ppermute | solution.py:920
  161.3 12.4 %collective-permute-start.20 = (bf16[1024,1024]{1,0:T(8,128)(2,1)}, bf16[1024,1024]{1,0:T(8,128)(2,1)}, u32[]{:S(2)}, u32[]{:S(2)}) collective-permute-start(bf16[1024,1024]{1,0:T(8,128)(2,1)} %collective-permute-done.19.refs_6_.refs_9_.refs_8_.refs_11_), channel_id=1, source_target_pairs={{16,20},{20,16},{24,28},{28,24},{17,21},{21,17},{25,29},{29,25},{1... | collective-permute-start | bytes 6291464 | tf_op jit(solution)/shard_map/ppermute | solution.py:938
  170.5 6.3 collective-permute-start.25
  172.8 5.5 collective-permute-start.24
  177.6 8.6 %collective-permute-start.26 = (bf16[512,1024]{1,0:T(8,128)(2,1)S(1)}, bf16[512,1024]{1,0:T(8,128)(2,1)S(1)}, u32[]{:S(2)}, u32[]{:S(2)}) collective-permute-start(bf16[512,1024]{1,0:T(8,128)(2,1)S(1)} %get-tuple-element.167.refs_3_), channel_id=1, source_target_pairs={{16,17},{17,16},{18,19},{19,18},{20,21},{21,20},{22,23},{23,22},{2... | collective-permute-start | bytes 3145736 | tf_op jit(solution)/shard_map/ppermute | solution.py:925
  188.6 16.8 %collective-permute-start.34 = (bf16[1024,1024]{1,0:T(8,128)(2,1)S(1)}, bf16[1024,1024]{1,0:T(8,128)(2,1)S(1)}, u32[]{:S(2)}, u32[]{:S(2)}) collective-permute-start(bf16[1024,1024]{1,0:T(8,128)(2,1)S(1)} %get-tuple-element.198), channel_id=1, source_target_pairs={{16,18},{17,19},{18,16},{19,17},{20,22},{21,23},{22,20},{23,21},{2... | collective-permute-start | bytes 6291464 | tf_op jit(solution)/shard_map/ppermute | solution.py:925
  193.9 11.4 %collective-permute-start.33 = (bf16[512,1024]{1,0:T(8,128)(2,1)S(1)}, bf16[512,1024]{1,0:T(8,128)(2,1)S(1)}, u32[]{:S(2)}, u32[]{:S(2)}) collective-permute-start(bf16[512,1024]{1,0:T(8,128)(2,1)S(1)} %get-tuple-element.191.refs_4_), channel_id=1, source_target_pairs={{16,17},{17,16},{18,19},{19,18},{20,21},{21,20},{22,23},{23,22},{2... | collective-permute-start | bytes 3145736 | tf_op jit(solution)/shard_map/ppermute | solution.py:925
  194.7 14.4 %collective-permute-start.36 = (bf16[512,1024]{1,0:T(8,128)(2,1)S(1)}, bf16[512,1024]{1,0:T(8,128)(2,1)S(1)}, u32[]{:S(2)}, u32[]{:S(2)}) collective-permute-start(bf16[512,1024]{1,0:T(8,128)(2,1)S(1)} %get-tuple-element.201.refs_4_), channel_id=1, source_target_pairs={{16,17},{17,16},{18,19},{19,18},{20,21},{21,20},{22,23},{23,22},{2... | collective-permute-start | bytes 3145736 | tf_op jit(solution)/shard_map/ppermute | solution.py:925
  204.6 144.8 %collective-permute-start.42 = (bf16[1024,1024]{1,0:T(8,128)(2,1)S(1)}, bf16[1024,1024]{1,0:T(8,128)(2,1)S(1)}, u32[]{:S(2)}, u32[]{:S(2)}) collective-permute-start(bf16[1024,1024]{1,0:T(8,128)(2,1)S(1)} %get-tuple-element.229), channel_id=1, source_target_pairs={{16,18},{17,19},{18,16},{19,17},{20,22},{21,23},{22,20},{23,21},{2... | collective-permute-start | bytes 6291464 | tf_op jit(solution)/shard_map/ppermute | solution.py:925
  208.2 141.1 %collective-permute-start.41 = (bf16[1024,1024]{1,0:T(8,128)(2,1)S(1)}, bf16[1024,1024]{1,0:T(8,128)(2,1)S(1)}, u32[]{:S(2)}, u32[]{:S(2)}) collective-permute-start(bf16[1024,1024]{1,0:T(8,128)(2,1)S(1)} %get-tuple-element.225.refs_17_), channel_id=1, source_target_pairs={{16,20},{28,24},{17,21},{29,25},{18,22},{30,26},{19,23},{31,27}} | collective-permute-start | bytes 6291464 | tf_op jit(solution)/shard_map/ppermute | solution.py:938
  213.1 130.1 %collective-permute-start.37 = (bf16[512,1024]{1,0:T(8,128)(2,1)S(1)}, bf16[512,1024]{1,0:T(8,128)(2,1)S(1)}, u32[]{:S(2)}, u32[]{:S(2)}) collective-permute-start(bf16[512,1024]{1,0:T(8,128)(2,1)S(1)} %get-tuple-element.205), channel_id=1, source_target_pairs={{16,0},{17,1},{18,2},{19,3},{20,4},{21,5},{22,6},{23,7},{24,8},{25... | collective-permute-start | bytes 3145736 | tf_op jit(solution)/shard_map/ppermute | solution.py:920
  214.4 134.9 %collective-permute-start.40 = (bf16[512,1024]{1,0:T(8,128)(2,1)S(1)}, bf16[512,1024]{1,0:T(8,128)(2,1)S(1)}, u32[]{:S(2)}, u32[]{:S(2)}) collective-permute-start(bf16[512,1024]{1,0:T(8,128)(2,1)S(1)} %get-tuple-element.222.refs_4_), channel_id=1, source_target_pairs={{16,17},{17,16},{18,19},{19,18},{20,21},{21,20},{22,23},{23,22},{2... | collective-permute-start | bytes 3145736 | tf_op jit(solution)/shard_map/ppermute | solution.py:925
  215.2 143.4 %collective-permute-start.29 = (bf16[512,1024]{1,0:T(8,128)(2,1)}, bf16[512,1024]{1,0:T(8,128)(2,1)}, u32[]{:S(2)}, u32[]{:S(2)}) collective-permute-start(bf16[512,1024]{1,0:T(8,128)(2,1)} %get-tuple-element.175), channel_id=1, source_target_pairs={{16,0},{17,1},{18,2},{19,3},{20,4},{21,5},{22,6},{23,7},{24,8},{25... | collective-permute-start | bytes 3145736 | tf_op jit(solution)/shard_map/ppermute | solution.py:920
  346.5 21.7 %collective-permute-start.38 = (bf16[512,1024]{1,0:T(8,128)(2,1)}, bf16[512,1024]{1,0:T(8,128)(2,1)}, u32[]{:S(2)}, u32[]{:S(2)}) collective-permute-start(bf16[512,1024]{1,0:T(8,128)(2,1)} %shard_map.197.refs_1_), channel_id=1, source_target_pairs={{0,1},{1,0},{2,3},{3,2},{4,5},{5,4},{6,7},{7,6},{8,9},{9,8},{10,11... | collective-permute-start | bytes 3145736 | tf_op jit(solution)/shard_map/ppermute | solution.py:925
  352.2 70.7 %collective-permute-start.46 = (bf16[1024,1024]{1,0:T(8,128)(2,1)}, bf16[1024,1024]{1,0:T(8,128)(2,1)}, u32[]{:S(2)}, u32[]{:S(2)}) collective-permute-start(bf16[1024,1024]{1,0:T(8,128)(2,1)} %get-tuple-element.242.refs_0_), channel_id=1, source_target_pairs={{16,20},{28,24},{17,21},{29,25},{18,22},{30,26},{19,23},{31,27}} | collective-permute-start | bytes 6291464 | tf_op jit(solution)/shard_map/ppermute | solution.py:938
  354.1 68.7 %collective-permute-start.47 = (bf16[1024,1024]{1,0:T(8,128)(2,1)}, bf16[1024,1024]{1,0:T(8,128)(2,1)}, u32[]{:S(2)}, u32[]{:S(2)}) collective-permute-start(bf16[1024,1024]{1,0:T(8,128)(2,1)} %get-tuple-element.243.refs_2_), channel_id=1, source_target_pairs={{20,24},{24,20},{21,25},{25,21},{22,26},{26,22},{23,27},{27,23}} | collective-permute-start | bytes 6291464 | tf_op jit(solution)/shard_map/ppermute | solution.py:938
  362.2 19.2 %collective-permute-start.30 = (bf16[512,1024]{1,0:T(8,128)(2,1)S(1)}, bf16[512,1024]{1,0:T(8,128)(2,1)S(1)}, u32[]{:S(2)}, u32[]{:S(2)}) collective-permute-start(bf16[512,1024]{1,0:T(8,128)(2,1)S(1)} %shard_map.191.refs_1_), channel_id=1, source_target_pairs={{0,1},{1,0},{2,3},{3,2},{4,5},{5,4},{6,7},{7,6},{8,9},{9,8},{10,11... | collective-permute-start | bytes 3145736 | tf_op jit(solution)/shard_map/ppermute | solution.py:925
  377.8 28.7 %collective-permute-start.39 = (bf16[512,1024]{1,0:T(8,128)(2,1)S(1)}, bf16[512,1024]{1,0:T(8,128)(2,1)S(1)}, u32[]{:S(2)}, u32[]{:S(2)}) collective-permute-start(bf16[512,1024]{1,0:T(8,128)(2,1)S(1)} %get-tuple-element.210.refs_4_), channel_id=1, source_target_pairs={{0,1},{1,0},{2,3},{3,2},{4,5},{5,4},{6,7},{7,6},{8,9},{9,8},{10,11... | collective-permute-start | bytes 3145736 | tf_op jit(solution)/shard_map/ppermute | solution.py:925
  380.8 13.2 %collective-permute-start.27 = (bf16[2,128,1024]{2,1,0:T(8,128)(2,1)S(1)}, bf16[2,128,1024]{2,1,0:T(8,128)(2,1)S(1)}, u32[]{:S(2)}, u32[]{:S(2)}) collective-permute-start(bf16[2,128,1024]{2,1,0:T(8,128)(2,1)S(1)} %fusion.24), channel_id=1, source_target_pairs={{0,2},{1,3},{2,0},{3,1},{4,6},{5,7},{6,4},{7,5},{8,10},{9,11},{10,... | collective-permute-start | bytes 1572872 | tf_op jit(solution)/shard_map/ppermute | solution.py:924
  390.9 38.5 %collective-permute-start.31 = (bf16[512,1024]{1,0:T(8,128)(2,1)}, bf16[512,1024]{1,0:T(8,128)(2,1)}, u32[]{:S(2)}, u32[]{:S(2)}) collective-permute-start(bf16[512,1024]{1,0:T(8,128)(2,1)} %get-tuple-element.180.refs_4_), channel_id=1, source_target_pairs={{0,1},{1,0},{2,3},{3,2},{4,5},{5,4},{6,7},{7,6},{8,9},{9,8},{10,11... | collective-permute-start | bytes 3145736 | tf_op jit(solution)/shard_map/ppermute | solution.py:925
  424.1 64.1 %collective-permute-start.52 = (bf16[1024,1024]{1,0:T(8,128)(2,1)}, bf16[1024,1024]{1,0:T(8,128)(2,1)}, u32[]{:S(2)}, u32[]{:S(2)}) collective-permute-start(bf16[1024,1024]{1,0:T(8,128)(2,1)} %get-tuple-element.244.refs_12_.refs_2_), channel_id=1, source_target_pairs={{20,24},{24,20},{21,25},{25,21},{22,26},{26,22},{23,27},{27,23}} | collective-permute-start | bytes 6291464 | tf_op jit(solution)/shard_map/ppermute | solution.py:938
  427.6 59.9 %collective-permute-start.51 = (bf16[512,1536]{1,0:T(8,128)(2,1)}, bf16[512,1536]{1,0:T(8,128)(2,1)}, u32[]{:S(2)}, u32[]{:S(2)}) collective-permute-start(bf16[512,1536]{1,0:T(8,128)(2,1)} %get-tuple-element.251), channel_id=1, source_target_pairs={{0,2},{1,3},{2,0},{3,1},{4,6},{5,7},{6,4},{7,5},{8,10},{9,11},{10,... | collective-permute-start | bytes 4718600 | tf_op jit(solution)/shard_map/ppermute | solution.py:924
  450.7 11.5 %collective-permute-start.32 = (bf16[2,1,128,1024]{3,2,0,1:T(8,128)(2,1)}, bf16[2,1,128,1024]{3,2,0,1:T(8,128)(2,1)}, u32[]{:S(2)}, u32[]{:S(2)}) collective-permute-start(bf16[2,1,128,1024]{3,2,0,1:T(8,128)(2,1)} %dynamic-slice_bitcast_fusion.3), channel_id=1, source_target_pairs={{0,1},{1,0},{2,3},{3,2},{4,5},{5,4},{6,7},{7,6},{8,9},{9,8},{10,11... | collective-permute-start | bytes 1572872 | tf_op jit(solution)/shard_map/ppermute | solution.py:925
  454.4 13.3 %collective-permute-start.43 = (bf16[2,1,128,1024]{3,2,0,1:T(8,128)(2,1)}, bf16[2,1,128,1024]{3,2,0,1:T(8,128)(2,1)}, u32[]{:S(2)}, u32[]{:S(2)}) collective-permute-start(bf16[2,1,128,1024]{3,2,0,1:T(8,128)(2,1)} %dynamic-slice_bitcast_fusion.1), channel_id=1, source_target_pairs={{0,1},{1,0},{2,3},{3,2},{4,5},{5,4},{6,7},{7,6},{8,9},{9,8},{10,11... | collective-permute-start | bytes 1572872 | tf_op jit(solution)/shard_map/ppermute | solution.py:925
  457.7 47.8 %collective-permute-start.54 = (bf16[1024,1024]{1,0:T(8,128)(2,1)}, bf16[1024,1024]{1,0:T(8,128)(2,1)S(1)}, u32[]{:S(2)}, u32[]{:S(2)}) collective-permute-start(bf16[1024,1024]{1,0:T(8,128)(2,1)} %get-tuple-element.253.refs_2_), channel_id=1, source_target_pairs={{20,16},{24,28},{21,17},{25,29},{22,18},{26,30},{23,19},{27,31}} | collective-permute-start | bytes 6291464 | tf_op jit(solution)/shard_map/ppermute | solution.py:938
  462.2 41.3 %collective-permute-start.50 = (bf16[512,1536]{1,0:T(8,128)(2,1)}, bf16[512,1536]{1,0:T(8,128)(2,1)}, u32[]{:S(2)}, u32[]{:S(2)}) collective-permute-start(bf16[512,1536]{1,0:T(8,128)(2,1)} %copy-done.127), channel_id=1, source_target_pairs={{0,2},{1,3},{2,0},{3,1},{4,6},{5,7},{6,4},{7,5},{8,10},{9,11},{10,... | collective-permute-start | bytes 4718600 | tf_op jit(solution)/shard_map/ppermute | solution.py:924
  467.8 29.3 %collective-permute-start.35 = (bf16[2,1,128,1024]{3,2,0,1:T(8,128)(2,1)}, bf16[2,1,128,1024]{3,2,0,1:T(8,128)(2,1)}, u32[]{:S(2)}, u32[]{:S(2)}) collective-permute-start(bf16[2,1,128,1024]{3,2,0,1:T(8,128)(2,1)} %dynamic-slice_bitcast_fusion.2), channel_id=1, source_target_pairs={{16,17},{17,16},{18,19},{19,18},{20,21},{21,20},{22,23},{23,22},{2... | collective-permute-start | bytes 1572872 | tf_op jit(solution)/shard_map/ppermute | solution.py:925
  487.5 39.4 %collective-permute-start.44 = (bf16[2,1,128,1024]{3,2,0,1:T(8,128)(2,1)S(1)}, bf16[2,1,128,1024]{3,2,0,1:T(8,128)(2,1)S(1)}, u32[]{:S(2)}, u32[]{:S(2)}) collective-permute-start(bf16[2,1,128,1024]{3,2,0,1:T(8,128)(2,1)S(1)} %copy-done.140), channel_id=1, source_target_pairs={{16,17},{17,16},{18,19},{19,18},{20,21},{21,20},{22,23},{23,22},{2... | collective-permute-start | bytes 1572872 | tf_op jit(solution)/shard_map/ppermute | solution.py:925
  493.0 23.5 %collective-permute-start.53 = (bf16[512,1536]{1,0:T(8,128)(2,1)S(1)}, bf16[512,1536]{1,0:T(8,128)(2,1)S(1)}, u32[]{:S(2)}, u32[]{:S(2)}) collective-permute-start(bf16[512,1536]{1,0:T(8,128)(2,1)S(1)} %get-tuple-element.252.refs_2_.refs_6_), channel_id=1, source_target_pairs={{0,4},{12,8},{1,5},{13,9},{2,6},{14,10},{3,7},{15,11},{16,20},{28,... | collective-permute-start | bytes 4718600 | tf_op jit(solution)/shard_map/ppermute | solution.py:933
  500.9 43.7 %collective-permute-start.49 = (bf16[512,2048]{1,0:T(8,128)(2,1)}, bf16[512,2048]{1,0:T(8,128)(2,1)}, u32[]{:S(2)}, u32[]{:S(2)}) collective-permute-start(bf16[512,2048]{1,0:T(8,128)(2,1)} %get-tuple-element.248), channel_id=1, source_target_pairs={{0,2},{1,3},{2,0},{3,1},{4,6},{5,7},{6,4},{7,5},{8,10},{9,11},{10,... | collective-permute-start | bytes 6291464 | tf_op jit(solution)/shard_map/ppermute | solution.py:925
  503.5 41.2 %collective-permute-start.58 = (bf16[1024,1024]{1,0:T(8,128)(2,1)}, bf16[1024,1024]{1,0:T(8,128)(2,1)}, u32[]{:S(2)}, u32[]{:S(2)}) collective-permute-start(bf16[1024,1024]{1,0:T(8,128)(2,1)} %get-tuple-element.266.refs_2_), channel_id=1, source_target_pairs={{20,16},{24,28},{21,17},{25,29},{22,18},{26,30},{23,19},{27,31}} | collective-permute-start | bytes 6291464 | tf_op jit(solution)/shard_map/ppermute | solution.py:938
  521.7 26.9 %collective-permute-start.56 = (bf16[512,1536]{1,0:T(8,128)(2,1)}, bf16[512,1536]{1,0:T(8,128)(2,1)S(1)}, u32[]{:S(2)}, u32[]{:S(2)}) collective-permute-start(bf16[512,1536]{1,0:T(8,128)(2,1)} %get-tuple-element.264.refs_2_.refs_9_), channel_id=1, source_target_pairs={{0,4},{12,8},{1,5},{13,9},{2,6},{14,10},{3,7},{15,11},{16,20},{28,... | collective-permute-start | bytes 4718600 | tf_op jit(solution)/shard_map/ppermute | solution.py:933
  526.2 22.4 %collective-permute-start.57 = (bf16[512,1536]{1,0:T(8,128)(2,1)}, bf16[512,1536]{1,0:T(8,128)(2,1)S(1)}, u32[]{:S(2)}, u32[]{:S(2)}) collective-permute-start(bf16[512,1536]{1,0:T(8,128)(2,1)} %get-tuple-element.265.refs_4_), channel_id=1, source_target_pairs={{4,8},{8,4},{5,9},{9,5},{6,10},{10,6},{7,11},{11,7},{20,24},{24,20... | collective-permute-start | bytes 4718600 | tf_op jit(solution)/shard_map/ppermute | solution.py:933
  532.1 9.2 %collective-permute-start.45 = (bf16[2,128,1024]{2,1,0:T(8,128)(2,1)S(1)}, bf16[2,128,1024]{2,1,0:T(8,128)(2,1)S(1)}, u32[]{:S(2)}, u32[]{:S(2)}) collective-permute-start(bf16[2,128,1024]{2,1,0:T(8,128)(2,1)S(1)} %fusion.20), channel_id=1, source_target_pairs={{0,2},{1,3},{2,0},{3,1},{4,6},{5,7},{6,4},{7,5},{8,10},{9,11},{10,... | collective-permute-start | bytes 1572872 | tf_op jit(solution)/shard_map/ppermute | solution.py:924
  542.7 41.7 %collective-permute-start.48 = (bf16[512,2048]{1,0:T(8,128)(2,1)S(1)}, bf16[512,2048]{1,0:T(8,128)(2,1)S(1)}, u32[]{:S(2)}, u32[]{:S(2)}) collective-permute-start(bf16[512,2048]{1,0:T(8,128)(2,1)S(1)} %copy-done.126), channel_id=1, source_target_pairs={{0,2},{1,3},{2,0},{3,1},{4,6},{5,7},{6,4},{7,5},{8,10},{9,11},{10,... | collective-permute-start | bytes 6291464 | tf_op jit(solution)/shard_map/ppermute | solution.py:925
  554.1 35.8 %collective-permute-start.60 = (bf16[512,2048]{1,0:T(8,128)(2,1)S(1)}, bf16[512,2048]{1,0:T(8,128)(2,1)S(1)}, u32[]{:S(2)}, u32[]{:S(2)}) collective-permute-start(bf16[512,2048]{1,0:T(8,128)(2,1)S(1)} %get-tuple-element.267.refs_2_.refs_8_), channel_id=1, source_target_pairs={{0,4},{12,8},{1,5},{13,9},{2,6},{14,10},{3,7},{15,11}} | collective-permute-start | bytes 6291464 | tf_op jit(solution)/shard_map/ppermute | solution.py:938
  561.0 23.5 %collective-permute-start.61 = (bf16[512,1536]{1,0:T(8,128)(2,1)S(1)}, bf16[512,1536]{1,0:T(8,128)(2,1)S(1)}, u32[]{:S(2)}, u32[]{:S(2)}) collective-permute-start(bf16[512,1536]{1,0:T(8,128)(2,1)S(1)} %get-tuple-element.268.refs_4_), channel_id=1, source_target_pairs={{4,8},{8,4},{5,9},{9,5},{6,10},{10,6},{7,11},{11,7},{20,24},{24,20... | collective-permute-start | bytes 4718600 | tf_op jit(solution)/shard_map/ppermute | solution.py:933
  561.7 28.2 %collective-permute-start.62 = (bf16[512,1536]{1,0:T(8,128)(2,1)S(1)}, bf16[512,1536]{1,0:T(8,128)(2,1)S(1)}, u32[]{:S(2)}, u32[]{:S(2)}) collective-permute-start(bf16[512,1536]{1,0:T(8,128)(2,1)S(1)} %get-tuple-element.269.refs_0_.refs_2_), channel_id=1, source_target_pairs={{4,0},{8,12},{5,1},{9,13},{6,2},{10,14},{7,3},{11,15},{20,16},{24,... | collective-permute-start | bytes 4718600 | tf_op jit(solution)/shard_map/ppermute | solution.py:933
  563.0 21.4 %collective-permute-start.63 = (f32[2,3,256]{2,1,0:T(4,128)S(1)}, f32[2,3,256]{2,1,0:T(4,128)S(1)}, u32[]{:S(2)}, u32[]{:S(2)}) collective-permute-start(f32[2,3,256]{2,1,0:T(4,128)S(1)} %fusion.33.refs_7_), channel_id=1, source_target_pairs={{0,4},{12,8},{1,5},{13,9},{2,6},{14,10},{3,7},{15,11},{16,20},{28,... | collective-permute-start | bytes 18440 | tf_op jit(solution)/shard_map/ppermute | solution.py:933
  595.4 25.0 %collective-permute-start.64 = (bf16[512,2048]{1,0:T(8,128)(2,1)S(1)}, bf16[512,2048]{1,0:T(8,128)(2,1)S(1)}, u32[]{:S(2)}, u32[]{:S(2)}) collective-permute-start(bf16[512,2048]{1,0:T(8,128)(2,1)S(1)} %get-tuple-element.270.refs_0_.refs_6_), channel_id=1, source_target_pairs={{0,4},{12,8},{1,5},{13,9},{2,6},{14,10},{3,7},{15,11}} | collective-permute-start | bytes 6291464 | tf_op jit(solution)/shard_map/ppermute | solution.py:938
  597.0 23.4 %collective-permute-start.65 = (bf16[512,2048]{1,0:T(8,128)(2,1)S(1)}, bf16[512,2048]{1,0:T(8,128)(2,1)S(1)}, u32[]{:S(2)}, u32[]{:S(2)}) collective-permute-start(bf16[512,2048]{1,0:T(8,128)(2,1)S(1)} %get-tuple-element.271.refs_2_), channel_id=1, source_target_pairs={{4,8},{8,4},{5,9},{9,5},{6,10},{10,6},{7,11},{11,7}} | collective-permute-start | bytes 6291464 | tf_op jit(solution)/shard_map/ppermute | solution.py:938
  597.8 22.4 %collective-permute-start.66 = (bf16[512,1536]{1,0:T(8,128)(2,1)S(1)}, bf16[512,1536]{1,0:T(8,128)(2,1)S(1)}, u32[]{:S(2)}, u32[]{:S(2)}) collective-permute-start(bf16[512,1536]{1,0:T(8,128)(2,1)S(1)} %get-tuple-element.272.refs_1_.refs_3_), channel_id=1, source_target_pairs={{4,0},{8,12},{5,1},{9,13},{6,2},{10,14},{7,3},{11,15},{20,16},{24,... | collective-permute-start | bytes 4718600 | tf_op jit(solution)/shard_map/ppermute | solution.py:933
  623.0 32.7 %collective-permute-start.68 = (bf16[512,2048]{1,0:T(8,128)(2,1)S(1)}, bf16[512,2048]{1,0:T(8,128)(2,1)S(1)}, u32[]{:S(2)}, u32[]{:S(2)}) collective-permute-start(bf16[512,2048]{1,0:T(8,128)(2,1)S(1)} %get-tuple-element.274.refs_8_.refs_0_), channel_id=1, source_target_pairs={{4,8},{8,4},{5,9},{9,5},{6,10},{10,6},{7,11},{11,7}} | collective-permute-start | bytes 6291464 | tf_op jit(solution)/shard_map/ppermute | solution.py:938
  623.9 31.9 %collective-permute-start.69 = (bf16[512,2048]{1,0:T(8,128)(2,1)S(1)}, bf16[512,2048]{1,0:T(8,128)(2,1)S(1)}, u32[]{:S(2)}, u32[]{:S(2)}) collective-permute-start(bf16[512,2048]{1,0:T(8,128)(2,1)S(1)} %get-tuple-element.273.refs_0_), channel_id=1, source_target_pairs={{4,0},{8,12},{5,1},{9,13},{6,2},{10,14},{7,3},{11,15}} | collective-permute-start | bytes 6291464 | tf_op jit(solution)/shard_map/ppermute | solution.py:938
  625.2 30.5 %collective-permute-start.70 = (f32[2,3,256]{2,1,0:T(4,128)S(1)}, f32[2,3,256]{2,1,0:T(4,128)S(1)}, u32[]{:S(2)}, u32[]{:S(2)}) collective-permute-start(f32[2,3,256]{2,1,0:T(4,128)S(1)} %add.170), channel_id=1, source_target_pairs={{4,0},{8,12},{5,1},{9,13},{6,2},{10,14},{7,3},{11,15},{20,16},{24,... | collective-permute-start | bytes 18440 | tf_op jit(solution)/shard_map/ppermute | solution.py:933
  659.5 27.9 %collective-permute-start.71 = (bf16[512,2048]{1,0:T(8,128)(2,1)S(1)}, bf16[512,2048]{1,0:T(8,128)(2,1)S(1)}, u32[]{:S(2)}, u32[]{:S(2)}) collective-permute-start(bf16[512,2048]{1,0:T(8,128)(2,1)S(1)} %shard_map.212.refs_1_.refs_8_), channel_id=1, source_target_pairs={{4,0},{8,12},{5,1},{9,13},{6,2},{10,14},{7,3},{11,15}} | collective-permute-start | bytes 6291464 | tf_op jit(solution)/shard_map/ppermute | solution.py:938
  (163 other events, 1875.6 us)
